TPU v7x, 32 devices: a whole 2x2x4 slice. The times are simulated.
32 devices in a mesh: dev: 32 (over z, y, x, core).
Axes of the slice: x: 2, y: 2, z: 4, core: 2. Of those that a mesh axis runs over, the one named last changes fastest.
Arguments:
- row_ids: int32 [4096, 16, 4], P('dev'), may hold values from 0 to 32767, as said below
- lengths: int32 [4096, 16], P('dev'), may hold values from 1 to 4
- counts: int32 [32], P('dev'), may hold values from 1 to 128, as said below
- mask: int32 [4096], P('dev'), may hold values 0 or 1
- labels: float32 [4096, 5], P('dev'), may hold values from 0 to 1
- row_home: int32 [16, 256], replicated, may hold values from 0 to 255, as said below
- mat_home: int32 [13], replicated, may hold values from 0 to 31, as said below
- table: float32 [524288, 64], P('dev'), may hold values from -3.5 to 3.5
- table_m: float32 [524288, 64], P('dev'), may hold values from -1.66893e-06 to 1.66893e-06
- table_v: float32 [524288], P('dev'), may hold values from 5.9604645e-15 to 2.3841858e-14
- experts_w: float32 [2, 1024, 512], replicated, may hold values from -0.1875 to 0.1875
- gates_w: float32 [5, 1024, 2], replicated, may hold values from -0.1875 to 0.1875
- towers_w: float32 [5, 512, 64], replicated, may hold values from -0.25 to 0.25
- small_params: float32 [1669], replicated, may hold values from -0.875 to 0.875
- experts_m: float32 [32, 2, 1024, 512], P('dev'), may hold values from -6.1035156e-05 to 6.1035156e-05
- experts_v: float32 [32, 2, 1024, 512], P('dev'), may hold values from 8.789062e-12 to 3.515625e-11
- gates_m: float32 [32, 5, 1024, 2], P('dev'), may hold values from -0.00030517578 to 0.00030517578
- gates_v: float32 [32, 5, 1024, 2], P('dev'), may hold values from 2.1972656e-10 to 8.789062e-10
- towers_m: float32 [32, 5, 512, 64], P('dev'), may hold values from -0.00015258789 to 0.00015258789
- towers_v: float32 [32, 5, 512, 64], P('dev'), may hold values from 5.493164e-11 to 2.1972656e-10
- small_m: float32 [32, 1669], P('dev'), may hold values from -0.00030517578 to 0.00030517578
- small_v: float32 [32, 1669], P('dev'), may hold values from 2.1972656e-10 to 8.789062e-10
Outputs:
- loss_sum: float32 [], replicated
- weight_sum: float32 [], replicated
- table_new: float32 [524288, 64], P('dev')
- table_m_new: float32 [524288, 64], P('dev')
- table_v_new: float32 [524288], P('dev')
- experts_new: float32 [2, 1024, 512], replicated
- gates_new: float32 [5, 1024, 2], replicated
- towers_new: float32 [5, 512, 64], replicated
- small_new: float32 [1669], replicated
- experts_m_new: float32 [32, 2, 1024, 512], P('dev')
- experts_v_new: float32 [32, 2, 1024, 512], P('dev')
- gates_m_new: float32 [32, 5, 1024, 2], P('dev')
- gates_v_new: float32 [32, 5, 1024, 2], P('dev')
- towers_m_new: float32 [32, 5, 512, 64], P('dev')
- towers_v_new: float32 [32, 5, 512, 64], P('dev')
- small_m_new: float32 [32, 1669], P('dev')
- small_v_new: float32 [32, 1669], P('dev')
- experts_low: bfloat16 [32, 2, 1024, 512], P('dev')
- gates_low: bfloat16 [32, 5, 1024, 2], P('dev')
- towers_low: bfloat16 [32, 5, 512, 64], P('dev')
- small_low: bfloat16 [32, 1669], P('dev')
Inputs may be any that keep to these rules, and one draw needn't show every extreme that they name: `row_ids`: A row number of table t for every slot of bag t, used or not. Of the 8192 ids of one device's sample slots, at most 384 are stored on any one device, and every device reaches 384 for some storing device. `row_home`: each table's row is a permutation: home h means device h // 8. Device i holds its first counts[i] sample slots; the last device holds all 128. `mat_home`: owners may repeat.
All inputs are finite; a program needn't handle non-finite values. No bound on the sum of `mask` on one device may be relied on, other than what follows from the above.
Results may differ from a plain program's by a relative error of at most 0.001.
Values sent between devices are 32-bit elements; how exact they have to be, the bound alone decides.
A program may use at most 192 MiB of HBM per device.

v0:
```python
import jax
import jax.numpy as jnp
from jax import lax
from jax.sharding import PartitionSpec as P

STEP = 5


HIGHEST = lax.Precision.HIGHEST
BETA_ONE = 0.9
BETA_TWO = 0.999
EPSILON = 1e-08
DECAY = 0.01
RATE_DENSE = 0.02
RATE_ROWS = 0.3


def from_root(block, axis, source):
    block = jnp.where(lax.axis_index(axis) == source, block, jnp.zeros_like(block))
    return lax.psum(block, axis)


def dense_forward(params, pooled, labels, weights):
    experts_w, gates_w, towers_w, small = params
    n_experts, _, hidden = experts_w.shape
    tasks, _, tower = towers_w.shape
    start = n_experts * hidden
    expert_bias = small[:start].reshape(n_experts, hidden)
    tower_bias = small[start : start + tasks * tower].reshape(tasks, tower)
    start = start + tasks * tower
    out_weight = small[start : start + tasks * tower].reshape(tasks, tower)
    task_bias = small[start + tasks * tower :]
    hidden_act = jax.nn.silu(
        jnp.einsum("si,eih->seh", pooled, experts_w, precision=HIGHEST) + expert_bias
    )
    gate = jax.nn.softmax(jnp.einsum("si,kie->ske", pooled, gates_w, precision=HIGHEST), axis=-1)
    mixed = jnp.einsum("ske,seh->skh", gate, hidden_act, precision=HIGHEST)
    zed = jax.nn.silu(jnp.einsum("skh,khc->skc", mixed, towers_w, precision=HIGHEST) + tower_bias)
    logit = jnp.sum(zed * out_weight, axis=-1) + task_bias
    losses = jax.nn.softplus(logit) - labels * logit
    return jnp.sum(weights[:, None] * losses)


def adam_step(weight, first, second, grad, rate):
    first_new = BETA_ONE * first + (1.0 - BETA_ONE) * grad
    second_new = BETA_TWO * second + (1.0 - BETA_TWO) * grad * grad
    first_hat = first_new / (1.0 - BETA_ONE**STEP)
    second_hat = second_new / (1.0 - BETA_TWO**STEP)
    weight_new = weight - rate * (first_hat / (jnp.sqrt(second_hat) + EPSILON) + DECAY * weight)
    return (weight_new, first_new, second_new)


def per_device(
    row_ids,
    lengths,
    counts,
    mask,
    labels,
    row_home,
    mat_home,
    table,
    table_m,
    table_v,
    experts_w,
    gates_w,
    towers_w,
    small_params,
    experts_m,
    experts_v,
    gates_m,
    gates_v,
    towers_m,
    towers_v,
    small_m,
    small_v,
):
    devices = lax.axis_size("dev")
    myself = lax.axis_index("dev")
    samples, tables, bag_slots = row_ids.shape
    rows_dev, width = table.shape
    per_table = row_home.shape[1] // devices
    block_rows = rows_dev // (tables * per_table)
    slots = samples * tables * bag_slots
    average = slots // devices
    capacity = average + average // 2
    present = jnp.arange(samples) < counts[0]
    weights = jnp.where(present & (mask == 1), 1.0, 0.0).astype(jnp.float32)
    live = present[:, None, None] & (jnp.arange(bag_slots)[None, None, :] < lengths[:, :, None])
    table_of = jnp.broadcast_to(jnp.arange(tables)[None, :, None], row_ids.shape)
    homes = row_home[table_of, row_ids // block_rows]
    owners = (homes // per_table).reshape(-1)
    local_rows = (
        (table_of * per_table + homes % per_table) * block_rows + row_ids % block_rows
    ).reshape(-1)
    live_flat = live.reshape(-1)
    live_float = live_flat.astype(jnp.float32)
    targets = jnp.where(live_flat, owners, devices)
    order = jnp.argsort(targets, stable=True)
    sorted_targets = targets[order]
    starts = jnp.searchsorted(sorted_targets, jnp.arange(devices + 1), side="left")
    sorted_rank = jnp.arange(slots, dtype=jnp.int32) - starts[sorted_targets]
    slot_rank = jnp.zeros(slots, jnp.int32).at[order].set(sorted_rank)
    slot_rank = jnp.where(live_flat, slot_rank, 0)
    requests = (
        jnp.zeros((devices, capacity), jnp.int32)
        .at[targets, slot_rank]
        .set(local_rows, mode="drop")
    )
    asked_rows = lax.all_to_all(requests, "dev", split_axis=0, concat_axis=0, tiled=True)
    found = table[asked_rows]
    arrived = lax.all_to_all(found, "dev", split_axis=0, concat_axis=0, tiled=True)
    safe_owner = jnp.minimum(owners, devices - 1)
    slot_rows = arrived[safe_owner, slot_rank] * live_float[:, None]
    pooled = jnp.sum(slot_rows.reshape(samples, tables, bag_slots, width), axis=2).reshape(
        samples, tables * width
    )
    params = (experts_w, gates_w, towers_w, small_params)
    local_loss, pull = jax.vjp(
        lambda dense, features: dense_forward(dense, features, labels, weights), params, pooled
    )
    loss_sum, weight_sum = lax.psum((local_loss, jnp.sum(weights)), "dev")
    local_grads, pooled_grad = pull(1.0 / weight_sum)
    slot_grads = (
        jnp.broadcast_to(
            pooled_grad.reshape(samples, tables, 1, width), (samples, tables, bag_slots, width)
        ).reshape(slots, width)
        * live_float[:, None]
    )
    outgoing = (
        jnp.zeros((devices, capacity, width), jnp.float32)
        .at[targets, slot_rank]
        .set(slot_grads, mode="drop")
    )
    incoming = lax.all_to_all(outgoing, "dev", split_axis=0, concat_axis=0, tiled=True)
    grad_table = (
        jnp.zeros((rows_dev, width), jnp.float32)
        .at[asked_rows.reshape(-1)]
        .add(incoming.reshape(-1, width))
    )
    table_m_new = BETA_ONE * table_m + (1.0 - BETA_ONE) * grad_table
    table_v_new = BETA_TWO * table_v + (1.0 - BETA_TWO) * jnp.mean(grad_table * grad_table, axis=1)
    first_hat = table_m_new / (1.0 - BETA_ONE**STEP)
    second_hat = table_v_new / (1.0 - BETA_TWO**STEP)
    table_new = table - RATE_ROWS * (
        first_hat / (jnp.sqrt(second_hat)[:, None] + EPSILON) + DECAY * table
    )
    grad_experts, grad_gates, grad_towers, grad_small = local_grads
    grad_experts, grad_gates, grad_towers, grad_small = lax.psum(
        (grad_experts, grad_gates, grad_towers, grad_small), "dev"
    )
    kinds = (
        (experts_w, experts_m[0], experts_v[0], grad_experts),
        (gates_w, gates_m[0], gates_v[0], grad_gates),
        (towers_w, towers_m[0], towers_v[0], grad_towers),
        (small_params[None], small_m, small_v, grad_small[None]),
    )
    finals = []
    first_outs = []
    second_outs = []
    base = 0
    for stack, firsts, seconds, grad in kinds:
        kind_weights = []
        kind_firsts = []
        kind_seconds = []
        for position in range(stack.shape[0]):
            owner_id = mat_home[base + position]
            is_owner = owner_id == myself
            weight_new, first_new, second_new = adam_step(
                stack[position], firsts[position], seconds[position], grad[position], RATE_DENSE
            )
            kind_firsts.append(jnp.where(is_owner, first_new, 0.0))
            kind_seconds.append(jnp.where(is_owner, second_new, 0.0))
            kept = jnp.where(is_owner, weight_new, stack[position])
            kind_weights.append(from_root(kept, "dev", owner_id))
        base = base + stack.shape[0]
        finals.append(jnp.stack(kind_weights))
        first_outs.append(jnp.stack(kind_firsts)[None])
        second_outs.append(jnp.stack(kind_seconds)[None])
    experts_new, gates_new, towers_new, small_stack = finals
    small_new = small_stack[0]
    return (
        loss_sum,
        weight_sum,
        table_new,
        table_m_new,
        table_v_new,
        experts_new,
        gates_new,
        towers_new,
        small_new,
        first_outs[0],
        second_outs[0],
        first_outs[1],
        second_outs[1],
        first_outs[2],
        second_outs[2],
        first_outs[3][0],
        second_outs[3][0],
        experts_new.astype(jnp.bfloat16)[None],
        gates_new.astype(jnp.bfloat16)[None],
        towers_new.astype(jnp.bfloat16)[None],
        small_new.astype(jnp.bfloat16)[None],
    )


def solution(mesh):
    return jax.shard_map(
        per_device,
        mesh=mesh,
        in_specs=(
            P("dev", None, None),
            P("dev", None),
            P("dev"),
            P("dev"),
            P("dev", None),
            P(),
            P(),
            P("dev", None),
            P("dev", None),
            P("dev"),
            P(),
            P(),
            P(),
            P(),
            P("dev", None, None, None),
            P("dev", None, None, None),
            P("dev", None, None, None),
            P("dev", None, None, None),
            P("dev", None, None, None),
            P("dev", None, None, None),
            P("dev", None),
            P("dev", None),
        ),
        out_specs=(
            P(),
            P(),
            P("dev", None),
            P("dev", None),
            P("dev"),
            P(),
            P(),
            P(),
            P(),
            P("dev", None, None, None),
            P("dev", None, None, None),
            P("dev", None, None, None),
            P("dev", None, None, None),
            P("dev", None, None, None),
            P("dev", None, None, None),
            P("dev", None),
            P("dev", None),
            P("dev", None, None, None),
            P("dev", None, None, None),
            P("dev", None, None, None),
            P("dev", None),
        ),
        check_vma=False,
    )
```

profile of v0, /device:TPU:0, one launch (start us, length us, event | category | flops | bytes accessed | tf_op | source)
XLA Modules:
  0.0 1274.9 jit_solution(16426326473874775970)
XLA Ops:
  15.9 65.0 %gather_fusion.1 = s32[8192]{0:T(1024)S(1)} fusion(s32[16,256]{1,0:T(8,128)S(1)} %copy-done, s32[8192]{0:T(1024)S(1)} %reshape.945), kind=kCustom, calls=%fused_computation.1 | custom fusion | bytes 131072 | tf_op jit(solution)/shard_map/gather | solution.py:90
  81.0 6.8 sort.17
  87.8 45.5 %gather_fusion.2 = s32[8192]{0:T(1024)S(1)} fusion(s32[8192]{0:T(1024)S(1)} %fusion.144, s32[8192]{0:T(1024)S(1)} %get-tuple-element.301), kind=kCustom, calls=%fused_computation.2 | custom fusion | bytes 98304 | tf_op jit(solution)/shard_map/gather | solution.py:99
  133.4 11.7 while.24
  155.7 16.5 %select_subtract_fusion = s32[8192]{0:T(1024)S(1)} fusion(pred[8192]{0:T(1024)(128)(4,1)S(1)} %get-tuple-element.217, pred[8192]{0:T(1024)(128)(4,1)S(1)} %get-tuple-element.216, pred[8192]{0:T(1024)(128)(4,1)S(1)} %get-tuple-element.215, pred[8192]{0:T(1024)(128)(4,1)S(1)} %get-tuple-element.214, pred[8192]{0:T(1024)(128)(4,1)S(1)} %get-tuple-element.213, ...), kind=kLoop, calls=%fused_computation.331 | loop fusion | flops 221184 | bytes 278632 | tf_op jit(solution)/shard_map/sub | solution.py:101
  172.2 30.5 %scatter_custom_fusion = s32[8192]{0:T(1024)S(1)} fusion(s32[8192]{0:T(1024)S(1)} %get-tuple-element.302, s32[8192]{0:T(1024)S(1)} %select_subtract_fusion, s32[]{:T(128)} %constant.106.clone.1), kind=kCustom, calls=%fused_computation.340 | custom fusion | bytes 32772 | tf_op jit(solution)/shard_map/scatter | solution.py:102
  205.0 31.1 %scatter_custom_fusion.2 = s32[12288]{0:T(1024)} fusion(s32[8192]{0:T(1024)S(1)} %broadcast_select_fusion.2, s32[8192]{0:T(1024)S(1)} %reshape.1031, s32[]{:T(128)} %constant.106.clone.1), kind=kCustom, calls=%fused_computation.335 | custom fusion | bytes 49156
  236.1 7.3 all-to-all-start
  243.4 6.9 copy.251
  250.8 44.4 %gather_fusion.3 = f32[12288,64]{1,0:T(8,128)} fusion(f32[16384,64]{1,0:T(8,128)} %copy.251, s32[12288]{0:T(1024)S(1)} %broadcast_clamp_fusion), kind=kCustom, calls=%fused_computation.3 | custom fusion | bytes 6340608 | tf_op jit(solution)/shard_map/gather | solution.py:110
  295.2 6.1 copy.252
  307.5 91.2 %psum.134 = f32[]{:T(128)} all-reduce(f32[]{:T(128)} %get-tuple-element.254), channel_id=1, replica_groups=mesh['dev'=32] {'dev'}, use_global_device_ids=true, to_apply=%region_12.13 | all-reduce | flops 1 | bytes 8 | tf_op jit(solution)/shard_map/psum | solution.py:121
  419.4 6.9 copy.261
  457.5 5.8 copy.253
  463.3 121.5 %gather_fusion.4 = f32[8192,64]{1,0:T(8,128)} fusion(f32[32,384,64]{2,1,0:T(8,128)} %copy.253, s32[8192]{0:T(1024)S(1)} %bitcast.630), kind=kCustom, calls=%fused_computation.4 | custom fusion | bytes 4259840 | tf_op jit(solution)/shard_map/gather | solution.py:113
  584.8 6.3 multiply_reduce_fusion.1
  606.4 5.7 fusion.11
  625.1 6.2 convolution_bitcast_fusion
  631.3 7.6 fusion.38
  646.0 28.2 %scatter_custom_fusion.3 = f32[12288,64]{1,0:T(8,128)} fusion(s32[8192]{0:T(1024)} %copy-done.41, f32[8192,64]{1,0:T(8,128)} %bitcast.636, f32[]{:T(128)} %constant.105.clone.1, f32[8192]{0:T(1024)S(1)} %convert_element_type.49), kind=kCustom, calls=%fused_computation.23 | custom fusion | flops 524288 | bytes 7373312
  674.2 6.1 copy.273
  684.2 91.9 %all-reduce.5 = (f32[5,1024,2]{1,0,2:T(8,128)S(1)}, f32[1669]{0:T(1024)S(1)}) all-reduce(f32[5,1024,2]{1,0,2:T(8,128)S(1)} %copy-done.27, f32[1669]{0:T(1024)S(1)} %pad_add_fusion.1), channel_id=1, replica_groups=mesh['dev'=32] {'dev'}, use_global_device_ids=true, to_apply=%region_20.21 | all-reduce | flops 11909 | bytes 95272 | tf_op jit(solution)/shard_map/psum | solution.py:148
  778.4 39.1 %all-reduce.4 = (f32[]{:T(128)}, f32[1024,2]{0,1:T(2,128)S(1)}, f32[1024,2]{0,1:T(2,128)S(1)}, f32[1024,2]{0,1:T(2,128)S(1)}, f32[1024,2]{0,1:T(2,128)S(1)}, /*index=5*/f32[1024,2]{0,1:T(2,128)S(1)}, f32[1669]{0:T(1024)S(1)}) all-reduce(f32[]{:T(128)} %get-tuple-element.306, ...), channel_id=1, replica_groups=mesh['dev'=32] {'dev'}, use_global_device_ids=true, to_apply=%region_10.11 | all-reduce | flops 11910 | bytes 95280 | tf_op jit(solution)/shard_map/psum | solution.py:121
  821.4 144.2 %all-reduce.13.cloned.1.call-done = (f32[2,1024,512]{1,2,0:T(8,128)}, f32[5,512,64]{1,2,0:T(8,128)}) async-done(((f32[2,1024,512]{1,2,0:T(8,128)}, f32[5,512,64]{1,2,0:T(8,128)}), (f32[2,1024,512]{1,2,0:T(8,128)}, f32[5,512,64]{1,2,0:T(8,128)})) %all-reduce.13.cloned.1.call-update) | async-done | bytes 4849680 | tf_op jit(solution)/shard_map/psum | solution.py:148
  970.2 7.9 fusion.19
  978.2 5.7 fusion.28
  999.5 127.1 %all-reduce.11.cloned.1.call-done = (f32[1024,512]{0,1:T(8,128)}, f32[1024,512]{0,1:T(8,128)}, f32[512,64]{0,1:T(8,128)}, f32[512,64]{0,1:T(8,128)}, f32[512,64]...) async-done(((f32[1024,512]{0,1:T(8,128)}, f32[1024,512]{0,1:T(8,128)}, f32[512,64]{0,1:T(8,128)}, f32[512,64]{0,1:T(8,128)}, f32[512,64]{0,1:T(8,128)}, ...) | async-done | bytes 4849680 | tf_op jit(solution)/shard_map/psum | solution.py:20
  1141.9 6.1 copy.327
  1148.1 83.5 %scatter_custom_fusion.1 = f32[16384,64]{1,0:T(8,128)} fusion(s32[12288]{0:T(1024)} %bitcast.654, f32[12288,64]{1,0:T(8,128)} %bitcast.643, f32[]{:T(128)} %constant.105.clone.1), kind=kCustom, calls=%fused_computation.25 | custom fusion | flops 786432 | bytes 4194816 | tf_op jit(solution)/shard_map/scatter-add | solution.py:138
  1237.8 16.2 %multiply_subtract_fusion = (f32[16384,64]{1,0:T(8,128)}, f32[16384,64]{1,0:T(8,128)}) fusion(f32[16384,64]{1,0:T(8,128)} %copy.251, f32[16384]{0:T(1024)S(1)} %get-tuple-element.246, f32[16384,64]{1,0:T(8,128)S(1)} %copy-done.2, f32[16384,64]{1,0:T(8,128)} %copy.261), kind=kLoop, calls=%fused_computation.17 | loop fusion | flops 9437184 | bytes 21037056 | tf_op jit(solution)/shard_map/sub | solution.py:144
  1254.0 6.8 copy.313
  1260.8 6.8 copy.314
  (347 shorter events, 159.5 us)
Async XLA Ops:
  14.3 66.6 %copy-start.13 = (pred[128,16,4]{2,1,0:T(8,128)(4,1)}, pred[128,16,4]{2,1,0:T(8,128)(4,1)S(1)}, u32[]{:S(2)}) copy-start(pred[128,16,4]{2,1,0:T(8,128)(4,1)S(1)} %copy.249) | copy-start | bytes 24580
  15.9 65.0 %copy-start.31 = (pred[8192]{0:T(1024)(128)(4,1)S(1)}, pred[8192]{0:T(1024)(128)(4,1)}, u32[]{:S(2)}) copy-start(pred[8192]{0:T(1024)(128)(4,1)} %and.80) | copy-start | bytes 24580
  87.8 45.6 %copy-start.37 = (u32[33]{0:T(128)S(1)}, u32[33]{0:T(128)}, u32[]{:S(2)}) copy-start(u32[33]{0:T(128)} %custom-call.4) | copy-start | bytes 400
  87.8 45.6 %copy-start.38 = (u32[33]{0:T(128)S(1)}, u32[33]{0:T(128)}, u32[]{:S(2)}) copy-start(u32[33]{0:T(128)} %custom-call.5) | copy-start | bytes 400
  133.4 69.7 %copy-start.67 = (s32[2]{0:T(128)S(1)}, s32[2]{0:T(128)}, u32[]{:S(2)}) copy-start(s32[2]{0:T(128)} %constant.237) | copy-start | bytes 28
  133.4 69.9 %copy-start.66 = (s32[2]{0:T(128)S(1)}, s32[2]{0:T(128)}, u32[]{:S(2)}) copy-start(s32[2]{0:T(128)} %constant.234) | copy-start | bytes 28
  145.1 58.3 %copy-start.6 = (s32[128,16,4]{2,1,0:T(8,128)S(1)}, s32[128,16,4]{2,1,0:T(8,128)}, u32[]{:S(2)}) copy-start(s32[128,16,4]{2,1,0:T(8,128)} %copy-done.5) | copy-start | bytes 98308
  145.2 58.3 %copy-start.14 = (pred[128,16,4]{2,1,0:T(8,128)(4,1)S(1)}, pred[128,16,4]{2,1,0:T(8,128)(4,1)}, u32[]{:S(2)}) copy-start(pred[128,16,4]{2,1,0:T(8,128)(4,1)} %copy-done.13) | copy-start | bytes 24580
  236.1 14.6 %all-to-all-start = ((s32[32,1,384]{2,1,0:T(1,128)}), s32[32,1,384]{2,1,0:T(1,128)S(1)}, u32[]{:S(2)}, u32[]{:S(2)}) async-start(s32[32,1,384]{2,1,0:T(1,128)} %bitcast.39), calls=%async_computation | async-start | bytes 98304 | tf_op jit(solution)/shard_map/all_to_all | solution.py:109
  301.3 97.4 %copy-start.39 = (f32[1669]{0:T(1024)S(1)}, f32[1669]{0:T(1024)}, u32[]{:S(2)}) copy-start(f32[1669]{0:T(1024)} %param.37) | copy-start | bytes 20032
  301.3 97.9 %copy-start.33 = (s32[13]{0:T(128)S(1)}, s32[13]{0:T(128)}, u32[]{:S(2)}) copy-start(s32[13]{0:T(128)} %param.30) | copy-start | bytes 160
  301.3 116.8 %slice-start = ((f32[1669]{0:T(1024)}), f32[1024]{0:T(1024)S(1)}, s32[]{:S(2)}) async-start(f32[1669]{0:T(1024)} %param.37), calls=%async_computation.5 | async-start | bytes 8192 | tf_op jit(solution)/shard_map/jvp()/slice | solution.py:28
  301.3 116.8 %copy-start.29 = (f32[1,5,1024,2]{2,3,1,0:T(2,128)S(1)}, f32[1,5,1024,2]{2,3,1,0:T(2,128)}, u32[]{:S(2)}) copy-start(f32[1,5,1024,2]{2,3,1,0:T(2,128)} %param.41) | copy-start | bytes 122884
  301.3 156.2 %all-to-all-start.1 = ((f32[32,384,64]{1,2,0:T(8,128)}), f32[32,384,64]{1,2,0:T(8,128)}, u32[]{:S(2)}, u32[]{:S(2)}) async-start(f32[32,384,64]{1,2,0:T(8,128)} %copy.252), calls=%async_computation.1 | async-start | bytes 6291456 | tf_op jit(solution)/shard_map/all_to_all | solution.py:111
  307.5 148.8 %copy-start.58 = (f32[128]{0:T(128)}, f32[128]{0:T(128)S(1)}, u32[]{:S(2)}) copy-start(f32[128]{0:T(128)S(1)} %get-tuple-element.255) | copy-start | bytes 1540
  463.3 121.5 %copy-start.10 = (f32[128,16,4]{2,1,0:T(8,128)S(1)}, f32[128,16,4]{2,1,0:T(8,128)}, u32[]{:S(2)}) copy-start(f32[128,16,4]{2,1,0:T(8,128)} %get-tuple-element.286) | copy-start | bytes 98308
  680.3 95.8 %copy-start.35 = (f32[1,1,1024,2]{2,3,1,0:T(2,128)S(1)}, f32[1,1,1024,2]{2,3,1,0:T(2,128)}, u32[]{:S(2)}) copy-start(f32[1,1,1024,2]{2,3,1,0:T(2,128)} %copy-done.34) | copy-start | bytes 24580
  680.3 95.8 %copy-start.42 = (f32[1,1024,2]{1,2,0:T(2,128)S(1)}, f32[1,1024,2]{1,2,0:T(2,128)}, u32[]{:S(2)}) copy-start(f32[1,1024,2]{1,2,0:T(2,128)} %get-tuple-element.296) | copy-start | bytes 24580
  680.3 95.8 %copy-start.43 = (f32[1,1024,2]{1,2,0:T(2,128)S(1)}, f32[1,1024,2]{1,2,0:T(2,128)}, u32[]{:S(2)}) copy-start(f32[1,1024,2]{1,2,0:T(2,128)} %get-tuple-element.297) | copy-start | bytes 24580
  680.3 95.9 %copy-start.28 = (f32[1,5,1024,2]{2,3,1,0:T(2,128)S(1)}, f32[1,5,1024,2]{2,3,1,0:T(2,128)}, u32[]{:S(2)}) copy-start(f32[1,5,1024,2]{2,3,1,0:T(2,128)} %param.40) | copy-start | bytes 122884
  680.3 95.9 %copy-start.30 = (f32[1,5,1024,2]{2,3,1,0:T(2,128)S(1)}, f32[1,5,1024,2]{2,3,1,0:T(2,128)}, u32[]{:S(2)}) copy-start(f32[1,5,1024,2]{2,3,1,0:T(2,128)} %param.41) | copy-start | bytes 122884
  680.4 96.7 %copy-start.40 = (f32[1669]{0:T(1024)S(1)}, f32[1669]{0:T(1024)}, u32[]{:S(2)}) copy-start(f32[1669]{0:T(1024)} %param.37) | copy-start | bytes 20032
  680.4 96.7 %copy-start.44 = (f32[1669]{0:T(1024)S(1)}, f32[1669]{0:T(1024)}, u32[]{:S(2)}) copy-start(f32[1669]{0:T(1024)} %get-tuple-element.362) | copy-start | bytes 20032
  680.4 96.7 %copy-start.45 = (f32[1669]{0:T(1024)S(1)}, f32[1669]{0:T(1024)}, u32[]{:S(2)}) copy-start(f32[1669]{0:T(1024)} %get-tuple-element.363) | copy-start | bytes 20032
  680.4 98.0 %copy-start.46 = (f32[1,1,1024,2]{2,0,3,1:T(1,128)S(1)}, f32[1,1,1024,2]{2,0,3,1:T(1,128)}, u32[]{:S(2)}) copy-start(f32[1,1,1024,2]{2,0,3,1:T(1,128)} %copy.362) | copy-start | bytes 24580
  680.4 461.5 %all-to-all-start.2 = ((f32[32,384,64]{1,2,0:T(8,128)}), f32[32,384,64]{1,2,0:T(8,128)}, u32[]{:S(2)}, u32[]{:S(2)}) async-start(f32[32,384,64]{1,2,0:T(8,128)} %copy.273), calls=%async_computation.2 | async-start | bytes 6291456 | tf_op jit(solution)/shard_map/all_to_all | solution.py:134
  684.1 281.5 %all-reduce.13.cloned.1.call-start = ((), (), s32[]{:S(2)}) async-start(), calls=%async_computation.4 | async-start | bytes 9699328 | tf_op jit(solution)/shard_map/psum | solution.py:148
  818.8 307.8 %all-reduce.11.cloned.1.call-start = ((), (), s32[]{:S(2)}) async-start(), calls=%async_computation.3 | async-start | bytes 9699328 | tf_op jit(solution)/shard_map/psum | solution.py:20
  821.3 156.8 %copy-start.64 = (f32[5,1024,2]{1,2,0:T(2,128)}, f32[5,1024,2]{1,2,0:T(2,128)S(1)}, u32[]{:S(2)}) copy-start(f32[5,1024,2]{1,2,0:T(2,128)S(1)} %constant_dynamic-update-slice_fusion) | copy-start | bytes 122884
  821.4 156.7 %copy-start.65 = (f32[5,1024,2]{1,2,0:T(2,128)}, f32[5,1024,2]{1,2,0:T(2,128)S(1)}, u32[]{:S(2)}) copy-start(f32[5,1024,2]{1,2,0:T(2,128)S(1)} %constant_dynamic-update-slice_fusion.5) | copy-start | bytes 122884
  999.3 132.1 %copy-start.48 = (f32[5,512,64]{1,2,0:T(8,128)}, f32[5,512,64]{1,2,0:T(8,128)S(1)}, u32[]{:S(2)}) copy-start(f32[5,512,64]{1,2,0:T(8,128)S(1)} %get-tuple-element.279) | copy-start | bytes 1966084
  999.5 127.1 %copy-start.49 = (f32[5,512,64]{1,2,0:T(8,128)}, f32[5,512,64]{1,2,0:T(8,128)S(1)}, u32[]{:S(2)}) copy-start(f32[5,512,64]{1,2,0:T(8,128)S(1)} %fusion.121) | copy-start | bytes 1966084
  (44 other events, 253.5 us)
Sparse Core Ops, SparseCore 0:
  819.0 146.6 all-reduce.12
  978.3 148.2 all-reduce.10
where the time goes:
time: 1280 us; the launch traced here: 1270 us
  local copies, waits for them, and re-layouts  473 us (37%)
  waiting for transfers between devices  272 us (21%)
  blocking collectives  222 us (17%)
  other arithmetic  216 us (17%)
  matrix products  41.3 us (3%)
  between operations  34 us (3%)
  starting transfers between devices  16.6 us (1%)
    psum x1, waiting for transfers between devices, per_device(): lax.psum((grad_experts, grad_gates, grad_towers, grad_small), 'dev')  144 us
    psum x2, blocking collectives, per_device(): loss_sum, weight_sum = lax.psum((local_loss, jnp.sum(weights)), 'dev')  130 us
    psum x1, waiting for transfers between devices, from_root(): return lax.psum(block, axis)  127 us
    gather x1, local copies, waits for them, and re-layouts, per_device(): slot_rows = arrived[safe_owner, slot_rank] * live_float[:, None]  121 us
    unnamed x168, local copies, waits for them, and re-layouts  96.7 us
    psum x1, blocking collectives, per_device(): lax.psum((grad_experts, grad_gates, grad_towers, grad_small), 'dev')  91.9 us
    scatter-add x1, other arithmetic, per_device(): grad_table = jnp.zeros((rows_dev, width), jnp.float32).at[asked_rows.resh...  83.5 us
    gather x2, local copies, waits for them, and re-layouts, per_device(): homes = row_home[table_of, row_ids // block_rows]  66.1 us
  transfers between devices with their start and end apart: 5, of which 3 were waited for; matrix products, arithmetic and copies ran while one was open for 8% of the time, Pallas kernels for 0%

commit v1 on v0

v1 whole, which is shorter than its diff:
```python
import functools
import jax
import jax.numpy as jnp
from jax import lax
from jax.experimental import pallas as pl
from jax.experimental.pallas import tpu as pltpu
from jax.sharding import PartitionSpec as P

MESH = pl.DeviceIdType.MESH
F32, BF16, I32 = jnp.float32, jnp.bfloat16, jnp.int32
NN, NT, TN = (((1,), (0,)), ((), ())), (((1,), (1,)), ((), ())), (((0,), (0,)), ((), ()))
LANES = 128


def iota(shape, dim):
    return lax.broadcasted_iota(I32, shape, dim)


def dot(a, b, dims=NN):
    return lax.dot_general(a, b, dims, preferred_element_type=F32)


def split3(x):
    high = x.astype(BF16)
    rest = x - high.astype(F32)
    middle = rest.astype(BF16)
    low = (rest - middle.astype(F32)).astype(BF16)
    return high, middle, low


def greet_all(n, me):
    barrier = pltpu.get_barrier_semaphore()

    def signal(k, carry):
        pl.semaphore_signal(barrier, inc=1, device_id=(me ^ k,), device_id_type=MESH)
        return carry

    lax.fori_loop(1, n, signal, 0)
    pl.semaphore_wait(barrier, n - 1)


def exchange(n, me, source, target, sends, receives, k):
    peer = me ^ k
    return pltpu.make_async_remote_copy(
        src_ref=source.at[peer],
        dst_ref=target.at[me],
        send_sem=sends.at[k],
        recv_sem=receives.at[k],
        device_id=(peer,),
        device_id_type=MESH,
    )


def for_range(low, high, body):
    def step(k, carry):
        body(k)
        return carry

    lax.fori_loop(low, high, step, 0)


def route_kernel(
    sizes,
    ids_ref, lengths_ref, counts_ref, mask_ref, labels_ref, homes_ref,
    fields_ref, pos_ref, owner_ref, rank_ref, local_ref, mine_ref, theirs_ref, stat_ref,
    outbox, inbox, message, replies, lists, field_scratch,
    send_a, recv_a, send_b, recv_b, local_sem,
):
    n, cap, tables, bag, tasks, per_table, block_rows, rows_dev = sizes
    rows = tables * bag
    me = lax.axis_index("dev")
    shift = lax.rem(me * 13, n)
    per_pair = LANES // n
    table_of = lax.div(iota((rows, LANES), 0), bag)
    slot_of = lax.rem(iota((rows, LANES), 0), bag)
    expand = jnp.where(lax.div(iota((rows, tables), 0), bag) == iota((rows, tables), 1), 1.0, 0.0).astype(BF16)
    used = dot(expand, lengths_ref[...].astype(F32).astype(BF16)).astype(I32)
    present = iota((1, LANES), 1) < counts_ref[0]
    live = present & (slot_of < used)
    field_scratch[0:rows, :] = jnp.where(live, ids_ref[...], -1).astype(F32)
    field_scratch[rows : rows + tasks, :] = labels_ref[...]
    field_scratch[rows + tasks : rows + tasks + 1, :] = jnp.where(present & (mask_ref[...] == 1), 1.0, 0.0)
    field_scratch[rows + tasks + 1 :, :] = jnp.zeros((LANES - rows - tasks - 1, LANES), F32)
    row = iota((n * 8, LANES), 0)
    peer_of, piece = lax.div(row, 8), lax.rem(row, 8)
    column = iota((n * 8, LANES), 1)
    pick = jnp.where((piece < per_pair) & (column == piece * n + lax.rem(peer_of - shift + n, n)), 1.0, 0.0).astype(BF16)
    high, middle, low = split3(field_scratch[...])
    spread = dot(pick, high, NT) + dot(pick, middle, NT) + dot(pick, low, NT)
    outbox[...] = spread.reshape(n, 8, LANES)
    greet_all(n, me)
    own_copy = pltpu.make_async_copy(outbox.at[me], inbox.at[me], local_sem)
    own_copy.start()
    for_range(1, n, lambda k: exchange(n, me, outbox, inbox, send_a, recv_a, k).start())
    homes = homes_ref[...]
    blocks = homes.shape[1]
    homes_rows = (
        dot(expand, (homes >> 5).astype(F32).astype(BF16)) * 32.0 + dot(expand, (homes & 31).astype(F32).astype(BF16))
    ).astype(I32)
    gather_back = jnp.where((piece < per_pair) & (column == peer_of * per_pair + piece), 1.0, 0.0).astype(BF16)
    before = jnp.where(iota((LANES, LANES), 0) < iota((LANES, LANES), 1), 1.0, 0.0).astype(BF16)
    ones = jnp.ones((LANES, LANES), BF16)
    r_out, r_in = iota((rows + 8, rows), 0), iota((rows + 8, rows), 1)
    parity_in = lax.rem(lax.div(r_in, bag), 2)
    earlier = (r_out < rows) & (r_in < r_out) & (parity_in == lax.rem(lax.div(r_out, bag), 2))
    totals = (r_out == rows + 2 + parity_in)
    above = jnp.where(earlier | totals, 1.0, 0.0).astype(BF16)
    for_range(1, n, lambda k: exchange(n, me, outbox, inbox, send_a, recv_a, k).wait())
    own_copy.wait()
    arrived = inbox[...].reshape(n * 8, LANES).T
    high, middle, low = split3(arrived)
    fields = dot(high, gather_back) + dot(middle, gather_back) + dot(low, gather_back)
    fields_ref[...] = fields[rows : rows + 8]
    ids = fields[0:rows].astype(I32)
    weight_count = jnp.sum(fields[rows + tasks : rows + tasks + 1], axis=1, keepdims=True).astype(I32)
    live = ids >= 0
    ids = jnp.maximum(ids, 0)
    block = lax.div(ids, block_rows)
    lane = block & (LANES - 1)
    home = jnp.zeros((rows, LANES), I32)
    for part in range(blocks // LANES):
        found = jnp.take_along_axis(homes_rows[:, part * LANES : (part + 1) * LANES], lane, axis=1, mode="promise_in_bounds")
        home = jnp.where(lax.div(block, LANES) == part, found, home)
    owner = jnp.where(live, lax.div(home, per_table), n)
    local = (table_of * per_table + lax.rem(home, per_table)) * block_rows + lax.rem(ids, block_rows)
    owner_ref[...] = owner
    local_ref[...] = local

    def rank_step(o, carry):
        rank, most = carry
        is_mine = owner == o
        flags = jnp.where(is_mine, 1.0, 0.0).astype(BF16)
        row_totals = dot(flags, ones).astype(BF16)
        bases = dot(above, row_totals)
        count = bases[rows : rows + 8].astype(I32)
        message[o] = count
        rank = jnp.where(is_mine, (dot(flags, before) + bases[0:rows]).astype(I32), rank)
        return rank, jnp.maximum(most, count)

    rank, most = lax.fori_loop(
        0, n, rank_step, (jnp.zeros((rows, LANES), I32), jnp.zeros((8, LANES), I32)), unroll=4
    )
    rank_ref[...] = rank
    most = jnp.max(most, axis=0, keepdims=True)
    pos_ref[...] = jnp.where(live, jnp.where(rank < cap, owner * cap + rank, n * cap + 1), n * cap)
    lists[...] = jnp.zeros_like(lists)
    device_row = iota((n, LANES), 0)
    rank_row = iota((LANES, LANES), 0)
    lane_value = (iota((n, LANES), 1)).astype(F32)

    def list_step(q, carry):
        for parity in range(2):
            picks, places = [], []
            for j in range(bag):
                r = (2 * q + parity) * bag + j
                owner_row = owner_ref[pl.ds(r, 1), :]
                local_row = local_ref[pl.ds(r, 1), :]
                hit = device_row == owner_row
                picks.append(
                    jnp.concatenate(
                        [
                            jnp.where(hit, ((local_row >> 7) + 1).astype(F32), 0.0),
                            jnp.where(hit, (local_row & 127).astype(F32), 0.0),
                            jnp.where(hit, (q + 1).astype(F32), 0.0),
                            jnp.where(hit, lane_value, 0.0),
                        ],
                        axis=0,
                    ).astype(BF16)
                )
                places.append(jnp.where(rank_row == rank_ref[pl.ds(r, 1), :], 1.0, 0.0).astype(BF16))
            lists[parity] += dot(jnp.concatenate(picks, axis=1), jnp.concatenate(places, axis=1), NT)
        return carry

    lax.fori_loop(0, tables // 2, list_step, 0)
    sub = iota((8, LANES), 0)
    is_last = iota((1, LANES), 1) == LANES - 1

    def post(k):
        o = me ^ k
        tile = message[o]
        rows_out = []
        for parity in range(2):
            count = tile[2 + parity : 3 + parity]
            got = [lists[parity, pl.ds(part * n + o, 1), :].astype(I32) for part in range(4)]
            asked = jnp.where(got[0] > 0, (got[0] - 1) * LANES + got[1], rows_dev)
            slot = jnp.where(got[0] > 0, (got[2] - 1) * LANES + got[3], tables // 2 * LANES)
            rows_out.append(jnp.where(is_last, count, asked))
            mine_ref[o, parity : parity + 1, :] = jnp.where(is_last, count, slot)
        tile = jnp.where(sub == 0, rows_out[0], jnp.where(sub == 1, rows_out[1], tile))
        message[o] = jnp.where(sub == 4, most, jnp.where(sub == 5, weight_count, tile))

    def post_and_send(k):
        post(k)
        exchange(n, me, message, replies, send_b, recv_b, k).start()

    for_range(1, n, post_and_send)
    post(0)
    own_copy = pltpu.make_async_copy(message.at[me], replies.at[me], local_sem)
    own_copy.start()
    for_range(1, n, lambda k: exchange(n, me, message, replies, send_b, recv_b, k).wait())
    own_copy.wait()

    def take(s, carry):
        most, total = carry
        tile = replies[s]
        theirs_ref[s] = tile[0:2]
        return jnp.maximum(most, tile), total + tile

    most, total = lax.fori_loop(0, n, take, (jnp.zeros((8, LANES), I32), jnp.zeros((8, LANES), I32)))
    stat_ref[...] = jnp.where(sub == 4, most, total)


def route(n, cap, row_ids, lengths, counts, mask, labels, row_home, rows_dev):
    samples, tables, bag = row_ids.shape
    tasks = labels.shape[1]
    per_table = row_home.shape[1] // n
    block_rows = rows_dev // (tables * per_table)
    sizes = (n, cap, tables, bag, tasks, per_table, block_rows, rows_dev)
    ids = row_ids.transpose(1, 2, 0).reshape(tables * bag, samples)
    vmem = pl.BlockSpec(memory_space=pltpu.VMEM)
    smem = pl.BlockSpec(memory_space=pltpu.SMEM)
    slots = jax.ShapeDtypeStruct((tables * bag, LANES), I32)
    lists = jax.ShapeDtypeStruct((n, 2, LANES), I32)
    return pl.pallas_call(
        functools.partial(route_kernel, sizes),
        out_shape=(
            jax.ShapeDtypeStruct((8, LANES), F32), slots, slots, slots, slots, lists, lists,
            jax.ShapeDtypeStruct((8, LANES), I32),
        ),
        in_specs=[vmem, vmem, smem, vmem, vmem, vmem],
        out_specs=(vmem,) * 8,
        scratch_shapes=[
            pltpu.VMEM((n, 8, LANES), F32), pltpu.VMEM((n, 8, LANES), F32),
            pltpu.VMEM((n, 8, LANES), I32), pltpu.VMEM((n, 8, LANES), I32),
            pltpu.VMEM((2, 4 * n, LANES), F32), pltpu.VMEM((LANES, LANES), F32),
            pltpu.SemaphoreType.DMA((n,)), pltpu.SemaphoreType.DMA((n,)),
            pltpu.SemaphoreType.DMA((n,)), pltpu.SemaphoreType.DMA((n,)),
            pltpu.SemaphoreType.DMA,
        ],
        compiler_params=pltpu.CompilerParams(collective_id=0, has_side_effects=True, vmem_limit_bytes=32 * 2**20),
        name="route",
    )(ids, lengths.T, counts, mask.reshape(1, samples), labels.T, row_home)

STEP = 5
BETA_ONE = 0.9
BETA_TWO = 0.999
EPSILON = 1e-08
DECAY = 0.01
RATE_DENSE = 0.02
RATE_ROWS = 0.3

def rows_exchange_kernel(n, cap, spare, from_table, lists_ref, source_ref, lines_ref, *scratch):
    if from_table:
        rows_ref, outbox, sends, receives = scratch
    else:
        outbox, sends, receives = scratch
        rows_ref = source_ref
    me = lax.axis_index("dev")
    greet_all(n, me)
    lines_ref[n] = jnp.zeros((cap, LANES), F32)
    if from_table:
        width, rows_dev = source_ref.shape
        rows_ref[rows_dev : rows_dev + spare, :] = jnp.zeros((spare, LANES), F32)

        def turn(b):
            at = pl.ds(pl.multiple_of(b * LANES, LANES), LANES)
            piece = source_ref[:, at]
            rows_ref[at, :] = jnp.concatenate([piece] * (LANES // width), axis=0).T

        for_range(0, rows_dev // LANES, turn)
    left = iota((1, LANES), 1) < LANES // 2

    def collect(peer, target, slot):
        def lines(g, carry):
            for i in range(8):
                r = g * 8 + i
                even = rows_ref[pl.ds(lists_ref[peer, 0, r], 1), :]
                odd = rows_ref[pl.ds(lists_ref[peer, 1, r], 1), :]
                target[slot, pl.ds(r, 1), :] = jnp.where(left, even, odd)
            return carry

        lax.fori_loop(0, cap // 8, lines, 0)

    def collect_and_send(i):
        k = n - i
        collect(me ^ k, outbox, me ^ k)
        exchange(n, me, outbox, lines_ref, sends, receives, k).start()

    for_range(1, n, collect_and_send)
    collect(me, lines_ref, me)
    for_range(1, n, lambda k: exchange(n, me, outbox, lines_ref, sends, receives, k).wait())


def rows_exchange(n, cap, lists, source, from_table, collective_id, name):
    spare = 8
    scratch = [pltpu.VMEM((n, cap, LANES), F32), pltpu.SemaphoreType.DMA((n,)), pltpu.SemaphoreType.DMA((n,))]
    if from_table:
        scratch = [pltpu.VMEM((source.shape[1] + spare, LANES), F32)] + scratch
    return pl.pallas_call(
        functools.partial(rows_exchange_kernel, n, cap, spare, from_table),
        out_shape=jax.ShapeDtypeStruct((n + 1, cap, LANES), F32),
        in_specs=[pl.BlockSpec(memory_space=pltpu.SMEM), pl.BlockSpec(memory_space=pltpu.VMEM)],
        out_specs=pl.BlockSpec(memory_space=pltpu.VMEM),
        scratch_shapes=scratch,
        compiler_params=pltpu.CompilerParams(
            collective_id=collective_id, has_side_effects=True, vmem_limit_bytes=40 * 2**20
        ),
        name=name,
    )(lists, source)


def pool_kernel(nothing, tables, bag, pos_ref, lines_ref, pooled_ref):
    samples = pos_ref.shape[1]
    pooled_ref[...] = jnp.zeros_like(pooled_ref)
    left = iota((1, LANES), 1) < LANES // 2

    def sample(s):
        @pl.when(pos_ref[0, s] != nothing)
        def _():
            for q in range(tables // 2):
                sums = []
                for parity in range(2):
                    base = (2 * q + parity) * bag
                    total = lines_ref[pl.ds(pos_ref[base, s], 1), :]
                    for j in range(1, bag):
                        total = total + lines_ref[pl.ds(pos_ref[base + j, s], 1), :]
                    sums.append(total)
                pooled_ref[pl.ds(q * samples + s, 1), :] = jnp.where(left, sums[0], sums[1])

    for_range(0, samples, sample)


def pool(n, cap, tables, bag, pos, lines):
    samples = pos.shape[1]
    return pl.pallas_call(
        functools.partial(pool_kernel, n * cap, tables, bag),
        out_shape=jax.ShapeDtypeStruct((tables // 2 * samples, LANES), F32),
        in_specs=[pl.BlockSpec(memory_space=pltpu.SMEM), pl.BlockSpec(memory_space=pltpu.VMEM)],
        out_specs=pl.BlockSpec(memory_space=pltpu.VMEM),
        compiler_params=pltpu.CompilerParams(vmem_limit_bytes=24 * 2**20),
        name="pool",
    )(pos, lines.reshape((n + 1) * cap, LANES))


def split2(x):
    high = x.astype(BF16)
    return high, (x - high.astype(F32)).astype(BF16)


def dot3(a, b, dims=NN):
    return dot(a[0], b[0], dims) + dot(a[0], b[1], dims) + dot(a[1], b[0], dims)


def sigmoid(x):
    return 1.0 / (1.0 + jnp.exp(-x))


def dense_kernel(
    sizes, stat_ref, fields_ref, pooled_ref, experts_ref, gates_ref, towers_ref, small_ref,
    grad_a_ref, grad_b_ref, rows_ref, side,
):
    experts, hidden, tasks, tower, half_tail = sizes
    samples = fields_ref.shape[1]
    features = pooled_ref.shape[0] // samples * LANES
    halves = (grad_a_ref, grad_b_ref)
    for ref in halves:
        ref[features:, :] = jnp.zeros((half_tail, hidden), F32)

    def put_tail(row, value):
        count = value.shape[0]
        for low, high, ref in ((0, half_tail, grad_a_ref), (half_tail, 2 * half_tail, grad_b_ref)):
            first, last = max(low, row), min(high, row + count)
            if first < last:
                ref[features + first - low : features + last - low, :] = value[first - row : last - row]

    start = experts * hidden
    tower_at = start
    weight_at = start + tasks * tower
    bias_at = weight_at + tasks * tower
    side[0:8, :] = fields_ref[...]
    side[8:, :] = jnp.zeros((samples - 8, samples), F32)
    by_sample = side[...].T
    weight = by_sample[:, tasks : tasks + 1]
    scale = weight / stat_ref[0].astype(F32)
    x = jnp.concatenate([pooled_ref[q * samples : (q + 1) * samples] for q in range(features // LANES)], axis=1)
    x2 = split2(x)
    gate_w = gates_ref[...]
    gate_w2 = split2(gate_w)
    gate_logits = dot3(x2, gate_w2, NT)
    pres, sigs, hids = [], [], []
    for e in range(experts):
        pre = dot3(x2, split2(experts_ref[e])) + small_ref[0:1, e * hidden : (e + 1) * hidden]
        sig = sigmoid(pre)
        pres.append(pre)
        sigs.append(sig)
        hids.append(pre * sig)
    dhids = [jnp.zeros((samples, hidden), F32) for _ in range(experts)]
    dgate_logits = []
    loss = jnp.zeros((samples, 1), F32)
    small_rows = []
    tower_bias_grads, out_weight_grads, task_bias_grads = [], [], []
    for k in range(tasks):
        logits = [gate_logits[:, k * experts + e : k * experts + e + 1] for e in range(experts)]
        top = functools.reduce(jnp.maximum, logits)
        powers = [jnp.exp(v - top) for v in logits]
        whole = functools.reduce(jnp.add, powers)
        gates = [v / whole for v in powers]
        mix = functools.reduce(jnp.add, [gates[e] * hids[e] for e in range(experts)])
        mix2 = split2(mix)
        tower2 = split2(towers_ref[k])
        at = tower_at + k * tower
        pre = dot3(mix2, tower2, NT) + small_ref[0:1, at : at + tower]
        sig = sigmoid(pre)
        zed = pre * sig
        at = weight_at + k * tower
        out_weight = small_ref[0:1, at : at + tower]
        logit = jnp.sum(zed * out_weight, axis=1, keepdims=True) + small_ref[0:1, bias_at + k : bias_at + k + 1]
        label = by_sample[:, k : k + 1]
        softplus = jnp.maximum(logit, 0.0) + jnp.log1p(jnp.exp(-jnp.abs(logit)))
        loss = loss + weight * (softplus - label * logit)
        dlogit = scale * (sigmoid(logit) - label)
        task_bias_grads.append(jnp.sum(dlogit, axis=0, keepdims=True))
        out_weight_grads.append(jnp.sum(dlogit * zed, axis=0, keepdims=True))
        dpre = dlogit * out_weight * (sig * (1.0 + pre * (1.0 - sig)))
        tower_bias_grads.append(jnp.sum(dpre, axis=0, keepdims=True))
        dpre2 = split2(dpre)
        put_tail(k * tower, dot3(split2(dpre.T), mix2))
        dmix = dot3(dpre2, tower2)
        dgates = [jnp.sum(dmix * hids[e], axis=1, keepdims=True) for e in range(experts)]
        mean = functools.reduce(jnp.add, [gates[e] * dgates[e] for e in range(experts)])
        for e in range(experts):
            dgate_logits.append(gates[e] * (dgates[e] - mean))
            dhids[e] = dhids[e] + gates[e] * dmix
    lane = iota((samples, LANES), 1)
    dgl = jnp.zeros((samples, LANES), F32)
    for i, v in enumerate(dgate_logits):
        dgl = jnp.where(lane == i, v, dgl)
    count = tasks * experts
    dgl_t2 = split2(dgl.T[0:16])
    dgates_w = dot3(dgl_t2, x2)
    tail_at = tasks * tower
    put_tail(tail_at, dgates_w[:, :hidden])
    put_tail(tail_at + 16, dgates_w[:, hidden:])
    x_t2 = split2(x.T)
    dx = dot3(split2(dgl[:, :count]), gate_w2)
    expert_bias_grads = []
    for e in range(experts):
        dpre = dhids[e] * (sigs[e] * (1.0 + pres[e] * (1.0 - sigs[e])))
        expert_bias_grads.append(jnp.sum(dpre, axis=0, keepdims=True))
        dpre2 = split2(dpre)
        halves[e][0:features, :] = dot3(x_t2, dpre2)
        dx = dx + dot3(dpre2, split2(experts_ref[e]), NT)
    for q in range(features // LANES):
        rows_ref[q * samples : (q + 1) * samples, :] = dx[:, q * LANES : (q + 1) * LANES]
    rows_ref[features // LANES * samples :, :] = jnp.zeros((8, LANES), F32)
    small_at = tail_at + 32
    pad = jnp.zeros((1, 2 * hidden - 2 * tasks * tower - tasks), F32)
    line = jnp.concatenate(tower_bias_grads + out_weight_grads + task_bias_grads + [pad], axis=1)
    loss_row = jnp.where(iota((1, hidden), 1) == 0, jnp.sum(loss, axis=0, keepdims=True), 0.0)
    for e in range(experts):
        put_tail(small_at + e, expert_bias_grads[e])
    for i in range(line.shape[1] // hidden):
        put_tail(small_at + experts + i, line[:, i * hidden : (i + 1) * hidden])
    put_tail(small_at + 8, loss_row)


def dense(half_tail, stat, fields, pooled, experts_w, gates_w, towers_w, small):
    experts, features, hidden = experts_w.shape
    tasks, _, tower = towers_w.shape
    samples = fields.shape[1]
    vmem = pl.BlockSpec(memory_space=pltpu.VMEM)
    grads = jax.ShapeDtypeStruct((features + half_tail, hidden), F32)
    return pl.pallas_call(
        functools.partial(dense_kernel, (experts, hidden, tasks, tower, half_tail)),
        out_shape=(grads, grads, jax.ShapeDtypeStruct((features // LANES * samples + 8, LANES), F32)),
        in_specs=[pl.BlockSpec(memory_space=pltpu.SMEM)] + [vmem] * 6,
        out_specs=(vmem,) * 3,
        scratch_shapes=[pltpu.VMEM((samples, samples), F32)],
        compiler_params=pltpu.CompilerParams(vmem_limit_bytes=56 * 2**20),
        name="dense",
    )(
        stat, fields, pooled, experts_w,
        gates_w.transpose(0, 2, 1).reshape(tasks * experts, features),
        towers_w.transpose(0, 2, 1), small.reshape(1, -1),
    )


def update_kernel(
    sizes, lists_ref, more_ref, lines_ref, table_ref, first_ref, second_ref, extra_ref,
    table_new_ref, first_new_ref, second_new_ref, sums_even, sums_odd, extra_block, extra_sem,
):
    n, cap, per_table = sizes
    step = pl.program_id(0)
    width, block = table_ref.shape
    table_rows = block // 2
    rows_dev = sums_even.shape[0] - 8
    sums = (sums_even, sums_odd)

    @pl.when(step == 0)
    def _():
        def clear(i):
            for parity in range(2):
                at = pl.multiple_of((2 * i + parity) * table_rows, table_rows)
                sums[parity][pl.ds(at, table_rows), :] = jnp.zeros((table_rows, LANES), F32)

        for_range(0, rows_dev // block, clear)

        def source(s):
            count = jnp.minimum(jnp.maximum(lists_ref[s, 0, LANES - 1], lists_ref[s, 1, LANES - 1]), cap)

            def add(g):
                for i in range(4):
                    r = g * 4 + i
                    line = lines_ref[pl.ds(s * cap + r, 1), :]
                    even, odd = lists_ref[s, 0, r], lists_ref[s, 1, r]
                    sums_even[pl.ds(even, 1), :] += line
                    sums_odd[pl.ds(odd, 1), :] += line

            for_range(0, (count + 3) // 4, add)

        for_range(0, n, source)

    @pl.when(more_ref[0] > cap)
    def _():
        copy = pltpu.make_async_copy(
            extra_ref.at[:, pl.ds(pl.multiple_of(step * block, block), block)], extra_block, extra_sem
        )
        copy.start()
        copy.wait()

    for parity in range(2):
        for b in range(table_rows // LANES):
            at = parity * table_rows + b * LANES
            here = slice(at, at + LANES)
            rows = sums[parity][pl.ds(pl.multiple_of(step * block + at, LANES), LANES), :].T
            grad = rows[parity * width : (parity + 1) * width]
            grad = jnp.where(more_ref[0] > cap, grad + extra_block[:, here], grad)
            first = BETA_ONE * first_ref[:, here] + (1.0 - BETA_ONE) * grad
            mean = jnp.sum(grad * grad, axis=0, keepdims=True) * (1.0 / width)
            second = BETA_TWO * second_ref[:, here] + (1.0 - BETA_TWO) * mean
            rate = (RATE_ROWS / (1.0 - BETA_ONE**STEP)) / (
                jnp.sqrt(second * (1.0 / (1.0 - BETA_TWO**STEP))) + EPSILON
            )
            old = table_ref[:, here]
            table_new_ref[:, here] = old - (first * rate + (RATE_ROWS * DECAY) * old)
            first_new_ref[:, here] = first
            second_new_ref[:, here] = second


def update(n, cap, per_table, tables, lists, most, lines, table, table_m, table_v, extra):
    rows_dev, width = table.shape
    block = 2 * per_table * LANES
    wide = pl.BlockSpec((width, block), lambda i, *_: (0, i))
    thin = pl.BlockSpec((1, block), lambda i, *_: (0, i))
    smem = pl.BlockSpec(memory_space=pltpu.SMEM)
    table_new, first_new, second_new = pl.pallas_call(
        functools.partial(update_kernel, (n, cap, per_table)),
        grid=(rows_dev // block,),
        out_shape=(
            jax.ShapeDtypeStruct((width, rows_dev), F32), jax.ShapeDtypeStruct((width, rows_dev), F32),
            jax.ShapeDtypeStruct((1, rows_dev), F32),
        ),
        in_specs=[
            smem, smem, pl.BlockSpec(((n + 1) * cap, LANES), lambda i: (0, 0)),
            wide, wide, thin, pl.BlockSpec(memory_space=pl.ANY),
        ],
        out_specs=(wide, wide, thin),
        scratch_shapes=[
            pltpu.VMEM((rows_dev + 8, LANES), F32), pltpu.VMEM((rows_dev + 8, LANES), F32),
            pltpu.VMEM((width, block), F32), pltpu.SemaphoreType.DMA,
        ],
        compiler_params=pltpu.CompilerParams(vmem_limit_bytes=48 * 2**20),
        name="update_rows",
    )(lists, most, lines.reshape((n + 1) * cap, LANES), table.T, table_m.T, table_v.reshape(1, rows_dev), extra)
    return table_new.T, first_new.T, second_new.reshape(rows_dev)

def orders(n):
    bits = [1 << i for i in range(n.bit_length() - 1)]
    first, rest = bits[0], bits[1:]
    return ([first] + rest, [first] + [rest[1], rest[0]] + rest[2:])


def swap(x, n, bit):
    return lax.ppermute(x, "dev", [(i, i ^ bit) for i in range(n)])


def halve(x, me, n, bit):
    half = x.shape[-2] // 2
    mine = (me // bit) % 2
    keep = lax.dynamic_slice_in_dim(x, mine * half, half, x.ndim - 2)
    send = lax.dynamic_slice_in_dim(x, (1 - mine) * half, half, x.ndim - 2)
    return keep + swap(send, n, bit)


def double(x, me, n, bit):
    other = swap(x, n, bit)
    mine = (me // bit) % 2
    axis = x.ndim - 2
    return jnp.where(mine == 0, jnp.concatenate([x, other], axis), jnp.concatenate([other, x], axis))


def scatter_sum(x, me, n, order):
    for bit in order:
        x = halve(x, me, n, bit)
    return x


def gather_all(x, me, n, order):
    for bit in order[::-1]:
        x = double(x, me, n, bit)
    return x


def slice_of(x, me, order):
    rows = x.shape[-2]
    start = 0
    for bit in order:
        rows = rows // 2
        start = start + ((me // bit) % 2) * rows
    return lax.dynamic_slice_in_dim(x, start, rows, x.ndim - 2)


GAP = 16


def pack(experts, gates, towers, small, half_tail):
    hidden = experts.shape[2]
    tasks, features, count = gates.shape
    gates = gates.transpose(0, 2, 1).reshape(tasks * count, features)
    lines = jnp.pad(small, (0, 4 * hidden - small.shape[0])).reshape(4, hidden)
    tail = jnp.concatenate(
        [
            towers.transpose(0, 2, 1).reshape(-1, hidden),
            jnp.pad(gates[:, :hidden], ((0, GAP - tasks * count), (0, 0))),
            jnp.pad(gates[:, hidden:], ((0, GAP - tasks * count), (0, 0))),
            lines,
        ]
    )
    tail = jnp.pad(tail, ((0, 2 * half_tail - tail.shape[0]), (0, 0)))
    return (
        jnp.concatenate([experts[0], tail[:half_tail]]),
        jnp.concatenate([experts[1], tail[half_tail:]]),
    )


def unpack(a, b, shapes):
    experts_shape, gates_shape, towers_shape, small_size = shapes
    features = experts_shape[1]
    hidden = experts_shape[2]
    tasks, _, count = gates_shape
    experts = jnp.stack([a[:features], b[:features]])
    tail = jnp.concatenate([a[features:], b[features:]])
    tower_rows = tasks * towers_shape[2]
    towers = tail[:tower_rows].reshape(tasks, towers_shape[2], hidden).transpose(0, 2, 1)
    gates = jnp.concatenate(
        [tail[tower_rows : tower_rows + tasks * count], tail[tower_rows + GAP : tower_rows + GAP + tasks * count]], axis=1
    )
    gates = gates.reshape(tasks, count, features).transpose(0, 2, 1)
    at = tower_rows + 2 * GAP
    small = tail[at : at + 4].reshape(-1)[:small_size]
    return experts, gates, towers, small, tail[at + 8, 0]


def moments(first, second, grad):
    return (
        BETA_ONE * first + (1.0 - BETA_ONE) * grad,
        BETA_TWO * second + (1.0 - BETA_TWO) * grad * grad,
    )


def stepped(weight, first_new, second_new):
    first_hat = first_new / (1.0 - BETA_ONE**STEP)
    second_hat = second_new / (1.0 - BETA_TWO**STEP)
    return weight - RATE_DENSE * (first_hat / (jnp.sqrt(second_hat) + EPSILON) + DECAY * weight)


def late_requests(n, cap, k, owner, rank, local):
    rows, samples = owner.shape
    inside = (owner < n) & (rank >= k * cap) & (rank < (k + 1) * cap)
    parity = jnp.broadcast_to((jnp.arange(rows) // 4 % 2)[:, None], owner.shape)
    target = jnp.where(inside, owner, n)
    place = jnp.where(inside, rank - k * cap, 0)
    asked = jnp.zeros((n, 2, cap), I32).at[target, parity, place].set(local, mode="drop")
    asked = lax.all_to_all(asked.reshape(n, 2 * cap), "dev", 0, 0, tiled=True)
    return inside, parity, target, place, asked


def late_pool(n, cap, most, owner, rank, local, table, pooled):
    width = table.shape[1]
    rows, samples = owner.shape

    def body(k, pooled):
        inside, parity, target, place, asked = late_requests(n, cap, k, owner, rank, local)
        found = table[asked].reshape(n, 2 * cap * width)
        got = lax.all_to_all(found, "dev", 0, 0, tiled=True).reshape(n, 2, cap, width)
        slot_rows = jnp.where(inside[..., None], got[jnp.minimum(target, n - 1), parity, place], 0.0)
        bags = jnp.sum(slot_rows.reshape(rows // 4, 4, samples, width), axis=1)
        bags = bags.reshape(rows // 8, 2, samples, width).transpose(0, 2, 1, 3)
        return pooled + bags.reshape(rows // 8 * samples, 2 * width)

    return lax.fori_loop(1, (most + cap - 1) // cap, body, pooled)


def late_grads(n, cap, most, owner, rank, local, rows_grad, rows_dev, width):
    rows, samples = owner.shape
    tables = rows // 4

    def body(k, extra):
        inside, parity, target, place, asked = late_requests(n, cap, k, owner, rank, local)
        lines = rows_grad[: tables // 2 * samples].reshape(tables // 2, samples, 2, width)
        bags = lines.transpose(0, 2, 1, 3).reshape(tables, 1, samples, width)
        slot_grads = jnp.broadcast_to(bags, (tables, 4, samples, width)).reshape(rows, samples, width)
        out = jnp.zeros((n, 2, cap, width), F32).at[target, parity, place].set(slot_grads, mode="drop")
        valid = jnp.zeros((n, 2, cap), F32).at[target, parity, place].set(1.0, mode="drop")
        got = lax.all_to_all(out.reshape(n, -1), "dev", 0, 0, tiled=True).reshape(-1, width)
        valid = lax.all_to_all(valid.reshape(n, -1), "dev", 0, 0, tiled=True).reshape(-1, 1)
        return extra + jnp.zeros((rows_dev, width), F32).at[asked.reshape(-1)].add(got * valid).T

    return lax.fori_loop(1, (most + cap - 1) // cap, body, jnp.zeros((width, rows_dev), F32))


def per_device(
    row_ids, lengths, counts, mask, labels, row_home, mat_home, table, table_m, table_v,
    experts_w, gates_w, towers_w, small_params,
    experts_m, experts_v, gates_m, gates_v, towers_m, towers_v, small_m, small_v,
):
    n = lax.axis_size("dev")
    me = lax.axis_index("dev")
    samples, tables, bag = row_ids.shape
    rows_dev, width = table.shape
    per_table = row_home.shape[1] // n
    cap = max(8, (samples * tables * bag // n * 5 // 16 + 7) // 8 * 8)
    experts, features, hidden = experts_w.shape
    tasks = towers_w.shape[0]
    half_tail = 256
    order_a, order_b = orders(n)

    owned = mat_home == me
    own_experts = owned[:experts, None, None]
    own_gates = owned[experts : experts + tasks, None, None]
    own_towers = owned[experts + tasks : experts + 2 * tasks, None, None]
    own_small = owned[experts + 2 * tasks]
    firsts = (experts_m[0], gates_m[0], towers_m[0], small_m[0])
    seconds = (experts_v[0], gates_v[0], towers_v[0], small_v[0])
    owns = (own_experts, own_gates, own_towers, own_small)

    def kept(items):
        return tuple(jnp.where(own, item, 0.0) for own, item in zip(owns, items))

    first_a, first_b = pack(*kept(firsts), half_tail)
    second_a, second_b = pack(*kept(seconds), half_tail)
    moments_a = scatter_sum(jnp.stack([first_a, second_a]), me, n, order_a)
    moments_b = scatter_sum(jnp.stack([first_b, second_b]), me, n, order_b)

    fields, pos, owner, rank, local, mine, theirs, stat = route(
        n, cap, row_ids, lengths, counts, mask, labels, row_home, rows_dev
    )
    most, weight_count = stat[4, 0], stat[5, 0]
    lines = rows_exchange(n, cap, theirs, table.T, True, 1, "fetch_rows")
    pooled = pool(n, cap, tables, bag, pos, lines)
    pooled = late_pool(n, cap, most, owner, rank, local, table, pooled)
    grad_a, grad_b, rows_grad = dense(
        half_tail, weight_count[None], fields, pooled, experts_w, gates_w, towers_w, small_params
    )
    back = rows_exchange(n, cap, mine, rows_grad, False, 2, "return_grads")
    extra = late_grads(n, cap, most, owner, rank, local, rows_grad, rows_dev, width)
    table_new, table_m_new, table_v_new = update(
        n, cap, per_table, tables, theirs, most[None], back, table, table_m, table_v, extra
    )

    weights = pack(experts_w, gates_w, towers_w, small_params, half_tail)
    both = []
    for grad, moment, weight, order in (
        (grad_a, moments_a, weights[0], order_a), (grad_b, moments_b, weights[1], order_b)
    ):
        grad = scatter_sum(grad, me, n, order)
        first, second = moments(moment[0], moment[1], grad)
        new = stepped(slice_of(weight, me, order), first, second)
        both.append(gather_all(jnp.stack([new, grad]), me, n, order))
    shapes = (experts_w.shape, gates_w.shape, towers_w.shape, small_params.shape[0])
    experts_new, gates_new, towers_new, small_new, _ = unpack(both[0][0], both[1][0], shapes)
    *grads, loss_sum = unpack(both[0][1], both[1][1], shapes)
    outs_m, outs_v = [], []
    for own, first, second, grad in zip(owns, firsts, seconds, grads):
        first, second = moments(first, second, grad)
        outs_m.append(jnp.where(own, first, 0.0)[None])
        outs_v.append(jnp.where(own, second, 0.0)[None])
    return (
        loss_sum, weight_count.astype(F32), table_new, table_m_new, table_v_new,
        experts_new, gates_new, towers_new, small_new,
        outs_m[0], outs_v[0], outs_m[1], outs_v[1], outs_m[2], outs_v[2], outs_m[3], outs_v[3],
        experts_new.astype(BF16)[None], gates_new.astype(BF16)[None],
        towers_new.astype(BF16)[None], small_new.astype(BF16)[None],
    )


def solution(mesh):
    def split(dims):
        return P("dev", *(None,) * (dims - 1))

    by_device = split(4)
    return jax.shard_map(
        per_device,
        mesh=mesh,
        in_specs=(
            split(3), split(2), split(1), split(1), split(2), P(), P(), split(2), split(2), split(1),
            P(), P(), P(), P(),
        ) + (by_device,) * 6 + (split(2),) * 2,
        out_specs=(P(), P(), split(2), split(2), split(1), P(), P(), P(), P())
        + (by_device,) * 6 + (split(2),) * 2 + (by_device,) * 3 + (split(2),),
        check_vma=False,
    )
```

time: 1280 us -> 433 us (0.34)
  local copies, waits for them, and re-layouts: 473 us -> 56.5 us
  blocking collectives: 222 us -> 0 us
  waiting for transfers between devices: 272 us -> 109 us
  Pallas kernels: 0 us -> 159 us
  other arithmetic: 216 us -> 59.7 us
  matrix products: 41.3 us -> 0 us
  between operations: 34 us -> 5.15 us
  loops' own time: 0.49 us -> 14 us
    gather x22 -> x0, local copies, waits for them, and re-layouts: 296 us -> none  [the longest x1 121 us: per_device(): slot_rows = arrived[safe_owner, slot_rank] * live_float[:, None]]
    psum x2 -> x0, waiting for transfers between devices: 271 us -> none  [the longest x1 144 us: per_device(): lax.psum((grad_experts, grad_gates, grad_towers, grad_small), 'dev')]
    psum x3 -> x0, blocking collectives: 222 us -> none  [the longest x2 130 us: per_device(): loss_sum, weight_sum = lax.psum((local_loss, jnp.sum(weights)), 'dev')]
    pallas_call x0 -> x6, Pallas kernels: none -> 159 us  [the longest x2 86.8 us: rows_exchange(): pl.pallas_call(functools.partial(rows_exchange_kernel, n, cap, spare, fro...]
    ppermute x0 -> x30, waiting for transfers between devices: none -> 109 us  [swap(): return lax.ppermute(x, 'dev', [(i, i ^ bit) for i in range(n)])]
    scatter-add x1 -> x0, other arithmetic: 83.5 us -> none  [per_device(): grad_table = jnp.zeros((rows_dev, width), jnp.float32).at[asked_rows.resh...]
    unnamed x168 -> x119, local copies, waits for them, and re-layouts: 96.7 us -> 15.1 us
    dot_general x12 -> x0, matrix products: 41.3 us -> none  [the longest x3 19.3 us: dense_forward(): jnp.einsum('si,eih->seh', pooled, experts_w, precision=HIGHEST)]
  transfers between devices with their start and end apart: 5 -> 30, of which waited for: 3 -> 17; matrix products, arithmetic and copies ran while one was open for 8% -> 14% of each run, Pallas kernels for 0% -> 14%
where the time goes in v1:
time: 433 us; the launch traced here: 429 us
  Pallas kernels  159 us (37%)
  waiting for transfers between devices  109 us (25%)
  other arithmetic  59.7 us (14%)
  local copies, waits for them, and re-layouts  56.5 us (13%)
  starting transfers between devices  25.6 us (6%)
  loops' own time  14 us (3%)
  between operations  5.15 us (1%)
    ppermute x30, waiting for transfers between devices, swap(): return lax.ppermute(x, 'dev', [(i, i ^ bit) for i in range(n)])  109 us
    pallas_call x2, Pallas kernels, rows_exchange(): pl.pallas_call(functools.partial(rows_exchange_kernel, n, cap, spare, fro...  86.8 us
    pallas_call x1, Pallas kernels, route(): pl.pallas_call(functools.partial(route_kernel, sizes), out_shape=(jax.Sha...  28.5 us
    ppermute x30, starting transfers between devices, swap(): return lax.ppermute(x, 'dev', [(i, i ^ bit) for i in range(n)])  25.6 us
    select_n x10, other arithmetic, double(): jnp.where(mine == 0, jnp.concatenate([x, other], axis), jnp.concatenate([...  22.9 us
    pallas_call x1, Pallas kernels, update(): pl.pallas_call(functools.partial(update_kernel, (n, cap, per_table)), gri...  21.6 us
    unnamed x119, local copies, waits for them, and re-layouts  15.1 us
    pallas_call x1, Pallas kernels, dense(): pl.pallas_call(functools.partial(dense_kernel, (experts, hidden, tasks, t...  14.1 us
  transfers between devices with their start and end apart: 30, of which 17 were waited for; matrix products, arithmetic and copies ran while one was open for 14% of the time, Pallas kernels for 14%

profile of v1, /device:TPU:0, one launch (start us, length us, event | category | flops | bytes accessed | tf_op | source)
XLA Modules:
  0.0 429.4 jit_solution(8516901429589276014)
XLA Ops:
  4.8 28.5 %route.1 = (f32[8,128]{1,0:T(8,128)S(1)}, s32[64,128]{1,0:T(8,128)S(1)}, s32[64,128]{1,0:T(8,128)S(1)}, s32[64,128]{1,0:T(8,128)S(1)}, s32[64,128]{1,0:T(8,128)}...) custom-call(s32[64,128]{1,0:T(8,128)S(1)} %bitcast.343, s32[16,128]{1,0:T(8,128)S(1)} %bitcast.344, ...), custom_call_target="tpu_custom_call" | custom-call | tf_op jit(solution)/shard_map/route/pallas_call | solution.py:224
  37.9 7.0 %copy.59 = f32[16384,64]{1,0:T(8,128)} copy(f32[16384,64]{0,1:T(8,128)} %param.33) | data formatting | bytes 8388608 | tf_op jit(solution)/shard_map/while | solution.py:701
  47.0 48.8 %fetch_rows.1 = f32[33,80,128]{2,1,0:T(8,128)S(1)} custom-call(s32[32,2,128]{2,1,0:T(2,128)S(1)} %get-tuple-element.228.lists_ref, f32[64,16384]{1,0:T(8,128)S(1)} %bitcast.338), custom_call_target="tpu_custom_call" | custom-call | tf_op jit(solution)/shard_map/fetch_rows/pallas_call | solution.py:299
  95.8 8.1 %pool.1 = f32[1024,128]{1,0:T(8,128)S(1)} custom-call(s32[64,128]{1,0:T(8,128)S(1)} %get-tuple-element.227.pos_ref, f32[2640,128]{1,0:T(8,128)S(1)} %bitcast.341), custom_call_target="tpu_custom_call" | custom-call | tf_op jit(solution)/shard_map/pool/pallas_call | solution.py:335
  104.2 9.0 %while.24 = (s32[]{:T(128)}, f32[1024,128]{0,1:T(8,128)S(1)}, s32[]{:T(128)}, s32[64,128]{1,0:T(8,128)S(1)}, s32[64,128]{1,0:T(8,128)S(1)}, /*index=5*/s32[64,12...) while((s32[]{:T(128)}, f32[1024,128]{0,1:T(8,128)S(1)}, ...), condition=%wide.region_3.4_spmd, body=%wide.region_0.3_spmd.sunk | while | flops 1554948 | bytes 23512892 | solution.py:701
  114.2 14.1 %dense.1 = (f32[1280,512]{1,0:T(8,128)}, f32[1280,512]{1,0:T(8,128)}, f32[1032,128]{1,0:T(8,128)}) custom-call(s32[1]{0:T(128)} %bitcast.51.stat_ref, f32[8,128]{1,0:T(8,128)} %copy-done.10, f32[1024,128]{1,0:T(8,128)} %copy.60.pooled_ref, f32[2,1024,512]{2,1,0:T(8,128)} %experts_ref.1, f32[10,1024]{1,0:T(8,128)} %reshape.817.gates_ref, ...), custom_call_target="tpu_custom_call" | custom-call | tf_op jit(solution)/shard_map/dense/pallas_call | solution.py:473
  137.5 3.3 bitcast_select_fusion.4
  159.2 11.9 %collective-permute-done.21 = f32[320,512]{1,0:T(8,128)S(1)} collective-permute-done((f32[320,512]{1,0:T(8,128)S(1)}, f32[320,512]{1,0:T(8,128)S(1)}, u32[]{:S(2)}, u32[]{:S(2)}) %collective-permute-start.21) | collective-permute-done | bytes 655392 | tf_op jit(solution)/shard_map/ppermute | solution.py:584
  186.0 3.4 collective-permute-done.23
  189.5 19.4 %collective-permute-done.1 = f32[2,320,512]{2,1,0:T(8,128)S(1)} collective-permute-done((f32[2,320,512]{2,1,0:T(8,128)S(1)}, f32[2,320,512]{2,1,0:T(8,128)S(1)}, u32[]{:S(2)}, u32[]{:S(2)}) %collective-permute-start.1) | collective-permute-done | bytes 1310752 | tf_op jit(solution)/shard_map/ppermute | solution.py:584
  213.3 12.3 %collective-permute-done.2 = f32[2,160,512]{2,1,0:T(8,128)S(1)} collective-permute-done((f32[2,160,512]{2,1,0:T(8,128)S(1)}, f32[2,160,512]{2,1,0:T(8,128)S(1)}, u32[]{:S(2)}, u32[]{:S(2)}) %collective-permute-start.2) | collective-permute-done | bytes 655392 | tf_op jit(solution)/shard_map/ppermute | solution.py:584
  228.0 10.2 %collective-permute-done.3 = f32[2,80,512]{2,1,0:T(8,128)S(1)} collective-permute-done((f32[2,80,512]{2,1,0:T(8,128)S(1)}, f32[2,80,512]{2,1,0:T(8,128)S(1)}, u32[]{:S(2)}, u32[]{:S(2)}) %collective-permute-start.3) | collective-permute-done | bytes 327712 | tf_op jit(solution)/shard_map/ppermute | solution.py:584
  238.3 4.4 %collective-permute-done.18 = f32[2,80,512]{2,1,0:T(8,128)S(1)} collective-permute-done((f32[2,80,512]{2,1,0:T(8,128)S(1)}, f32[2,80,512]{2,1,0:T(8,128)S(1)}, u32[]{:S(2)}, u32[]{:S(2)}) %collective-permute-start.18) | collective-permute-done | bytes 327712 | tf_op jit(solution)/shard_map/ppermute | solution.py:584
  243.0 8.8 %collective-permute-done.4 = f32[2,40,512]{2,1,0:T(8,128)S(1)} collective-permute-done((f32[2,40,512]{2,1,0:T(8,128)S(1)}, f32[2,40,512]{2,1,0:T(8,128)S(1)}, u32[]{:S(2)}, u32[]{:S(2)}) %collective-permute-start.4) | collective-permute-done | bytes 163872 | tf_op jit(solution)/shard_map/ppermute | solution.py:584
  252.0 3.3 collective-permute-done.19
  255.5 7.2 %collective-permute-done.10 = f32[2,40,512]{2,1,0:T(8,128)S(1)} collective-permute-done((f32[2,40,512]{2,1,0:T(8,128)S(1)}, f32[2,40,512]{2,1,0:T(8,128)S(1)}, u32[]{:S(2)}, u32[]{:S(2)}) %collective-permute-start.10) | collective-permute-done | bytes 163872 | tf_op jit(solution)/shard_map/ppermute | solution.py:584
  263.4 2.8 collective-permute-done.25
  266.4 7.1 %collective-permute-done.11 = f32[2,80,512]{2,1,0:T(8,128)S(1)} collective-permute-done((f32[2,80,512]{2,1,0:T(8,128)S(1)}, f32[2,80,512]{2,1,0:T(8,128)S(1)}, u32[]{:S(2)}, u32[]{:S(2)}) %collective-permute-start.11) | collective-permute-done | bytes 327712 | tf_op jit(solution)/shard_map/ppermute | solution.py:584
  273.5 2.8 collective-permute-start.12
  278.5 3.2 collective-permute-start.27
  281.7 5.7 %collective-permute-done.12 = f32[2,160,512]{2,1,0:T(8,128)S(1)} collective-permute-done((f32[2,160,512]{2,1,0:T(8,128)S(1)}, f32[2,160,512]{2,1,0:T(8,128)S(1)}, u32[]{:S(2)}, u32[]{:S(2)}) %collective-permute-start.12) | collective-permute-done | bytes 655392 | tf_op jit(solution)/shard_map/ppermute | solution.py:584
  290.7 6.7 %collective-permute-done.27 = f32[2,160,512]{2,1,0:T(8,128)S(1)} collective-permute-done((f32[2,160,512]{2,1,0:T(8,128)S(1)}, f32[2,160,512]{2,1,0:T(8,128)S(1)}, u32[]{:S(2)}, u32[]{:S(2)}) %collective-permute-start.27) | collective-permute-done | bytes 655392 | tf_op jit(solution)/shard_map/ppermute | solution.py:584
  301.2 38.0 %return_grads.1 = f32[33,80,128]{2,1,0:T(8,128)S(1)} custom-call(s32[32,2,128]{2,1,0:T(2,128)S(1)} %get-tuple-element.234.lists_ref, f32[1032,128]{1,0:T(8,128)S(1)} %copy-done.2), custom_call_target="tpu_custom_call" | custom-call | tf_op jit(solution)/shard_map/return_grads/pallas_call | solution.py:299
  339.2 4.7 %maximum_select_fusion.2 = f32[2,640,512]{2,1,0:T(8,128)} fusion(f32[2,320,512]{2,1,0:T(8,128)} %collective-permute-done.13, f32[2,320,512]{2,1,0:T(8,128)} %maximum_select_fusion.4, pred[]{:T(512)S(6)} %eq.75), kind=kLoop, calls=%fused_computation.106 | loop fusion | flops 1966080 | bytes 5242881 | tf_op jit(solution)/shard_map/jit(_where)/select_n | solution.py:599
  343.9 4.7 %maximum_select_fusion.3 = f32[2,640,512]{2,1,0:T(8,128)} fusion(f32[2,320,512]{2,1,0:T(8,128)} %collective-permute-done.28, f32[2,320,512]{2,1,0:T(8,128)} %maximum_select_fusion.5, pred[]{:T(512)S(6)} %eq.76), kind=kLoop, calls=%fused_computation.109 | loop fusion | flops 1966080 | bytes 5242881 | tf_op jit(solution)/shard_map/jit(_where)/select_n | solution.py:599
  349.1 3.6 broadcast_in_dim.204
  352.7 5.0 %while.25 = (s32[]{:T(128)}, f32[64,16384]{0,1:T(8,128)}, s32[]{:T(128)}, s32[64,128]{1,0:T(8,128)S(1)}, s32[64,128]{1,0:T(8,128)S(1)}, /*index=5*/s32[64,128]{1...) while((s32[]{:T(128)}, f32[64,16384]{0,1:T(8,128)}, ...), condition=%wide.region_9.10_spmd, body=%wide.region_4.9_spmd.sunk | while | flops 2082308 | bytes 39434784 | solution.py:719
  357.7 6.8 %copy.62.extra_ref = f32[64,16384]{1,0:T(8,128)} copy(f32[64,16384]{0,1:T(8,128)} %get-tuple-element.597) | data formatting | bytes 8388608 | tf_op jit(solution)/shard_map/while | solution.py:719
  366.7 21.6 %update_rows.1 = (f32[64,16384]{1,0:T(8,128)}, f32[64,16384]{1,0:T(8,128)}, f32[1,16384]{1,0:T(1,128)}) custom-call(s32[32,2,128]{2,1,0:T(2,128)S(1)} %copy-done.4, s32[1]{0:T(128)} %bitcast.62.more_ref, f32[2640,128]{1,0:T(8,128)S(1)} %bitcast.340, f32[64,16384]{1,0:T(8,128)S(1)} %bitcast.339, f32[64,16384]{1,0:T(8,128)} %bitcast.360, ...), custom_call_target="tpu_custom_call" | custom-call | tf_op jit(solution)/shard_map/update_rows/pallas_call | solution.py:556
  388.3 5.4 %maximum_select_fusion = f32[2,1280,512]{2,1,0:T(8,128)S(1)} fusion(f32[2,640,512]{2,1,0:T(8,128)} %collective-permute-done.14, f32[2,640,512]{2,1,0:T(8,128)} %maximum_select_fusion.2, pred[]{:T(512)S(6)} %eq.74), kind=kLoop, calls=%fused_computation.89 | loop fusion | flops 3932160 | bytes 10485761 | tf_op jit(solution)/shard_map/jit(_where)/select_n | solution.py:599
  396.8 5.4 %maximum_select_fusion.1 = f32[2,1280,512]{2,1,0:T(8,128)S(1)} fusion(f32[2,640,512]{2,1,0:T(8,128)} %collective-permute-done.29, f32[2,640,512]{2,1,0:T(8,128)} %maximum_select_fusion.3, pred[]{:T(512)S(6)} %eq.74), kind=kLoop, calls=%fused_computation.90 | loop fusion | flops 3932160 | bytes 10485761 | tf_op jit(solution)/shard_map/jit(_where)/select_n | solution.py:599
  423.8 4.2 fusion.25
  (275 shorter events, 96.8 us)
Async XLA Ops:
  131.1 21.1 %collective-permute-start.20 = (f32[640,512]{1,0:T(8,128)}, f32[640,512]{1,0:T(8,128)}, u32[]{:S(2)}, u32[]{:S(2)}) collective-permute-start(f32[640,512]{1,0:T(8,128)} %constant_dynamic-slice_fusion.4), channel_id=1, source_target_pairs={{0,1},{1,0},{2,3},{3,2},{4,5},{5,4},{6,7},{7,6},{8,9},{9,8},{10,11... | collective-permute-start | bytes 3932168 | tf_op jit(solution)/shard_map/ppermute | solution.py:584
  132.3 23.2 %collective-permute-start.5 = (f32[640,512]{1,0:T(8,128)}, f32[640,512]{1,0:T(8,128)}, u32[]{:S(2)}, u32[]{:S(2)}) collective-permute-start(f32[640,512]{1,0:T(8,128)} %constant_dynamic-slice_fusion.13), channel_id=1, source_target_pairs={{0,1},{1,0},{2,3},{3,2},{4,5},{5,4},{6,7},{7,6},{8,9},{9,8},{10,11... | collective-permute-start | bytes 3932168 | tf_op jit(solution)/shard_map/ppermute | solution.py:584
  144.7 31.3 %collective-permute-start = (f32[2,640,512]{2,1,0:T(8,128)}, f32[2,640,512]{2,1,0:T(8,128)}, u32[]{:S(2)}, u32[]{:S(2)}) collective-permute-start(f32[2,640,512]{2,1,0:T(8,128)} %fusion.29), channel_id=1, source_target_pairs={{0,1},{1,0},{2,3},{3,2},{4,5},{5,4},{6,7},{7,6},{8,9},{9,8},{10,11... | collective-permute-start | bytes 7864328 | tf_op jit(solution)/shard_map/ppermute | solution.py:584
  148.8 31.0 %collective-permute-start.15 = (f32[2,640,512]{2,1,0:T(8,128)}, f32[2,640,512]{2,1,0:T(8,128)}, u32[]{:S(2)}, u32[]{:S(2)}) collective-permute-start(f32[2,640,512]{2,1,0:T(8,128)} %fusion.26), channel_id=1, source_target_pairs={{0,1},{1,0},{2,3},{3,2},{4,5},{5,4},{6,7},{7,6},{8,9},{9,8},{10,11... | collective-permute-start | bytes 7864328 | tf_op jit(solution)/shard_map/ppermute | solution.py:584
  154.4 16.7 %collective-permute-start.21 = (f32[320,512]{1,0:T(8,128)S(1)}, f32[320,512]{1,0:T(8,128)S(1)}, u32[]{:S(2)}, u32[]{:S(2)}) collective-permute-start(f32[320,512]{1,0:T(8,128)S(1)} %constant_dynamic-slice_fusion.3), channel_id=1, source_target_pairs={{0,2},{1,3},{2,0},{3,1},{4,6},{5,7},{6,4},{7,5},{8,10},{9,11},{10,... | collective-permute-start | bytes 1966088 | tf_op jit(solution)/shard_map/ppermute | solution.py:584
  157.3 17.3 %collective-permute-start.6 = (f32[320,512]{1,0:T(8,128)S(1)}, f32[320,512]{1,0:T(8,128)S(1)}, u32[]{:S(2)}, u32[]{:S(2)}) collective-permute-start(f32[320,512]{1,0:T(8,128)S(1)} %constant_dynamic-slice_fusion.12), channel_id=1, source_target_pairs={{0,4},{1,5},{2,6},{3,7},{4,0},{5,1},{6,2},{7,3},{8,12},{9,13},{10,... | collective-permute-start | bytes 1966088 | tf_op jit(solution)/shard_map/ppermute | solution.py:584
  159.2 16.7 %copy-start.15 = (f32[1,1280,512]{2,1,0:T(8,128)S(1)}, f32[1,1280,512]{2,1,0:T(8,128)}, u32[]{:S(2)}) copy-start(f32[1,1280,512]{2,1,0:T(8,128)} %copy-done.14) | copy-start | bytes 7864324
  171.3 12.4 %collective-permute-start.22 = (f32[160,512]{1,0:T(8,128)S(1)}, f32[160,512]{1,0:T(8,128)S(1)}, u32[]{:S(2)}, u32[]{:S(2)}) collective-permute-start(f32[160,512]{1,0:T(8,128)S(1)} %constant_dynamic-slice_fusion.2), channel_id=1, source_target_pairs={{0,4},{1,5},{2,6},{3,7},{4,0},{5,1},{6,2},{7,3},{8,12},{9,13},{10,... | collective-permute-start | bytes 983048 | tf_op jit(solution)/shard_map/ppermute | solution.py:584
  174.7 9.2 %collective-permute-start.7 = (f32[160,512]{1,0:T(8,128)S(1)}, f32[160,512]{1,0:T(8,128)S(1)}, u32[]{:S(2)}, u32[]{:S(2)}) collective-permute-start(f32[160,512]{1,0:T(8,128)S(1)} %constant_dynamic-slice_fusion.11), channel_id=1, source_target_pairs={{0,2},{1,3},{2,0},{3,1},{4,6},{5,7},{6,4},{7,5},{8,10},{9,11},{10,... | collective-permute-start | bytes 983048 | tf_op jit(solution)/shard_map/ppermute | solution.py:584
  178.6 30.4 %collective-permute-start.1 = (f32[2,320,512]{2,1,0:T(8,128)S(1)}, f32[2,320,512]{2,1,0:T(8,128)S(1)}, u32[]{:S(2)}, u32[]{:S(2)}) collective-permute-start(f32[2,320,512]{2,1,0:T(8,128)S(1)} %constant_dynamic-slice_fusion.17), channel_id=1, source_target_pairs={{0,4},{1,5},{2,6},{3,7},{4,0},{5,1},{6,2},{7,3},{8,12},{9,13},{10,... | collective-permute-start | bytes 3932168 | tf_op jit(solution)/shard_map/ppermute | solution.py:584
  182.7 29.6 %collective-permute-start.16 = (f32[2,320,512]{2,1,0:T(8,128)S(1)}, f32[2,320,512]{2,1,0:T(8,128)S(1)}, u32[]{:S(2)}, u32[]{:S(2)}) collective-permute-start(f32[2,320,512]{2,1,0:T(8,128)S(1)} %constant_dynamic-slice_fusion.8), channel_id=1, source_target_pairs={{0,2},{1,3},{2,0},{3,1},{4,6},{5,7},{6,4},{7,5},{8,10},{9,11},{10,... | collective-permute-start | bytes 3932168 | tf_op jit(solution)/shard_map/ppermute | solution.py:584
  183.8 5.6 %collective-permute-start.23 = (f32[80,512]{1,0:T(8,128)S(1)}, f32[80,512]{1,0:T(8,128)S(1)}, u32[]{:S(2)}, u32[]{:S(2)}) collective-permute-start(f32[80,512]{1,0:T(8,128)S(1)} %constant_dynamic-slice_fusion.1), channel_id=1, source_target_pairs={{0,8},{1,9},{2,10},{3,11},{4,12},{5,13},{6,14},{7,15},{8,0},{9,1},... | collective-permute-start | bytes 491528 | tf_op jit(solution)/shard_map/ppermute | solution.py:584
  183.9 29.2 %collective-permute-start.8 = (f32[80,512]{1,0:T(8,128)S(1)}, f32[80,512]{1,0:T(8,128)S(1)}, u32[]{:S(2)}, u32[]{:S(2)}) collective-permute-start(f32[80,512]{1,0:T(8,128)S(1)} %constant_dynamic-slice_fusion.10), channel_id=1, source_target_pairs={{0,8},{1,9},{2,10},{3,11},{4,12},{5,13},{6,14},{7,15},{8,0},{9,1},... | collective-permute-start | bytes 491528 | tf_op jit(solution)/shard_map/ppermute | solution.py:584
  189.4 65.9 %collective-permute-start.24 = (f32[40,512]{1,0:T(8,128)S(1)}, f32[40,512]{1,0:T(8,128)S(1)}, u32[]{:S(2)}, u32[]{:S(2)}) collective-permute-start(f32[40,512]{1,0:T(8,128)S(1)} %constant_dynamic-slice_fusion), channel_id=1, source_target_pairs={{0,16},{1,17},{2,18},{3,19},{4,20},{5,21},{6,22},{7,23},{8,24},{9,... | collective-permute-start | bytes 245768 | tf_op jit(solution)/shard_map/ppermute | solution.py:584
  209.3 16.2 %collective-permute-start.2 = (f32[2,160,512]{2,1,0:T(8,128)S(1)}, f32[2,160,512]{2,1,0:T(8,128)S(1)}, u32[]{:S(2)}, u32[]{:S(2)}) collective-permute-start(f32[2,160,512]{2,1,0:T(8,128)S(1)} %constant_dynamic-slice_fusion.16), channel_id=1, source_target_pairs={{0,2},{1,3},{2,0},{3,1},{4,6},{5,7},{6,4},{7,5},{8,10},{9,11},{10,... | collective-permute-start | bytes 1966088 | tf_op jit(solution)/shard_map/ppermute | solution.py:584
  212.6 13.6 %collective-permute-start.17 = (f32[2,160,512]{2,1,0:T(8,128)S(1)}, f32[2,160,512]{2,1,0:T(8,128)S(1)}, u32[]{:S(2)}, u32[]{:S(2)}) collective-permute-start(f32[2,160,512]{2,1,0:T(8,128)S(1)} %constant_dynamic-slice_fusion.7), channel_id=1, source_target_pairs={{0,4},{1,5},{2,6},{3,7},{4,0},{5,1},{6,2},{7,3},{8,12},{9,13},{10,... | collective-permute-start | bytes 1966088 | tf_op jit(solution)/shard_map/ppermute | solution.py:584
  213.2 38.6 %collective-permute-start.9 = (f32[40,512]{1,0:T(8,128)S(1)}, f32[40,512]{1,0:T(8,128)S(1)}, u32[]{:S(2)}, u32[]{:S(2)}) collective-permute-start(f32[40,512]{1,0:T(8,128)S(1)} %constant_dynamic-slice_fusion.9), channel_id=1, source_target_pairs={{0,16},{1,17},{2,18},{3,19},{4,20},{5,21},{6,22},{7,23},{8,24},{9,... | collective-permute-start | bytes 245768 | tf_op jit(solution)/shard_map/ppermute | solution.py:584
  225.7 12.5 %collective-permute-start.3 = (f32[2,80,512]{2,1,0:T(8,128)S(1)}, f32[2,80,512]{2,1,0:T(8,128)S(1)}, u32[]{:S(2)}, u32[]{:S(2)}) collective-permute-start(f32[2,80,512]{2,1,0:T(8,128)S(1)} %constant_dynamic-slice_fusion.15), channel_id=1, source_target_pairs={{0,8},{1,9},{2,10},{3,11},{4,12},{5,13},{6,14},{7,15},{8,0},{9,1},... | collective-permute-start | bytes 983048 | tf_op jit(solution)/shard_map/ppermute | solution.py:584
  226.3 16.5 %collective-permute-start.18 = (f32[2,80,512]{2,1,0:T(8,128)S(1)}, f32[2,80,512]{2,1,0:T(8,128)S(1)}, u32[]{:S(2)}, u32[]{:S(2)}) collective-permute-start(f32[2,80,512]{2,1,0:T(8,128)S(1)} %constant_dynamic-slice_fusion.6), channel_id=1, source_target_pairs={{0,8},{1,9},{2,10},{3,11},{4,12},{5,13},{6,14},{7,15},{8,0},{9,1},... | collective-permute-start | bytes 983048 | tf_op jit(solution)/shard_map/ppermute | solution.py:584
  238.3 13.5 %collective-permute-start.4 = (f32[2,40,512]{2,1,0:T(8,128)S(1)}, f32[2,40,512]{2,1,0:T(8,128)S(1)}, u32[]{:S(2)}, u32[]{:S(2)}) collective-permute-start(f32[2,40,512]{2,1,0:T(8,128)S(1)} %constant_dynamic-slice_fusion.14), channel_id=1, source_target_pairs={{0,16},{1,17},{2,18},{3,19},{4,20},{5,21},{6,22},{7,23},{8,24},{9,... | collective-permute-start | bytes 491528 | tf_op jit(solution)/shard_map/ppermute | solution.py:584
  242.9 12.4 %collective-permute-start.19 = (f32[2,40,512]{2,1,0:T(8,128)S(1)}, f32[2,40,512]{2,1,0:T(8,128)S(1)}, u32[]{:S(2)}, u32[]{:S(2)}) collective-permute-start(f32[2,40,512]{2,1,0:T(8,128)S(1)} %constant_dynamic-slice_fusion.5), channel_id=1, source_target_pairs={{0,16},{1,17},{2,18},{3,19},{4,20},{5,21},{6,22},{7,23},{8,24},{9,... | collective-permute-start | bytes 491528 | tf_op jit(solution)/shard_map/ppermute | solution.py:584
  251.9 10.8 %collective-permute-start.10 = (f32[2,40,512]{2,1,0:T(8,128)S(1)}, f32[2,40,512]{2,1,0:T(8,128)S(1)}, u32[]{:S(2)}, u32[]{:S(2)}) collective-permute-start(f32[2,40,512]{2,1,0:T(8,128)S(1)} %pad_maximum_fusion.5), channel_id=1, source_target_pairs={{0,16},{1,17},{2,18},{3,19},{4,20},{5,21},{6,22},{7,23},{8,24},{9,... | collective-permute-start | bytes 491528 | tf_op jit(solution)/shard_map/ppermute | solution.py:584
  255.5 10.8 %collective-permute-start.25 = (f32[2,40,512]{2,1,0:T(8,128)S(1)}, f32[2,40,512]{2,1,0:T(8,128)S(1)}, u32[]{:S(2)}, u32[]{:S(2)}) collective-permute-start(f32[2,40,512]{2,1,0:T(8,128)S(1)} %pad_maximum_fusion.6), channel_id=1, source_target_pairs={{0,16},{1,17},{2,18},{3,19},{4,20},{5,21},{6,22},{7,23},{8,24},{9,... | collective-permute-start | bytes 491528 | tf_op jit(solution)/shard_map/ppermute | solution.py:584
  262.8 10.7 %collective-permute-start.11 = (f32[2,80,512]{2,1,0:T(8,128)S(1)}, f32[2,80,512]{2,1,0:T(8,128)S(1)}, u32[]{:S(2)}, u32[]{:S(2)}) collective-permute-start(f32[2,80,512]{2,1,0:T(8,128)S(1)} %maximum_select_fusion.8), channel_id=1, source_target_pairs={{0,8},{1,9},{2,10},{3,11},{4,12},{5,13},{6,14},{7,15},{8,0},{9,1},... | collective-permute-start | bytes 983048 | tf_op jit(solution)/shard_map/ppermute | solution.py:584
  266.3 12.2 %collective-permute-start.26 = (f32[2,80,512]{2,1,0:T(8,128)S(1)}, f32[2,80,512]{2,1,0:T(8,128)S(1)}, u32[]{:S(2)}, u32[]{:S(2)}) collective-permute-start(f32[2,80,512]{2,1,0:T(8,128)S(1)} %maximum_select_fusion.9), channel_id=1, source_target_pairs={{0,8},{1,9},{2,10},{3,11},{4,12},{5,13},{6,14},{7,15},{8,0},{9,1},... | collective-permute-start | bytes 983048 | tf_op jit(solution)/shard_map/ppermute | solution.py:584
  273.5 13.9 %collective-permute-start.12 = (f32[2,160,512]{2,1,0:T(8,128)S(1)}, f32[2,160,512]{2,1,0:T(8,128)S(1)}, u32[]{:S(2)}, u32[]{:S(2)}) collective-permute-start(f32[2,160,512]{2,1,0:T(8,128)S(1)} %maximum_select_fusion.6), channel_id=1, source_target_pairs={{0,2},{1,3},{2,0},{3,1},{4,6},{5,7},{6,4},{7,5},{8,10},{9,11},{10,... | collective-permute-start | bytes 1966088 | tf_op jit(solution)/shard_map/ppermute | solution.py:584
  278.5 18.9 %collective-permute-start.27 = (f32[2,160,512]{2,1,0:T(8,128)S(1)}, f32[2,160,512]{2,1,0:T(8,128)S(1)}, u32[]{:S(2)}, u32[]{:S(2)}) collective-permute-start(f32[2,160,512]{2,1,0:T(8,128)S(1)} %maximum_select_fusion.7), channel_id=1, source_target_pairs={{0,4},{1,5},{2,6},{3,7},{4,0},{5,1},{6,2},{7,3},{8,12},{9,13},{10,... | collective-permute-start | bytes 1966088 | tf_op jit(solution)/shard_map/ppermute | solution.py:584
  281.7 19.2 %copy-start.2 = (f32[1032,128]{1,0:T(8,128)S(1)}, f32[1032,128]{1,0:T(8,128)}, u32[]{:S(2)}) copy-start(f32[1032,128]{1,0:T(8,128)} %get-tuple-element.275.source_ref) | copy-start | bytes 1585156
  288.6 50.6 %collective-permute-start.13 = (f32[2,320,512]{2,1,0:T(8,128)}, f32[2,320,512]{2,1,0:T(8,128)}, u32[]{:S(2)}, u32[]{:S(2)}) collective-permute-start(f32[2,320,512]{2,1,0:T(8,128)} %maximum_select_fusion.4), channel_id=1, source_target_pairs={{0,4},{1,5},{2,6},{3,7},{4,0},{5,1},{6,2},{7,3},{8,12},{9,13},{10,... | collective-permute-start | bytes 3932168 | tf_op jit(solution)/shard_map/ppermute | solution.py:584
  298.6 45.3 %collective-permute-start.28 = (f32[2,320,512]{2,1,0:T(8,128)}, f32[2,320,512]{2,1,0:T(8,128)}, u32[]{:S(2)}, u32[]{:S(2)}) collective-permute-start(f32[2,320,512]{2,1,0:T(8,128)} %maximum_select_fusion.5), channel_id=1, source_target_pairs={{0,2},{1,3},{2,0},{3,1},{4,6},{5,7},{6,4},{7,5},{8,10},{9,11},{10,... | collective-permute-start | bytes 3932168 | tf_op jit(solution)/shard_map/ppermute | solution.py:584
  343.9 44.4 %collective-permute-start.14 = (f32[2,640,512]{2,1,0:T(8,128)}, f32[2,640,512]{2,1,0:T(8,128)}, u32[]{:S(2)}, u32[]{:S(2)}) collective-permute-start(f32[2,640,512]{2,1,0:T(8,128)} %maximum_select_fusion.2), channel_id=1, source_target_pairs={{0,1},{1,0},{2,3},{3,2},{4,5},{5,4},{6,7},{7,6},{8,9},{9,8},{10,11... | collective-permute-start | bytes 7864328 | tf_op jit(solution)/shard_map/ppermute | solution.py:584
  348.6 48.2 %collective-permute-start.29 = (f32[2,640,512]{2,1,0:T(8,128)}, f32[2,640,512]{2,1,0:T(8,128)}, u32[]{:S(2)}, u32[]{:S(2)}) collective-permute-start(f32[2,640,512]{2,1,0:T(8,128)} %maximum_select_fusion.3), channel_id=1, source_target_pairs={{0,1},{1,0},{2,3},{3,2},{4,5},{5,4},{6,7},{7,6},{8,9},{9,8},{10,11... | collective-permute-start | bytes 7864328 | tf_op jit(solution)/shard_map/ppermute | solution.py:584
  (56 other events, 248.5 us)

commit v2 on v1

--- a/solution.py
+++ b/solution.py
@@ -58,19 +58,75 @@
 
     lax.fori_loop(low, high, step, 0)
 
-
-def route_kernel(
+STEP = 5
+BETA_ONE = 0.9
+BETA_TWO = 0.999
+EPSILON = 1e-08
+DECAY = 0.01
+RATE_DENSE = 0.02
+RATE_ROWS = 0.3
+
+def axis_orders(n):
+    bits = [1 << i for i in range(n.bit_length() - 1)]
+    core, rest = bits[:1], bits[1:]
+    a = len(rest) // 3
+    b = (len(rest) - a) // 2
+    x, y, z = rest[:a], rest[a : a + b], rest[a + b :]
+    return core + x + y + z, core + y + x + z, core + z + x + y, core + z + y + x
+
+
+def bit_of(me, bit):
+    return lax.rem(lax.div(me, bit), 2)
+
+
+def start_of(me, order, rows):
+    start = 0
+    for bit in order:
+        rows = rows // 2
+        start = start + bit_of(me, bit) * rows
+    return start
+
+
+def rows_at(start, count):
+    return pl.ds(pl.multiple_of(start, 8), count)
+
+
+def halving(me, source, stages, sends, receives, chain, order, i):
+    bit = order[i]
+    before = source if i == 0 else stages[i - 1]
+    half = stages[i].shape[-2]
+    peer = me ^ bit
+    at = rows_at((1 - bit_of(me, bit)) * half, half)
+    return pltpu.make_async_remote_copy(
+        src_ref=before.at[at] if len(before.shape) == 2 else before.at[:, at],
+        dst_ref=stages[i],
+        send_sem=sends.at[chain, i],
+        recv_sem=receives.at[chain, i],
+        device_id=(peer,),
+        device_id_type=MESH,
+    )
+
+
+def forward_kernel(
     sizes,
-    ids_ref, lengths_ref, counts_ref, mask_ref, labels_ref, homes_ref,
-    fields_ref, pos_ref, owner_ref, rank_ref, local_ref, mine_ref, theirs_ref, stat_ref,
-    outbox, inbox, message, replies, lists, field_scratch,
-    send_a, recv_a, send_b, recv_b, local_sem,
+    ids_ref, lengths_ref, counts_ref, mask_ref, labels_ref, homes_ref, table_ref,
+    items_ref, experts_m_ref, experts_v_ref, tail_m_ref, tail_v_ref,
+    fields_ref, pos_ref, owner_ref, rank_ref, local_ref, mine_ref, theirs_ref, stat_ref, lines_ref,
+    moments_a_ref, moments_b_ref, moments_c_ref, moments_d_ref,
+    outbox, inbox, message, replies, lists, field_scratch, asked_smem, rows_ref, rows_out,
+    kept_a, kept_b, *rest,
 ):
-    n, cap, tables, bag, tasks, per_table, block_rows, rows_dev = sizes
+    n, cap, tables, bag, tasks, experts, gap, per_table, block_rows, rows_dev = sizes
+    levels = n.bit_length() - 1
+    stages = [list(rest[c * (levels - 1) : (c + 1) * (levels - 1)]) for c in range(4)]
+    for stage, final in zip(stages, (moments_a_ref, moments_b_ref, moments_c_ref, moments_d_ref)):
+        stage.append(final)
+    send_a, recv_a, send_b, recv_b, send_c, recv_c, send_m, recv_m, sems = rest[4 * (levels - 1) :]
     rows = tables * bag
     me = lax.axis_index("dev")
     shift = lax.rem(me * 13, n)
     per_pair = LANES // n
+    orders = axis_orders(n)
     table_of = lax.div(iota((rows, LANES), 0), bag)
     slot_of = lax.rem(iota((rows, LANES), 0), bag)
     expand = jnp.where(lax.div(iota((rows, tables), 0), bag) == iota((rows, tables), 1), 1.0, 0.0).astype(BF16)
@@ -89,9 +145,81 @@
     spread = dot(pick, high, NT) + dot(pick, middle, NT) + dot(pick, low, NT)
     outbox[...] = spread.reshape(n, 8, LANES)
     greet_all(n, me)
-    own_copy = pltpu.make_async_copy(outbox.at[me], inbox.at[me], local_sem)
+    own_copy = pltpu.make_async_copy(outbox.at[me], inbox.at[me], sems.at[0])
     own_copy.start()
     for_range(1, n, lambda k: exchange(n, me, outbox, inbox, send_a, recv_a, k).start())
+    sources = ((experts_m_ref, experts_v_ref), (tail_m_ref, tail_v_ref))
+    parity = bit_of(me, 1)
+
+    def first_hops():
+        hops = []
+        for c in range(4):
+            half = stages[c][0].shape[1]
+            for w in range(2):
+                whole = sources[c // 2][w].at[c % 2]
+                hops.append(
+                    pltpu.make_async_remote_copy(
+                        src_ref=whole.at[rows_at((1 - parity) * half, half)],
+                        dst_ref=stages[c][0].at[w],
+                        send_sem=send_m.at[c, levels + w],
+                        recv_sem=recv_m.at[c, levels + w],
+                        device_id=(me ^ 1,),
+                        device_id_type=MESH,
+                    )
+                )
+        return hops
+
+    keeps = []
+    for c, kept in ((0, kept_a), (1, kept_b)):
+        half = kept.shape[1]
+        for w in range(2):
+            keeps.append(
+                pltpu.make_async_copy(
+                    sources[0][w].at[c, rows_at(parity * half, half)], kept.at[w], sems.at[1 + 2 * c + w]
+                )
+            )
+    for copy in first_hops() + keeps:
+        copy.start()
+
+    def chosen(c, i, start, count):
+        bit = orders[c][i]
+        if c < 2:
+            return bit_of(items_ref[c], bit) == bit_of(me, bit)
+        towers = tasks * 64
+        row = (c - 2) * tail_m_ref.shape[1] + start + iota((count, LANES), 0)
+        item = lax.div(row, 64) + experts + tasks
+        for part in range(2):
+            inside = (row >= towers + part * gap) & (row < towers + part * gap + tasks * experts)
+            item = jnp.where(inside, experts + lax.div(row - towers - part * gap, experts), item)
+        item = jnp.where(row >= towers + 2 * gap, experts + 2 * tasks, item)
+        home = jnp.zeros((count, LANES), I32)
+        for k in range(experts, experts + 2 * tasks + 1):
+            home = jnp.where(item == k, items_ref[k], home)
+        return (bit_of(home, bit) == bit_of(me, bit))[:, :1]
+
+    def settle(i):
+        if i == 0:
+            for copy in first_hops() + keeps:
+                copy.wait()
+        for c in range(4):
+            order, stage = orders[c], stages[c]
+            if i > 0:
+                halving(me, None, stage, send_m, recv_m, c, order, i).wait()
+            half = stage[i].shape[1]
+            mine = rows_at(bit_of(me, order[i]) * half, half)
+            total = 2 * stage[0].shape[1]
+            flag = chosen(c, i, start_of(me, order[: i + 1], total), half)
+            for w in range(2):
+                if i > 0:
+                    kept = stage[i - 1][w, mine, :]
+                elif c < 2:
+                    kept = (kept_a, kept_b)[c][w]
+                else:
+                    kept = sources[1][w][c - 2, mine, :]
+                stage[i][w] = jnp.where(flag, kept, stage[i][w])
+            if i + 1 < levels:
+                halving(me, None, stage, send_m, recv_m, c, order, i + 1).start()
+
     homes = homes_ref[...]
     blocks = homes.shape[1]
     homes_rows = (
@@ -178,15 +306,15 @@
     def post(k):
         o = me ^ k
         tile = message[o]
-        rows_out = []
+        rows_list = []
         for parity in range(2):
             count = tile[2 + parity : 3 + parity]
             got = [lists[parity, pl.ds(part * n + o, 1), :].astype(I32) for part in range(4)]
             asked = jnp.where(got[0] > 0, (got[0] - 1) * LANES + got[1], rows_dev)
             slot = jnp.where(got[0] > 0, (got[2] - 1) * LANES + got[3], tables // 2 * LANES)
-            rows_out.append(jnp.where(is_last, count, asked))
+            rows_list.append(jnp.where(is_last, count, asked))
             mine_ref[o, parity : parity + 1, :] = jnp.where(is_last, count, slot)
-        tile = jnp.where(sub == 0, rows_out[0], jnp.where(sub == 1, rows_out[1], tile))
+        tile = jnp.where(sub == 0, rows_list[0], jnp.where(sub == 1, rows_list[1], tile))
         message[o] = jnp.where(sub == 4, most, jnp.where(sub == 5, weight_count, tile))
 
     def post_and_send(k):
@@ -195,119 +323,243 @@
 
     for_range(1, n, post_and_send)
     post(0)
-    own_copy = pltpu.make_async_copy(message.at[me], replies.at[me], local_sem)
+    own_copy = pltpu.make_async_copy(message.at[me], replies.at[me], sems.at[0])
     own_copy.start()
+    settle(0)
+    width = table_ref.shape[0]
+    rows_ref[rows_dev:, :] = jnp.zeros((rows_ref.shape[0] - rows_dev, LANES), F32)
+
+    def turn(b):
+        at = pl.ds(pl.multiple_of(b * LANES, LANES), LANES)
+        rows_ref[at, :] = jnp.concatenate([table_ref[:, at]] * (LANES // width), axis=0).T
+
+    for_range(0, rows_dev // LANES, turn)
     for_range(1, n, lambda k: exchange(n, me, message, replies, send_b, recv_b, k).wait())
     own_copy.wait()
 
     def take(s, carry):
         most, total = carry
         tile = replies[s]
-        theirs_ref[s] = tile[0:2]
+        theirs_ref[s] = jnp.clip(tile[0:2], 0, rows_dev)
         return jnp.maximum(most, tile), total + tile
 
     most, total = lax.fori_loop(0, n, take, (jnp.zeros((8, LANES), I32), jnp.zeros((8, LANES), I32)))
     stat_ref[...] = jnp.where(sub == 4, most, total)
-
-
-def route(n, cap, row_ids, lengths, counts, mask, labels, row_home, rows_dev):
-    samples, tables, bag = row_ids.shape
-    tasks = labels.shape[1]
-    per_table = row_home.shape[1] // n
-    block_rows = rows_dev // (tables * per_table)
-    sizes = (n, cap, tables, bag, tasks, per_table, block_rows, rows_dev)
-    ids = row_ids.transpose(1, 2, 0).reshape(tables * bag, samples)
-    vmem = pl.BlockSpec(memory_space=pltpu.VMEM)
-    smem = pl.BlockSpec(memory_space=pltpu.SMEM)
-    slots = jax.ShapeDtypeStruct((tables * bag, LANES), I32)
-    lists = jax.ShapeDtypeStruct((n, 2, LANES), I32)
-    return pl.pallas_call(
-        functools.partial(route_kernel, sizes),
-        out_shape=(
-            jax.ShapeDtypeStruct((8, LANES), F32), slots, slots, slots, slots, lists, lists,
-            jax.ShapeDtypeStruct((8, LANES), I32),
-        ),
-        in_specs=[vmem, vmem, smem, vmem, vmem, vmem],
-        out_specs=(vmem,) * 8,
-        scratch_shapes=[
-            pltpu.VMEM((n, 8, LANES), F32), pltpu.VMEM((n, 8, LANES), F32),
-            pltpu.VMEM((n, 8, LANES), I32), pltpu.VMEM((n, 8, LANES), I32),
-            pltpu.VMEM((2, 4 * n, LANES), F32), pltpu.VMEM((LANES, LANES), F32),
-            pltpu.SemaphoreType.DMA((n,)), pltpu.SemaphoreType.DMA((n,)),
-            pltpu.SemaphoreType.DMA((n,)), pltpu.SemaphoreType.DMA((n,)),
-            pltpu.SemaphoreType.DMA,
-        ],
-        compiler_params=pltpu.CompilerParams(collective_id=0, has_side_effects=True, vmem_limit_bytes=32 * 2**20),
-        name="route",
-    )(ids, lengths.T, counts, mask.reshape(1, samples), labels.T, row_home)
-
-STEP = 5
-BETA_ONE = 0.9
-BETA_TWO = 0.999
-EPSILON = 1e-08
-DECAY = 0.01
-RATE_DENSE = 0.02
-RATE_ROWS = 0.3
-
-def rows_exchange_kernel(n, cap, spare, from_table, lists_ref, source_ref, lines_ref, *scratch):
-    if from_table:
-        rows_ref, outbox, sends, receives = scratch
-    else:
-        outbox, sends, receives = scratch
-        rows_ref = source_ref
-    me = lax.axis_index("dev")
-    greet_all(n, me)
+    to_scalars = pltpu.make_async_copy(theirs_ref, asked_smem, sems.at[0])
+    to_scalars.start()
+    to_scalars.wait()
     lines_ref[n] = jnp.zeros((cap, LANES), F32)
-    if from_table:
-        width, rows_dev = source_ref.shape
-        rows_ref[rows_dev : rows_dev + spare, :] = jnp.zeros((spare, LANES), F32)
-
-        def turn(b):
-            at = pl.ds(pl.multiple_of(b * LANES, LANES), LANES)
-            piece = source_ref[:, at]
-            rows_ref[at, :] = jnp.concatenate([piece] * (LANES // width), axis=0).T
-
-        for_range(0, rows_dev // LANES, turn)
+    collect = collector(cap, asked_smem, rows_ref)
+
+    def collect_and_send(i):
+        k = n - i
+        collect(me ^ k, rows_out, me ^ k)
+        exchange(n, me, rows_out, lines_ref, send_c, recv_c, k).start()
+
+    for_range(1, n // 2 + 1, collect_and_send)
+    settle(1)
+    for_range(n // 2 + 1, n, collect_and_send)
+    collect(me, lines_ref, me)
+    for i in range(2, levels):
+        settle(i)
+    for_range(1, n, lambda k: exchange(n, me, rows_out, lines_ref, send_c, recv_c, k).wait())
+
+
+def collector(cap, lists_ref, rows_ref):
     left = iota((1, LANES), 1) < LANES // 2
 
     def collect(peer, target, slot):
-        def lines(g, carry):
+        def lines(g):
             for i in range(8):
                 r = g * 8 + i
                 even = rows_ref[pl.ds(lists_ref[peer, 0, r], 1), :]
                 odd = rows_ref[pl.ds(lists_ref[peer, 1, r], 1), :]
                 target[slot, pl.ds(r, 1), :] = jnp.where(left, even, odd)
-            return carry
-
-        lax.fori_loop(0, cap // 8, lines, 0)
+
+        for_range(0, cap // 8, lines)
+
+    return collect
+
+
+def chain_rows(features, half_tail):
+    return features, features, half_tail, half_tail
+
+
+def forward(n, cap, row_ids, lengths, counts, mask, labels, row_home, table, mat_home, experts_m, experts_v, tail_m, tail_v):
+    samples, tables, bag = row_ids.shape
+    rows_dev, width = table.shape
+    tasks = labels.shape[1]
+    experts, features, hidden = experts_m.shape
+    half_tail = tail_m.shape[1]
+    per_table = row_home.shape[1] // n
+    block_rows = rows_dev // (tables * per_table)
+    levels = n.bit_length() - 1
+    sizes = (n, cap, tables, bag, tasks, experts, GAP, per_table, block_rows, rows_dev)
+    ids = row_ids.transpose(1, 2, 0).reshape(tables * bag, samples)
+    vmem = pl.BlockSpec(memory_space=pltpu.VMEM)
+    smem = pl.BlockSpec(memory_space=pltpu.SMEM)
+    hbm = pl.BlockSpec(memory_space=pl.ANY)
+    slots = jax.ShapeDtypeStruct((tables * bag, LANES), I32)
+    lists = jax.ShapeDtypeStruct((n, 2, LANES), I32)
+    chains = chain_rows(features, half_tail)
+    small = pltpu.VMEM((n, 8, LANES), F32)
+    numbers = pltpu.VMEM((n, 8, LANES), I32)
+    dma = pltpu.SemaphoreType.DMA((n,))
+    hops = pltpu.SemaphoreType.DMA((4, levels + 2))
+    return pl.pallas_call(
+        functools.partial(forward_kernel, sizes),
+        out_shape=(
+            jax.ShapeDtypeStruct((8, LANES), F32), slots, slots, slots, slots, lists, lists,
+            jax.ShapeDtypeStruct((8, LANES), I32), jax.ShapeDtypeStruct((n + 1, cap, LANES), F32),
+        ) + tuple(jax.ShapeDtypeStruct((2, count // n, hidden), F32) for count in chains),
+        in_specs=[vmem, vmem, smem, vmem, vmem, vmem, vmem, smem, hbm, hbm, vmem, vmem],
+        out_specs=(vmem,) * 13,
+        scratch_shapes=[
+            small, small, numbers, numbers,
+            pltpu.VMEM((2, 4 * n, LANES), F32), pltpu.VMEM((LANES, LANES), F32),
+            pltpu.SMEM((n, 2, LANES), I32), pltpu.VMEM((rows_dev + 8, LANES), F32), pltpu.VMEM((n, cap, LANES), F32),
+            pltpu.VMEM((2, features // 2, hidden), F32), pltpu.VMEM((2, features // 2, hidden), F32),
+        ]
+        + [pltpu.VMEM((2, count >> (i + 1), hidden), F32) for count in chains for i in range(levels - 1)]
+        + [dma] * 6 + [hops] * 2 + [pltpu.SemaphoreType.DMA((8,))],
+        compiler_params=pltpu.CompilerParams(collective_id=0, has_side_effects=True, vmem_limit_bytes=56 * 2**20),
+        name="forward",
+    )(
+        ids, lengths.T, counts, mask.reshape(1, samples), labels.T, row_home, table.T,
+        mat_home, experts_m, experts_v, tail_m, tail_v,
+    )
+
+
+def backward_kernel(n, cap, lists_ref, rows_ref, grad_a_ref, grad_b_ref, grad_tail_ref, lines_ref, *rest):
+    levels = n.bit_length() - 1
+    finals, rest = rest[:4], rest[4:]
+    stages = [list(rest[c * (levels - 1) : (c + 1) * (levels - 1)]) + [finals[c]] for c in range(4)]
+    rows_out, send_c, recv_c, sends, receives = rest[4 * (levels - 1) :]
+    me = lax.axis_index("dev")
+    orders = axis_orders(n)
+    sources = (grad_a_ref, grad_b_ref, grad_tail_ref.at[0], grad_tail_ref.at[1])
+    greet_all(n, me)
+
+    def begin(i):
+        for c in range(4):
+            halving(me, sources[c], stages[c], sends, receives, c, orders[c], i).start()
+
+    def settle(i):
+        for c in range(4):
+            halving(me, sources[c], stages[c], sends, receives, c, orders[c], i).wait()
+            before = sources[c] if i == 0 else stages[c][i - 1]
+            half = stages[c][i].shape[0]
+            stages[c][i][...] += before[rows_at(bit_of(me, orders[c][i]) * half, half), :]
+            if i + 1 < levels:
+                halving(me, sources[c], stages[c], sends, receives, c, orders[c], i + 1).start()
+
+    begin(0)
+    lines_ref[n] = jnp.zeros((cap, LANES), F32)
+    collect = collector(cap, lists_ref, rows_ref)
 
     def collect_and_send(i):
         k = n - i
-        collect(me ^ k, outbox, me ^ k)
-        exchange(n, me, outbox, lines_ref, sends, receives, k).start()
-
-    for_range(1, n, collect_and_send)
+        collect(me ^ k, rows_out, me ^ k)
+        exchange(n, me, rows_out, lines_ref, send_c, recv_c, k).start()
+
+    for_range(1, n // 4 + 1, collect_and_send)
+    settle(0)
+    for_range(n // 4 + 1, n // 2 + 1, collect_and_send)
+    for_range(n // 2 + 1, n, collect_and_send)
     collect(me, lines_ref, me)
-    for_range(1, n, lambda k: exchange(n, me, outbox, lines_ref, sends, receives, k).wait())
-
-
-def rows_exchange(n, cap, lists, source, from_table, collective_id, name):
-    spare = 8
-    scratch = [pltpu.VMEM((n, cap, LANES), F32), pltpu.SemaphoreType.DMA((n,)), pltpu.SemaphoreType.DMA((n,))]
-    if from_table:
-        scratch = [pltpu.VMEM((source.shape[1] + spare, LANES), F32)] + scratch
+    for i in range(1, levels):
+        settle(i)
+    for_range(1, n, lambda k: exchange(n, me, rows_out, lines_ref, send_c, recv_c, k).wait())
+
+
+def backward(n, cap, lists, rows, grad_a, grad_b, grad_tail):
+    levels = n.bit_length() - 1
+    features, hidden = grad_a.shape
+    chains = chain_rows(features, grad_tail.shape[1])
+    vmem = pl.BlockSpec(memory_space=pltpu.VMEM)
     return pl.pallas_call(
-        functools.partial(rows_exchange_kernel, n, cap, spare, from_table),
-        out_shape=jax.ShapeDtypeStruct((n + 1, cap, LANES), F32),
-        in_specs=[pl.BlockSpec(memory_space=pltpu.SMEM), pl.BlockSpec(memory_space=pltpu.VMEM)],
-        out_specs=pl.BlockSpec(memory_space=pltpu.VMEM),
-        scratch_shapes=scratch,
-        compiler_params=pltpu.CompilerParams(
-            collective_id=collective_id, has_side_effects=True, vmem_limit_bytes=40 * 2**20
-        ),
-        name=name,
-    )(lists, source)
-
+        functools.partial(backward_kernel, n, cap),
+        out_shape=(jax.ShapeDtypeStruct((n + 1, cap, LANES), F32),)
+        + tuple(jax.ShapeDtypeStruct((count // n, hidden), F32) for count in chains),
+        in_specs=[pl.BlockSpec(memory_space=pltpu.SMEM)] + [vmem] * 4,
+        out_specs=(vmem,) * 5,
+        scratch_shapes=[pltpu.VMEM((count >> (i + 1), hidden), F32) for count in chains for i in range(levels - 1)]
+        + [pltpu.VMEM((n, cap, LANES), F32)]
+        + [pltpu.SemaphoreType.DMA((n,))] * 2 + [pltpu.SemaphoreType.DMA((4, levels))] * 2,
+        compiler_params=pltpu.CompilerParams(collective_id=1, has_side_effects=True, vmem_limit_bytes=40 * 2**20),
+        name="backward",
+    )(lists, rows, grad_a, grad_b, grad_tail)
+
+
+def spread_kernel(n, *refs):
+    grads, moments_in, weights = refs[0:4], refs[4:8], refs[8:12]
+    wholes = refs[12:16]
+    news = refs[16:20]
+    sends, receives, local = refs[20:]
+    levels = n.bit_length() - 1
+    me = lax.axis_index("dev")
+    orders = axis_orders(n)
+    copies = []
+    starts = []
+    for c in range(4):
+        count = grads[c].shape[0]
+        total = wholes[c].shape[1]
+        start = start_of(me, orders[c], total)
+        first, second = moments(moments_in[c][0], moments_in[c][1], grads[c][...])
+        news[c][0] = stepped(weights[c][...], first, second)
+        news[c][1] = grads[c][...]
+        copies.append(pltpu.make_async_copy(news[c], wholes[c].at[:, rows_at(start, count)], local.at[c]))
+    for copy in copies:
+        copy.start()
+    greet_bits(n, me)
+    for copy in copies:
+        copy.wait()
+
+    def doubling(c, i):
+        order = orders[c]
+        total = wholes[c].shape[1]
+        size = total >> (i + 1)
+        at = rows_at(start_of(me, order[: i + 1], total), size)
+        return pltpu.make_async_remote_copy(
+            src_ref=wholes[c].at[:, at],
+            dst_ref=wholes[c].at[:, at],
+            send_sem=sends.at[c, i],
+            recv_sem=receives.at[c, i],
+            device_id=(me ^ order[i],),
+            device_id_type=MESH,
+        )
+
+    for i in reversed(range(levels)):
+        for c in range(4):
+            if i + 1 < levels:
+                doubling(c, i + 1).wait()
+            doubling(c, i).start()
+    for c in range(4):
+        doubling(c, 0).wait()
+
+
+def greet_bits(n, me):
+    barrier = pltpu.get_barrier_semaphore()
+    levels = n.bit_length() - 1
+    for i in range(levels):
+        pl.semaphore_signal(barrier, inc=1, device_id=(me ^ (1 << i),), device_id_type=MESH)
+    pl.semaphore_wait(barrier, levels)
+
+
+def spread(n, grads, moments_in, weights):
+    levels = n.bit_length() - 1
+    hidden = grads[0].shape[1]
+    vmem = pl.BlockSpec(memory_space=pltpu.VMEM)
+    return pl.pallas_call(
+        functools.partial(spread_kernel, n),
+        out_shape=tuple(jax.ShapeDtypeStruct((2, g.shape[0] * n, hidden), F32) for g in grads),
+        in_specs=[vmem] * 12,
+        out_specs=(vmem,) * 4,
+        scratch_shapes=[pltpu.VMEM((2,) + g.shape, F32) for g in grads]
+        + [pltpu.SemaphoreType.DMA((4, levels))] * 2 + [pltpu.SemaphoreType.DMA((4,))],
+        compiler_params=pltpu.CompilerParams(collective_id=2, has_side_effects=True, vmem_limit_bytes=40 * 2**20),
+        name="spread",
+    )(*grads, *moments_in, *weights)
 
 def pool_kernel(nothing, tables, bag, pos_ref, lines_ref, pooled_ref):
     samples = pos_ref.shape[1]
@@ -357,21 +609,21 @@
 
 def dense_kernel(
     sizes, stat_ref, fields_ref, pooled_ref, experts_ref, gates_ref, towers_ref, small_ref,
-    grad_a_ref, grad_b_ref, rows_ref, side,
+    grad_a_ref, grad_b_ref, tail_ref, rows_ref, side,
 ):
     experts, hidden, tasks, tower, half_tail = sizes
     samples = fields_ref.shape[1]
     features = pooled_ref.shape[0] // samples * LANES
     halves = (grad_a_ref, grad_b_ref)
-    for ref in halves:
-        ref[features:, :] = jnp.zeros((half_tail, hidden), F32)
+    tail_ref[...] = jnp.zeros_like(tail_ref)
 
     def put_tail(row, value):
         count = value.shape[0]
-        for low, high, ref in ((0, half_tail, grad_a_ref), (half_tail, 2 * half_tail, grad_b_ref)):
-            first, last = max(low, row), min(high, row + count)
+        for part in range(2):
+            first, last = max(part * half_tail, row), min((part + 1) * half_tail, row + count)
             if first < last:
-                ref[features + first - low : features + last - low, :] = value[first - row : last - row]
+                at = slice(first - part * half_tail, last - part * half_tail)
+                tail_ref[part, at, :] = value[first - row : last - row]
 
     start = experts * hidden
     tower_at = start
@@ -440,7 +692,7 @@
     dgates_w = dot3(dgl_t2, x2)
     tail_at = tasks * tower
     put_tail(tail_at, dgates_w[:, :hidden])
-    put_tail(tail_at + 16, dgates_w[:, hidden:])
+    put_tail(tail_at + GAP, dgates_w[:, hidden:])
     x_t2 = split2(x.T)
     dx = dot3(split2(dgl[:, :count]), gate_w2)
     expert_bias_grads = []
@@ -448,12 +700,12 @@
         dpre = dhids[e] * (sigs[e] * (1.0 + pres[e] * (1.0 - sigs[e])))
         expert_bias_grads.append(jnp.sum(dpre, axis=0, keepdims=True))
         dpre2 = split2(dpre)
-        halves[e][0:features, :] = dot3(x_t2, dpre2)
+        halves[e][...] = dot3(x_t2, dpre2)
         dx = dx + dot3(dpre2, split2(experts_ref[e]), NT)
     for q in range(features // LANES):
         rows_ref[q * samples : (q + 1) * samples, :] = dx[:, q * LANES : (q + 1) * LANES]
     rows_ref[features // LANES * samples :, :] = jnp.zeros((8, LANES), F32)
-    small_at = tail_at + 32
+    small_at = tail_at + 2 * GAP
     pad = jnp.zeros((1, 2 * hidden - 2 * tasks * tower - tasks), F32)
     line = jnp.concatenate(tower_bias_grads + out_weight_grads + task_bias_grads + [pad], axis=1)
     loss_row = jnp.where(iota((1, hidden), 1) == 0, jnp.sum(loss, axis=0, keepdims=True), 0.0)
@@ -469,12 +721,13 @@
     tasks, _, tower = towers_w.shape
     samples = fields.shape[1]
     vmem = pl.BlockSpec(memory_space=pltpu.VMEM)
-    grads = jax.ShapeDtypeStruct((features + half_tail, hidden), F32)
+    grads = jax.ShapeDtypeStruct((features, hidden), F32)
+    tail = jax.ShapeDtypeStruct((2, half_tail, hidden), F32)
     return pl.pallas_call(
         functools.partial(dense_kernel, (experts, hidden, tasks, tower, half_tail)),
-        out_shape=(grads, grads, jax.ShapeDtypeStruct((features // LANES * samples + 8, LANES), F32)),
+        out_shape=(grads, grads, tail, jax.ShapeDtypeStruct((features // LANES * samples + 8, LANES), F32)),
         in_specs=[pl.BlockSpec(memory_space=pltpu.SMEM)] + [vmem] * 6,
-        out_specs=(vmem,) * 3,
+        out_specs=(vmem,) * 4,
         scratch_shapes=[pltpu.VMEM((samples, samples), F32)],
         compiler_params=pltpu.CompilerParams(vmem_limit_bytes=56 * 2**20),
         name="dense",
@@ -574,91 +827,35 @@
     )(lists, most, lines.reshape((n + 1) * cap, LANES), table.T, table_m.T, table_v.reshape(1, rows_dev), extra)
     return table_new.T, first_new.T, second_new.reshape(rows_dev)
 
-def orders(n):
-    bits = [1 << i for i in range(n.bit_length() - 1)]
-    first, rest = bits[0], bits[1:]
-    return ([first] + rest, [first] + [rest[1], rest[0]] + rest[2:])
-
-
-def swap(x, n, bit):
-    return lax.ppermute(x, "dev", [(i, i ^ bit) for i in range(n)])
-
-
-def halve(x, me, n, bit):
-    half = x.shape[-2] // 2
-    mine = (me // bit) % 2
-    keep = lax.dynamic_slice_in_dim(x, mine * half, half, x.ndim - 2)
-    send = lax.dynamic_slice_in_dim(x, (1 - mine) * half, half, x.ndim - 2)
-    return keep + swap(send, n, bit)
-
-
-def double(x, me, n, bit):
-    other = swap(x, n, bit)
-    mine = (me // bit) % 2
-    axis = x.ndim - 2
-    return jnp.where(mine == 0, jnp.concatenate([x, other], axis), jnp.concatenate([other, x], axis))
-
-
-def scatter_sum(x, me, n, order):
-    for bit in order:
-        x = halve(x, me, n, bit)
-    return x
-
-
-def gather_all(x, me, n, order):
-    for bit in order[::-1]:
-        x = double(x, me, n, bit)
-    return x
-
-
-def slice_of(x, me, order):
-    rows = x.shape[-2]
-    start = 0
-    for bit in order:
-        rows = rows // 2
-        start = start + ((me // bit) % 2) * rows
-    return lax.dynamic_slice_in_dim(x, start, rows, x.ndim - 2)
-
-
 GAP = 16
 
 
-def pack(experts, gates, towers, small, half_tail):
-    hidden = experts.shape[2]
+def pack_tail(gates, towers, small, half_tail):
     tasks, features, count = gates.shape
+    hidden = towers.shape[1]
     gates = gates.transpose(0, 2, 1).reshape(tasks * count, features)
     lines = jnp.pad(small, (0, 4 * hidden - small.shape[0])).reshape(4, hidden)
+    gap = ((0, GAP - tasks * count), (0, 0))
     tail = jnp.concatenate(
         [
             towers.transpose(0, 2, 1).reshape(-1, hidden),
-            jnp.pad(gates[:, :hidden], ((0, GAP - tasks * count), (0, 0))),
-            jnp.pad(gates[:, hidden:], ((0, GAP - tasks * count), (0, 0))),
+            jnp.pad(gates[:, :hidden], gap),
+            jnp.pad(gates[:, hidden:], gap),
             lines,
         ]
     )
-    tail = jnp.pad(tail, ((0, 2 * half_tail - tail.shape[0]), (0, 0)))
-    return (
-        jnp.concatenate([experts[0], tail[:half_tail]]),
-        jnp.concatenate([experts[1], tail[half_tail:]]),
-    )
-
-
-def unpack(a, b, shapes):
-    experts_shape, gates_shape, towers_shape, small_size = shapes
-    features = experts_shape[1]
-    hidden = experts_shape[2]
-    tasks, _, count = gates_shape
-    experts = jnp.stack([a[:features], b[:features]])
-    tail = jnp.concatenate([a[features:], b[features:]])
-    tower_rows = tasks * towers_shape[2]
-    towers = tail[:tower_rows].reshape(tasks, towers_shape[2], hidden).transpose(0, 2, 1)
-    gates = jnp.concatenate(
-        [tail[tower_rows : tower_rows + tasks * count], tail[tower_rows + GAP : tower_rows + GAP + tasks * count]], axis=1
-    )
+    return jnp.pad(tail, ((0, 2 * half_tail - tail.shape[0]), (0, 0))).reshape(2, half_tail, hidden)
+
+
+def unpack_tail(tail, gates_shape, towers_shape, small_size):
+    tasks, features, count = gates_shape
+    _, hidden, tower = towers_shape
+    at = tasks * tower
+    towers = tail[:at].reshape(tasks, tower, hidden).transpose(0, 2, 1)
+    gates = jnp.concatenate([tail[at : at + tasks * count], tail[at + GAP : at + GAP + tasks * count]], axis=1)
     gates = gates.reshape(tasks, count, features).transpose(0, 2, 1)
-    at = tower_rows + 2 * GAP
-    small = tail[at : at + 4].reshape(-1)[:small_size]
-    return experts, gates, towers, small, tail[at + 8, 0]
+    at = at + 2 * GAP
+    return gates, towers, tail[at : at + 4].reshape(-1)[:small_size], tail[at + 8, 0]
 
 
 def moments(first, second, grad):
@@ -717,6 +914,15 @@
         return extra + jnp.zeros((rows_dev, width), F32).at[asked.reshape(-1)].add(got * valid).T
 
     return lax.fori_loop(1, (most + cap - 1) // cap, body, jnp.zeros((width, rows_dev), F32))
+
+
+def blank(shape):
+    return pl.pallas_call(
+        lambda out_ref: None,
+        out_shape=jax.ShapeDtypeStruct(shape, F32),
+        out_specs=pl.BlockSpec(memory_space=pl.ANY),
+        name="blank",
+    )()
 
 
 def per_device(
@@ -732,57 +938,61 @@
     cap = max(8, (samples * tables * bag // n * 5 // 16 + 7) // 8 * 8)
     experts, features, hidden = experts_w.shape
     tasks = towers_w.shape[0]
-    half_tail = 256
-    order_a, order_b = orders(n)
-
-    owned = mat_home == me
-    own_experts = owned[:experts, None, None]
-    own_gates = owned[experts : experts + tasks, None, None]
-    own_towers = owned[experts + tasks : experts + 2 * tasks, None, None]
-    own_small = owned[experts + 2 * tasks]
-    firsts = (experts_m[0], gates_m[0], towers_m[0], small_m[0])
-    seconds = (experts_v[0], gates_v[0], towers_v[0], small_v[0])
-    owns = (own_experts, own_gates, own_towers, own_small)
-
-    def kept(items):
-        return tuple(jnp.where(own, item, 0.0) for own, item in zip(owns, items))
-
-    first_a, first_b = pack(*kept(firsts), half_tail)
-    second_a, second_b = pack(*kept(seconds), half_tail)
-    moments_a = scatter_sum(jnp.stack([first_a, second_a]), me, n, order_a)
-    moments_b = scatter_sum(jnp.stack([first_b, second_b]), me, n, order_b)
-
-    fields, pos, owner, rank, local, mine, theirs, stat = route(
-        n, cap, row_ids, lengths, counts, mask, labels, row_home, rows_dev
+    used_rows = tasks * towers_w.shape[2] + 2 * GAP + 16
+    half_tail = -(-used_rows // 2 // (8 * n)) * 8 * n
+
+    tail_m = pack_tail(gates_m[0], towers_m[0], small_m[0], half_tail)
+    tail_v = pack_tail(gates_v[0], towers_v[0], small_v[0], half_tail)
+    fields, pos, owner, rank, local, mine, theirs, stat, lines, *moment_slices = forward(
+        n, cap, row_ids, lengths, counts, mask, labels, row_home, table, mat_home,
+        experts_m[0], experts_v[0], tail_m, tail_v,
     )
     most, weight_count = stat[4, 0], stat[5, 0]
-    lines = rows_exchange(n, cap, theirs, table.T, True, 1, "fetch_rows")
+    more = most > cap
     pooled = pool(n, cap, tables, bag, pos, lines)
-    pooled = late_pool(n, cap, most, owner, rank, local, table, pooled)
-    grad_a, grad_b, rows_grad = dense(
+    pooled = lax.cond(
+        more, lambda *args: late_pool(n, cap, *args), lambda *args: args[-1], most, owner, rank, local, table, pooled
+    )
+    grad_a, grad_b, grad_tail, rows_grad = dense(
         half_tail, weight_count[None], fields, pooled, experts_w, gates_w, towers_w, small_params
     )
-    back = rows_exchange(n, cap, mine, rows_grad, False, 2, "return_grads")
-    extra = late_grads(n, cap, most, owner, rank, local, rows_grad, rows_dev, width)
+    back, *grad_slices = backward(n, cap, mine, rows_grad, grad_a, grad_b, grad_tail)
+    extra = lax.cond(
+        more,
+        lambda *args: late_grads(n, cap, *args, rows_dev, width),
+        lambda *args: blank((width, rows_dev)),
+        most, owner, rank, local, rows_grad,
+    )
     table_new, table_m_new, table_v_new = update(
         n, cap, per_table, tables, theirs, most[None], back, table, table_m, table_v, extra
     )
-
-    weights = pack(experts_w, gates_w, towers_w, small_params, half_tail)
-    both = []
-    for grad, moment, weight, order in (
-        (grad_a, moments_a, weights[0], order_a), (grad_b, moments_b, weights[1], order_b)
+    tail_w = pack_tail(gates_w, towers_w, small_params, half_tail)
+    orders = axis_orders(n)
+    weights = []
+    for source, order in zip((experts_w[0], experts_w[1], tail_w[0], tail_w[1]), orders):
+        rows = source.shape[0]
+        weights.append(lax.dynamic_slice_in_dim(source, start_of(me, order, rows), rows // n, 0))
+    wholes = spread(n, grad_slices, moment_slices, weights)
+    experts_new = jnp.stack([wholes[0][0], wholes[1][0]])
+    grad_experts = jnp.stack([wholes[0][1], wholes[1][1]])
+    tails = jnp.concatenate([wholes[2], wholes[3]], axis=1)
+    gates_new, towers_new, small_new, _ = unpack_tail(tails[0], gates_w.shape, towers_w.shape, small_params.shape[0])
+    grad_gates, grad_towers, grad_small, loss_sum = unpack_tail(
+        tails[1], gates_w.shape, towers_w.shape, small_params.shape[0]
+    )
+    owned = mat_home == me
+    owns = (
+        owned[:experts, None, None],
+        owned[experts : experts + tasks, None, None],
+        owned[experts + tasks : experts + 2 * tasks, None, None],
+        owned[experts + 2 * tasks],
+    )
+    outs_m, outs_v = [], []
+    for own, first, second, grad in zip(
+        owns, (experts_m, gates_m, towers_m, small_m), (experts_v, gates_v, towers_v, small_v),
+        (grad_experts, grad_gates, grad_towers, grad_small),
     ):
-        grad = scatter_sum(grad, me, n, order)
-        first, second = moments(moment[0], moment[1], grad)
-        new = stepped(slice_of(weight, me, order), first, second)
-        both.append(gather_all(jnp.stack([new, grad]), me, n, order))
-    shapes = (experts_w.shape, gates_w.shape, towers_w.shape, small_params.shape[0])
-    experts_new, gates_new, towers_new, small_new, _ = unpack(both[0][0], both[1][0], shapes)
-    *grads, loss_sum = unpack(both[0][1], both[1][1], shapes)
-    outs_m, outs_v = [], []
-    for own, first, second, grad in zip(owns, firsts, seconds, grads):
-        first, second = moments(first, second, grad)
+        first, second = moments(first[0], second[0], grad)
         outs_m.append(jnp.where(own, first, 0.0)[None])
         outs_v.append(jnp.where(own, second, 0.0)[None])
     return (

time: 433 us -> 331 us (0.76)
  Pallas kernels: 159 us -> 274 us
  waiting for transfers between devices: 109 us -> 0 us
  other arithmetic: 59.7 us -> 16.5 us
  starting transfers between devices: 25.6 us -> 0 us
  local copies, waits for them, and re-layouts: 56.5 us -> 35 us
  loops' own time: 14 us -> 0.64 us
    pallas_call x3 -> x4, Pallas kernels: 115 us -> 230 us  [the longest x1 103 us: forward(): pl.pallas_call(functools.partial(forward_kernel, sizes), out_shape=(jax.S...]
    ppermute x30 -> x0, waiting for transfers between devices: 109 us -> none  [swap(): return lax.ppermute(x, 'dev', [(i, i ^ bit) for i in range(n)])]
    select_n x12 -> x0, other arithmetic: 26.4 us -> none  [the longest x10 22.9 us: double(): jnp.where(mine == 0, jnp.concatenate([x, other], axis), jnp.concatenate([...]
    ppermute x30 -> x0, starting transfers between devices: 25.6 us -> none  [swap(): return lax.ppermute(x, 'dev', [(i, i ^ bit) for i in range(n)])]
    while x5 -> x0, local copies, waits for them, and re-layouts: 15.2 us -> none  [the longest x3 8.15 us: late_pool(): return lax.fori_loop(1, (most + cap - 1) // cap, body, pooled)]
    another operation x2, loops' own time: 14 us -> 0.64 us  [the longest x1 0.36 us: per_device(): lax.cond(more, lambda *args: late_pool(n, cap, *args), lambda *args: args...]
    add x18 -> x0, other arithmetic: 10 us -> none  [halve(): return keep + swap(send, n, bit)]
    another operation x12 -> x2, other arithmetic: 9.5 us -> 4.13 us  [per_device(): experts_new = jnp.stack([wholes[0][0], wholes[1][0]])]
  transfers between devices with their start and end apart: 30 -> 0, of which waited for: 17 -> 0; matrix products, arithmetic and copies ran while one was open for 14% -> 0% of each run, Pallas kernels for 14% -> 0%
where the time goes in v2:
time: 331 us; the launch traced here: 330 us
  Pallas kernels  274 us (83%)
  local copies, waits for them, and re-layouts  35 us (11%)
  other arithmetic  16.5 us (5%)
  between operations  4.47 us (1%)
    pallas_call x1, Pallas kernels, forward(): pl.pallas_call(functools.partial(forward_kernel, sizes), out_shape=(jax.S...  103 us
    pallas_call x1, Pallas kernels, spread(): pl.pallas_call(functools.partial(spread_kernel, n), out_shape=tuple((jax....  71 us
    pallas_call x1, Pallas kernels, backward(): pl.pallas_call(functools.partial(backward_kernel, n, cap), out_shape=(jax...  56.3 us
    pallas_call x1, Pallas kernels, update(): pl.pallas_call(functools.partial(update_kernel, (n, cap, per_table)), gri...  21.3 us
    unnamed x78, local copies, waits for them, and re-layouts  18 us
    pallas_call x1, Pallas kernels, dense(): pl.pallas_call(functools.partial(dense_kernel, (experts, hidden, tasks, t...  14 us
    pallas_call x1, Pallas kernels, pool(): pl.pallas_call(functools.partial(pool_kernel, n * cap, tables, bag), out_...  8.26 us

profile of v2, /device:TPU:0, one launch (start us, length us, event | category | flops | bytes accessed | tf_op | source)
XLA Modules:
  0.0 330.1 jit_solution(13326191879587252381)
XLA Ops:
  3.3 1.3 reshape.803.small_ref
  6.9 0.8 reshape.802.gates_ref
  7.7 0.8 reshape.798
  8.5 0.8 reshape.794
  9.4 1.1 slice.174
  10.5 1.1 fusion.26
  11.8 1.1 pad.42
  13.0 1.1 pad.46
  14.6 102.7 %forward.1 = (f32[8,128]{1,0:T(8,128)}, s32[64,128]{1,0:T(8,128)}, s32[64,128]{1,0:T(8,128)S(1)}, s32[64,128]{1,0:T(8,128)S(1)}, s32[64,128]{1,0:T(8,128)S(1)}, ...) custom-call(s32[64,128]{1,0:T(8,128)} %bitcast.297, ...), custom_call_target="tpu_custom_call" | custom-call | tf_op jit(solution)/shard_map/forward/pallas_call | solution.py:409
  117.3 1.3 fusion.52
  119.9 1.3 copy-done.7
  121.2 0.8 copy-done.16
  121.9 8.3 %pool.1 = f32[1024,128]{1,0:T(8,128)S(1)} custom-call(s32[64,128]{1,0:T(8,128)S(1)} %copy-done.16, f32[2640,128]{1,0:T(8,128)S(1)} %bitcast.269), custom_call_target="tpu_custom_call" | custom-call | tf_op jit(solution)/shard_map/pool/pallas_call | solution.py:587
  130.6 2.9 fusion.46
  133.5 14.0 %dense.1 = (f32[1024,512]{1,0:T(8,128)}, f32[1024,512]{1,0:T(8,128)}, f32[2,256,512]{2,1,0:T(8,128)}, f32[1032,128]{1,0:T(8,128)S(1)}) custom-call(s32[1]{0:T(128)} %bitcast.44.stat_ref, f32[8,128]{1,0:T(8,128)} %get-tuple-element.282.fields_ref, f32[1024,128]{1,0:T(8,128)} %copy-done.22, f32[2,1024,512]{2,1,0:T(8,128)} %experts_ref.1, ...), custom_call_target="tpu_custom_call" | custom-call | tf_op jit(solution)/shard_map/dense/pallas_call | solution.py:726
  147.5 1.6 copy-done.5
  149.1 1.6 copy-done.6
  150.7 1.2 copy-done.8
  151.9 56.3 %backward.1 = (f32[33,80,128]{2,1,0:T(8,128)S(1)}, f32[32,512]{1,0:T(8,128)S(1)}, f32[32,512]{1,0:T(8,128)S(1)}, f32[8,512]{1,0:T(8,128)S(1)}, f32[8,512]{1,0:T(8,128)S(1)}) custom-call(s32[32,2,128]{2,1,0:T(2,128)S(1)} %copy-done.13, f32[1032,128]{1,0:T(8,128)S(1)} %get-tuple-element.288.rows_ref, f32[1024,512]{1,0:T(8,128)S(1)} %copy-done.5, ...), custom_call_target="tpu_custom_call" | custom-call | tf_op jit(solution)/shard_map/backward/pallas_call | solution.py:480
  209.1 2.2 copy-done.4
  211.3 21.3 %update_rows.1 = (f32[64,16384]{1,0:T(8,128)}, f32[64,16384]{1,0:T(8,128)}, f32[1,16384]{1,0:T(1,128)}) custom-call(s32[32,2,128]{2,1,0:T(2,128)S(1)} %copy-done.12, s32[1]{0:T(128)} %bitcast.56.more_ref, f32[2640,128]{1,0:T(8,128)S(1)} %bitcast.268, f32[64,16384]{1,0:T(8,128)} %bitcast.277, f32[64,16384]{1,0:T(8,128)S(1)} %bitcast.267, ...), custom_call_target="tpu_custom_call" | custom-call | tf_op jit(solution)/shard_map/update_rows/pallas_call | solution.py:809
  232.7 71.0 %spread.1 = (f32[2,1024,512]{2,1,0:T(8,128)S(1)}, f32[2,1024,512]{2,1,0:T(8,128)S(1)}, f32[2,256,512]{2,1,0:T(8,128)S(1)}, f32[2,256,512]{2,1,0:T(8,128)S(1)}) custom-call(f32[32,512]{1,0:T(8,128)S(1)} %get-tuple-element.292.refs_0_, f32[32,512]{1,0:T(8,128)S(1)} %get-tuple-element.293.refs_1_, f32[8,512]{1,0:T(8,128)S(1)} %get-tuple-element.294.refs_2_, ...), custom_call_target="tpu_custom_call" | custom-call | tf_op jit(solution)/shard_map/spread/pallas_call | solution.py:553
  303.7 2.0 copy-done
  305.7 2.0 copy-done.2
  313.2 0.8 convert_bitcast_fusion.2
  314.0 1.4 fusion.33
  316.0 1.7 copy-done.1
  317.8 1.5 pad_maximum_fusion.2
  319.8 2.6 pad_maximum_fusion
  322.4 1.1 copy-done.20
  323.5 1.3 copy-done.21
  324.8 4.2 %fusion.25 = (f32[1,2,1024,512]{3,2,1,0:T(8,128)}, f32[1,2,1024,512]{3,2,1,0:T(8,128)}) fusion(f32[1,2,1024,512]{3,2,1,0:T(8,128)S(1)} %copy-done.21, f32[1,1,1024,512]{3,2,1,0:T(8,128)S(1)} %get-tuple-element.389, f32[1,1,1024,512]{3,2,1,0:T(8,128)S(1)} %get-tuple-element.387, pred[2]{0:T(512)(128)(4,1)S(1)} %bitcast.301, f32[1,2,1024,512]{3,2,1,0:T(8,128)S(1)} %copy-done.20), kind=kLoop, calls=%fused_computation.82 | loop fusion | flops 10485760 | bytes 20971522 | tf_op jit(solution)/shard_map/jit(_where)/select_n | solution.py:997
  (109 shorter events, 12.6 us)
Async XLA Ops:
  0.7 12.2 %copy-start.26 = (f32[1,5,512,64]{2,3,1,0:T(8,128)S(1)}, f32[1,5,512,64]{2,3,1,0:T(8,128)}, u32[]{:S(2)}) copy-start(f32[1,5,512,64]{2,3,1,0:T(8,128)} %param.49) | copy-start | bytes 1966084
  0.7 11.0 %copy-start.24 = (f32[1,5,512,64]{2,3,1,0:T(8,128)S(1)}, f32[1,5,512,64]{2,3,1,0:T(8,128)}, u32[]{:S(2)}) copy-start(f32[1,5,512,64]{2,3,1,0:T(8,128)} %param.48) | copy-start | bytes 1966084
  5.4 4.0 %copy-start.31 = (f32[1669]{0:T(1024)}, f32[1669]{0:T(1024)S(1)}, u32[]{:S(2)}) copy-start(f32[1669]{0:T(1024)S(1)} %reduce.13) | copy-start | bytes 20032
  6.1 3.3 copy-start.33
  7.7 5.3 %copy-start.28 = (f32[10,1024]{1,0:T(8,128)}, f32[10,1024]{1,0:T(8,128)S(1)}, u32[]{:S(2)}) copy-start(f32[10,1024]{1,0:T(8,128)S(1)} %reshape.802.gates_ref) | copy-start | bytes 122884
  11.6 2.9 copy-start.17
  119.8 1.3 copy-start.7
  130.6 2.9 copy-start.22
  133.4 14.1 %copy-start.13 = (s32[32,2,128]{2,1,0:T(2,128)S(1)}, s32[32,2,128]{2,1,0:T(2,128)}, u32[]{:S(2)}) copy-start(s32[32,2,128]{2,1,0:T(2,128)} %get-tuple-element.280.lists_ref) | copy-start | bytes 98308
  147.5 1.6 copy-start.5
  149.1 1.6 copy-start.6
  209.1 2.2 copy-start.4
  211.3 21.4 %copy-start.9 = (f32[2,32,512]{2,1,0:T(8,128)S(1)}, f32[2,32,512]{2,1,0:T(8,128)}, u32[]{:S(2)}) copy-start(f32[2,32,512]{2,1,0:T(8,128)} %get-tuple-element.296.refs_4_) | copy-start | bytes 393220
  211.3 21.4 %copy-start.10 = (f32[2,32,512]{2,1,0:T(8,128)S(1)}, f32[2,32,512]{2,1,0:T(8,128)}, u32[]{:S(2)}) copy-start(f32[2,32,512]{2,1,0:T(8,128)} %get-tuple-element.297.refs_5_) | copy-start | bytes 393220
  211.3 21.4 %copy-start.14 = (f32[2,8,512]{2,1,0:T(8,128)S(1)}, f32[2,8,512]{2,1,0:T(8,128)}, u32[]{:S(2)}) copy-start(f32[2,8,512]{2,1,0:T(8,128)} %get-tuple-element.298.refs_6_) | copy-start | bytes 98308
  211.3 21.4 %copy-start.15 = (f32[2,8,512]{2,1,0:T(8,128)S(1)}, f32[2,8,512]{2,1,0:T(8,128)}, u32[]{:S(2)}) copy-start(f32[2,8,512]{2,1,0:T(8,128)} %get-tuple-element.299.refs_7_) | copy-start | bytes 98308
  211.3 96.4 %copy-start.32 = (f32[1669]{0:T(1024)S(1)}, f32[1669]{0:T(1024)}, u32[]{:S(2)}) copy-start(f32[1669]{0:T(1024)} %copy-done.31) | copy-start | bytes 20032
  211.3 96.4 %copy-start.34 = (f32[1669]{0:T(1024)S(1)}, f32[1669]{0:T(1024)}, u32[]{:S(2)}) copy-start(f32[1669]{0:T(1024)} %copy-done.33) | copy-start | bytes 20032
  211.3 100.2 %copy-start.29 = (f32[1,5,1024,2]{2,3,1,0:T(2,128)S(1)}, f32[1,5,1024,2]{2,3,1,0:T(2,128)}, u32[]{:S(2)}) copy-start(f32[1,5,1024,2]{2,3,1,0:T(2,128)} %param.46) | copy-start | bytes 122884
  211.3 100.2 %copy-start.30 = (f32[1,5,1024,2]{2,3,1,0:T(2,128)S(1)}, f32[1,5,1024,2]{2,3,1,0:T(2,128)}, u32[]{:S(2)}) copy-start(f32[1,5,1024,2]{2,3,1,0:T(2,128)} %param.47) | copy-start | bytes 122884
  211.3 100.2 %copy-start.41 = (pred[5]{0:T(512)(128)(4,1)S(1)}, pred[5]{0:T(512)(128)(4,1)}, u32[]{:S(2)}) copy-start(pred[5]{0:T(512)(128)(4,1)} %get-tuple-element.416) | copy-start | bytes 19
  303.7 2.0 copy-start
  305.7 2.0 copy-start.2
  312.3 1.6 copy-start.25
  312.4 1.6 copy-start.27
  312.4 1.6 copy-start.42
  312.5 2.9 copy-start.3
  313.2 2.8 copy-start.23
  315.5 2.2 copy-start.1
  319.3 3.1 copy-start.40
  319.8 3.7 %copy-start.20 = (f32[1,2,1024,512]{3,2,1,0:T(8,128)S(1)}, f32[1,2,1024,512]{3,2,1,0:T(8,128)}, u32[]{:S(2)}) copy-start(f32[1,2,1024,512]{3,2,1,0:T(8,128)} %param.44) | copy-start | bytes 12582916
  319.8 5.0 %copy-start.21 = (f32[1,2,1024,512]{3,2,1,0:T(8,128)S(1)}, f32[1,2,1024,512]{3,2,1,0:T(8,128)}, u32[]{:S(2)}) copy-start(f32[1,2,1024,512]{3,2,1,0:T(8,128)} %param.45) | copy-start | bytes 12582916
  (5 other events, 4.8 us)

commit v3 on v0

--- a/solution.py
+++ b/solution.py
@@ -1,23 +1,998 @@
+import functools
 import jax
 import jax.numpy as jnp
 from jax import lax
+from jax.experimental import pallas as pl
+from jax.experimental.pallas import tpu as pltpu
 from jax.sharding import PartitionSpec as P
 
+MESH = pl.DeviceIdType.MESH
+F32, BF16, I32 = jnp.float32, jnp.bfloat16, jnp.int32
+NN, NT, TN = (((1,), (0,)), ((), ())), (((1,), (1,)), ((), ())), (((0,), (0,)), ((), ()))
+LANES = 128
+
+
+def iota(shape, dim):
+    return lax.broadcasted_iota(I32, shape, dim)
+
+
+def dot(a, b, dims=NN):
+    return lax.dot_general(a, b, dims, preferred_element_type=F32)
+
+
+def split3(x):
+    high = x.astype(BF16)
+    rest = x - high.astype(F32)
+    middle = rest.astype(BF16)
+    low = (rest - middle.astype(F32)).astype(BF16)
+    return high, middle, low
+
+
+def greet_all(n, me):
+    barrier = pltpu.get_barrier_semaphore()
+
+    def signal(k, carry):
+        pl.semaphore_signal(barrier, inc=1, device_id=(me ^ k,), device_id_type=MESH)
+        return carry
+
+    lax.fori_loop(1, n, signal, 0)
+    pl.semaphore_wait(barrier, n - 1)
+
+
+def exchange(n, me, source, target, sends, receives, k):
+    peer = me ^ k
+    return pltpu.make_async_remote_copy(
+        src_ref=source.at[peer],
+        dst_ref=target.at[me],
+        send_sem=sends.at[k],
+        recv_sem=receives.at[k],
+        device_id=(peer,),
+        device_id_type=MESH,
+    )
+
+
+def for_range(low, high, body):
+    def step(k, carry):
+        body(k)
+        return carry
+
+    lax.fori_loop(low, high, step, 0)
+
 STEP = 5
-
-
-HIGHEST = lax.Precision.HIGHEST
 BETA_ONE = 0.9
 BETA_TWO = 0.999
 EPSILON = 1e-08
 DECAY = 0.01
 RATE_DENSE = 0.02
 RATE_ROWS = 0.3
+GAP = 16
+
+def axis_orders(n):
+    bits = [1 << i for i in range(n.bit_length() - 1)]
+    core, rest = bits[:1], bits[1:]
+    a = len(rest) // 3
+    b = (len(rest) - a) // 2
+    x, y, z = rest[:a], rest[a : a + b], rest[a + b :]
+    return core + x + y + z, core + y + x + z, core + z + x + y, core + z + y + x
+
+
+def early_levels(n):
+    rest = n.bit_length() - 2
+    a = rest // 3
+    return 1 + a + (rest - a) // 2
+
+
+def bit_of(me, bit):
+    return lax.rem(lax.div(me, bit), 2)
+
+
+def start_of(me, order, rows):
+    start = 0
+    for bit in order:
+        rows = rows // 2
+        start = start + bit_of(me, bit) * rows
+    return start
+
+
+def rows_at(start, count):
+    return pl.ds(pl.multiple_of(start, 8), count)
+
+
+def plan(n, experts, features, tail_rows):
+    unit = 8 * n
+    along_x, along_y, along_z, along_w = axis_orders(n)
+    chains = []
+    for k in range(features // unit):
+        for e in range(experts):
+            chains.append((e, k * unit, along_y if e % 2 else along_x, k))
+    for k in range(tail_rows // unit):
+        chains.append((experts, k * unit, along_w if k % 2 else along_z, k // 2))
+    return chains
+
+
+def halving(me, source, stages, sends, receives, c, order, i, lane=0):
+    bit = order[i]
+    before = source if i == 0 else stages[i - 1].at[c]
+    target = stages[i].at[c]
+    half = stages[i].shape[-2]
+    at = rows_at((1 - bit_of(me, bit)) * half, half)
+    if i == 0 and len(stages[0].shape) == 4:
+        target = target.at[lane]
+        lane_sem = lane * len(order)
+    else:
+        lane_sem = i
+    return pltpu.make_async_remote_copy(
+        src_ref=before.at[at] if len(before.shape) == 2 else before.at[:, at],
+        dst_ref=target,
+        send_sem=sends.at[c, lane_sem],
+        recv_sem=receives.at[c, lane_sem],
+        device_id=(me ^ bit,),
+        device_id_type=MESH,
+    )
+
+
+def fill_tail(tail, towers, gates, small):
+    tasks, tower, hidden = towers.shape
+    count = gates.shape[1]
+    size = small.shape[1]
+    tail[...] = jnp.zeros_like(tail)
+    tail[0 : tasks * tower, :] = towers[...].reshape(tasks * tower, hidden)
+    for part in range(2):
+        for k in range(tasks):
+            at = tasks * tower + part * GAP + k * count
+            tail[at : at + count, :] = gates[k][:, part * hidden : (part + 1) * hidden]
+    at = tasks * tower + 2 * GAP
+    for i in range(-(-size // hidden)):
+        last = min(size, (i + 1) * hidden)
+        tail[at + i : at + i + 1, 0 : last - i * hidden] = small[0:1, i * hidden : last]
+
+
+def owner_side(me, n, items_ref, experts, tasks, tower):
+    def chosen(chain, i, count):
+        array, first, order, _ = chain
+        bit = order[i]
+        if array < experts:
+            return bit_of(items_ref[array], bit) == bit_of(me, bit)
+        towers = tasks * tower
+        row = first + start_of(me, order[: i + 1], 8 * n) + iota((count, LANES), 0)
+        item = lax.div(row, tower) + experts + tasks
+        for part in range(2):
+            at = towers + part * GAP
+            item = jnp.where((row >= at) & (row < at + tasks * experts), experts + lax.div(row - at, experts), item)
+        item = jnp.where(row >= towers + 2 * GAP, experts + 2 * tasks, item)
+        home = jnp.zeros((count, LANES), I32)
+        for k in range(experts, experts + 2 * tasks + 1):
+            home = jnp.where(item == k, items_ref[k], home)
+        return (bit_of(home, bit) == bit_of(me, bit))[:, :1]
+
+    return chosen
+
+
+def forward_kernel(
+    sizes,
+    ids_ref, lengths_ref, counts_ref, mask_ref, labels_ref, homes_ref, table_ref, items_ref,
+    experts_m_ref, experts_v_ref, towers_m_ref, towers_v_ref, gates_m_ref, gates_v_ref, small_m_ref, small_v_ref,
+    fields_ref, pos_ref, mine_ref, theirs_ref, pairs_ref, stat_ref, lines_ref, moments_ref,
+    outbox, inbox, message, replies, lists, field_scratch, owner_ref, rank_ref, local_ref, asked_smem, rows_ref, rows_out,
+    tails, kept_ref, *rest,
+):
+    n, cap, tables, bag, tasks, experts, per_table, block_rows, rows_dev = sizes
+    levels = early_levels(n)
+    stages = list(rest[: levels - 1]) + [moments_ref]
+    send_a, recv_a, send_b, recv_b, send_c, recv_c, send_m, recv_m, keep_sem, sems = rest[levels - 1 :]
+    chains = plan(n, experts, experts_m_ref.shape[1], tails.shape[1])
+    unit = 8 * n
+    rows = tables * bag
+    me = lax.axis_index("dev")
+    shift = lax.rem(me * 13, n)
+    per_pair = LANES // n
+    table_of = lax.div(iota((rows, LANES), 0), bag)
+    slot_of = lax.rem(iota((rows, LANES), 0), bag)
+    expand = jnp.where(lax.div(iota((rows, tables), 0), bag) == iota((rows, tables), 1), 1.0, 0.0).astype(BF16)
+    used = dot(expand, lengths_ref[...].astype(F32).astype(BF16)).astype(I32)
+    present = iota((1, LANES), 1) < counts_ref[0]
+    live = present & (slot_of < used)
+    field_scratch[0:rows, :] = jnp.where(live, ids_ref[...], -1).astype(F32)
+    field_scratch[rows : rows + tasks, :] = labels_ref[...]
+    field_scratch[rows + tasks : rows + tasks + 1, :] = jnp.where(present & (mask_ref[...] == 1), 1.0, 0.0)
+    field_scratch[rows + tasks + 1 :, :] = jnp.zeros((LANES - rows - tasks - 1, LANES), F32)
+    row = iota((n * 8, LANES), 0)
+    peer_of, piece = lax.div(row, 8), lax.rem(row, 8)
+    column = iota((n * 8, LANES), 1)
+    pick = jnp.where((piece < per_pair) & (column == piece * n + lax.rem(peer_of - shift + n, n)), 1.0, 0.0).astype(BF16)
+    high, middle, low = split3(field_scratch[...])
+    spread = dot(pick, high, NT) + dot(pick, middle, NT) + dot(pick, low, NT)
+    outbox[...] = spread.reshape(n, 8, LANES)
+    greet_all(n, me)
+    own_copy = pltpu.make_async_copy(outbox.at[me], inbox.at[me], sems.at[0])
+    own_copy.start()
+    for_range(1, n, lambda k: exchange(n, me, outbox, inbox, send_a, recv_a, k).start())
+    fill_tail(tails.at[0], towers_m_ref, gates_m_ref, small_m_ref)
+    fill_tail(tails.at[1], towers_v_ref, gates_v_ref, small_v_ref)
+
+    def whole(c, w):
+        array, first, _, _ = chains[c]
+        source = tails.at[w] if array == experts else (experts_m_ref, experts_v_ref)[w].at[array]
+        return source.at[first : first + unit]
+
+    def hop(c, i, lane=0):
+        return halving(me, whole(c, lane) if i == 0 else None, stages, send_m, recv_m, c, chains[c][2], i, lane)
+
+    def keep(c, w):
+        at = rows_at(bit_of(me, 1) * (unit // 2), unit // 2)
+        return pltpu.make_async_copy(whole(c, w).at[at], kept_ref.at[c, w], keep_sem.at[c, w])
+
+    for c in range(len(chains)):
+        for w in range(2):
+            hop(c, 0, w).start()
+            keep(c, w).start()
+
+    chosen = owner_side(me, n, items_ref, experts, tasks, towers_m_ref.shape[1])
+
+    def settle(c, i):
+        order = chains[c][2]
+        for w in range(2 if i == 0 else 1):
+            hop(c, i, w).wait()
+            if i == 0:
+                keep(c, w).wait()
+        half = stages[i].shape[2]
+        mine = rows_at(bit_of(me, order[i]) * half, half)
+        flag = chosen(chains[c], i, half)
+        for w in range(2):
+            kept = kept_ref[c, w] if i == 0 else stages[i - 1][c, w, mine, :]
+            stages[i][c, w] = jnp.where(flag, kept, stages[i][c, w])
+        if i + 1 < levels:
+            hop(c, i + 1).start()
+
+    steps = len(set(chain[3] for chain in chains)) + levels - 1
+
+    def settle_step(s):
+        for c, chain in enumerate(chains):
+            if 0 <= s - chain[3] < levels:
+                settle(c, s - chain[3])
+
+    homes = homes_ref[...]
+    blocks = homes.shape[1]
+    homes_rows = (
+        dot(expand, (homes >> 5).astype(F32).astype(BF16)) * 32.0 + dot(expand, (homes & 31).astype(F32).astype(BF16))
+    ).astype(I32)
+    gather_back = jnp.where((piece < per_pair) & (column == peer_of * per_pair + piece), 1.0, 0.0).astype(BF16)
+    before = jnp.where(iota((LANES, LANES), 0) < iota((LANES, LANES), 1), 1.0, 0.0).astype(BF16)
+    ones = jnp.ones((LANES, LANES), BF16)
+    r_out, r_in = iota((rows + 8, rows), 0), iota((rows + 8, rows), 1)
+    parity_in = lax.rem(lax.div(r_in, bag), 2)
+    earlier = (r_out < rows) & (r_in < r_out) & (parity_in == lax.rem(lax.div(r_out, bag), 2))
+    totals = (r_out == rows + 2 + parity_in)
+    above = jnp.where(earlier | totals, 1.0, 0.0).astype(BF16)
+    for_range(1, n, lambda k: exchange(n, me, outbox, inbox, send_a, recv_a, k).wait())
+    own_copy.wait()
+    settle_step(0)
+    arrived = inbox[...].reshape(n * 8, LANES).T
+    high, middle, low = split3(arrived)
+    fields = dot(high, gather_back) + dot(middle, gather_back) + dot(low, gather_back)
+    fields_ref[...] = fields[rows : rows + 8]
+    ids = fields[0:rows].astype(I32)
+    weight_count = jnp.sum(fields[rows + tasks : rows + tasks + 1], axis=1, keepdims=True).astype(I32)
+    live = ids >= 0
+    ids = jnp.maximum(ids, 0)
+    block = lax.div(ids, block_rows)
+    lane = block & (LANES - 1)
+    home = jnp.zeros((rows, LANES), I32)
+    for part in range(blocks // LANES):
+        found = jnp.take_along_axis(homes_rows[:, part * LANES : (part + 1) * LANES], lane, axis=1, mode="promise_in_bounds")
+        home = jnp.where(lax.div(block, LANES) == part, found, home)
+    owner = jnp.where(live, lax.div(home, per_table), n)
+    local = (table_of * per_table + lax.rem(home, per_table)) * block_rows + lax.rem(ids, block_rows)
+    owner_ref[...] = owner
+    local_ref[...] = local
+
+    def rank_step(o, carry):
+        rank, most = carry
+        is_mine = owner == o
+        flags = jnp.where(is_mine, 1.0, 0.0).astype(BF16)
+        row_totals = dot(flags, ones).astype(BF16)
+        bases = dot(above, row_totals)
+        count = bases[rows : rows + 8].astype(I32)
+        message[o] = count
+        rank = jnp.where(is_mine, (dot(flags, before) + bases[0:rows]).astype(I32), rank)
+        return rank, jnp.maximum(most, count)
+
+    rank, most = lax.fori_loop(
+        0, n, rank_step, (jnp.zeros((rows, LANES), I32), jnp.zeros((8, LANES), I32)), unroll=4
+    )
+    rank_ref[...] = rank
+    settle_step(1)
+    most = jnp.max(most, axis=0, keepdims=True)
+    pos_ref[...] = jnp.where(live, jnp.where(rank < cap, owner * cap + rank, n * cap + 1), n * cap)
+    lists[...] = jnp.zeros_like(lists)
+    device_row = iota((n, LANES), 0)
+    rank_row = iota((LANES, LANES), 0)
+    lane_value = (iota((n, LANES), 1)).astype(F32)
+
+    def list_step(q, carry):
+        for parity in range(2):
+            picks, places = [], []
+            for j in range(bag):
+                r = (2 * q + parity) * bag + j
+                owner_row = owner_ref[pl.ds(r, 1), :]
+                local_row = local_ref[pl.ds(r, 1), :]
+                hit = device_row == owner_row
+                picks.append(
+                    jnp.concatenate(
+                        [
+                            jnp.where(hit, ((local_row >> 7) + 1).astype(F32), 0.0),
+                            jnp.where(hit, (local_row & 127).astype(F32), 0.0),
+                            jnp.where(hit, (q + 1).astype(F32), 0.0),
+                            jnp.where(hit, lane_value, 0.0),
+                        ],
+                        axis=0,
+                    ).astype(BF16)
+                )
+                places.append(jnp.where(rank_row == rank_ref[pl.ds(r, 1), :], 1.0, 0.0).astype(BF16))
+            lists[parity] += dot(jnp.concatenate(picks, axis=1), jnp.concatenate(places, axis=1), NT)
+        return carry
+
+    lax.fori_loop(0, tables // 2, list_step, 0)
+    sub = iota((8, LANES), 0)
+    is_last = iota((1, LANES), 1) == LANES - 1
+
+    def post(k):
+        o = me ^ k
+        tile = message[o]
+        rows_list = []
+        for parity in range(2):
+            count = tile[2 + parity : 3 + parity]
+            got = [lists[parity, pl.ds(part * n + o, 1), :].astype(I32) for part in range(4)]
+            asked = jnp.where(got[0] > 0, (got[0] - 1) * LANES + got[1], rows_dev)
+            slot = jnp.where(got[0] > 0, (got[2] - 1) * LANES + got[3], tables // 2 * LANES)
+            rows_list.append(jnp.where(is_last, count, asked))
+            mine_ref[o, parity : parity + 1, :] = jnp.where(is_last, count, slot)
+        tile = jnp.where(sub == 0, rows_list[0], jnp.where(sub == 1, rows_list[1], tile))
+        message[o] = jnp.where(sub == 4, most, jnp.where(sub == 5, weight_count, tile))
+
+    def post_and_send(k):
+        post(k)
+        exchange(n, me, message, replies, send_b, recv_b, k).start()
+
+    for_range(1, n, post_and_send)
+    post(0)
+    own_copy = pltpu.make_async_copy(message.at[me], replies.at[me], sems.at[0])
+    own_copy.start()
+    settle_step(2)
+    width = table_ref.shape[0]
+    rows_ref[rows_dev:, :] = jnp.zeros((rows_ref.shape[0] - rows_dev, LANES), F32)
+
+    def turn(b):
+        at = pl.ds(pl.multiple_of(b * LANES, LANES), LANES)
+        rows_ref[at, :] = jnp.concatenate([table_ref[:, at]] * (LANES // width), axis=0).T
+
+    for_range(0, rows_dev // LANES, turn)
+    settle_step(3)
+    for_range(1, n, lambda k: exchange(n, me, message, replies, send_b, recv_b, k).wait())
+    own_copy.wait()
+
+    def take(s, carry):
+        most, total = carry
+        tile = replies[s]
+        asked = jnp.clip(tile[0:2], 0, rows_dev)
+        theirs_ref[s] = asked
+        table_rows = per_table * block_rows
+        paired = lax.div(asked, 2 * table_rows) * table_rows + lax.rem(asked, table_rows)
+        pairs_ref[s] = jnp.where(is_last, asked, paired)
+        return jnp.maximum(most, tile), total + tile
+
+    most, total = lax.fori_loop(0, n, take, (jnp.zeros((8, LANES), I32), jnp.zeros((8, LANES), I32)))
+    stat_ref[...] = jnp.where(sub == 4, most, total)
+    to_scalars = pltpu.make_async_copy(theirs_ref, asked_smem, sems.at[0])
+    to_scalars.start()
+    to_scalars.wait()
+    lines_ref[n] = jnp.zeros((cap, LANES), F32)
+    collect = collector(cap, asked_smem, rows_ref)
+
+    def collect_and_send(i):
+        k = n - i
+        collect(me ^ k, rows_out, me ^ k)
+        exchange(n, me, rows_out, lines_ref, send_c, recv_c, k).start()
+
+    group = n // 4
+    for s in range(1, 4):
+        for_range((s - 1) * group + 1, s * group + 1, collect_and_send)
+        settle_step(3 + s)
+    for_range(3 * group + 1, n, collect_and_send)
+    collect(me, lines_ref, me)
+    for s in range(7, steps):
+        settle_step(s)
+    for_range(1, n, lambda k: exchange(n, me, rows_out, lines_ref, send_c, recv_c, k).wait())
+
+
+def collector(cap, lists_ref, rows_ref):
+    left = iota((1, LANES), 1) < LANES // 2
+
+    def collect(peer, target, slot):
+        def lines(g):
+            for i in range(8):
+                r = g * 8 + i
+                even = rows_ref[pl.ds(lists_ref[peer, 0, r], 1), :]
+                odd = rows_ref[pl.ds(lists_ref[peer, 1, r], 1), :]
+                target[slot, pl.ds(r, 1), :] = jnp.where(left, even, odd)
+
+        for_range(0, cap // 8, lines)
+
+    return collect
+
+
+def forward(
+    n, cap, tail_rows, row_ids, lengths, counts, mask, labels, row_home, table, mat_home,
+    experts_m, experts_v, towers_m, towers_v, gates_m, gates_v, small_m, small_v,
+):
+    samples, tables, bag = row_ids.shape
+    rows_dev, width = table.shape
+    tasks = labels.shape[1]
+    experts, features, hidden = experts_m.shape
+    per_table = row_home.shape[1] // n
+    block_rows = rows_dev // (tables * per_table)
+    levels = early_levels(n)
+    sizes = (n, cap, tables, bag, tasks, experts, per_table, block_rows, rows_dev)
+    ids = row_ids.transpose(1, 2, 0).reshape(tables * bag, samples)
+    vmem = pl.BlockSpec(memory_space=pltpu.VMEM)
+    smem = pl.BlockSpec(memory_space=pltpu.SMEM)
+    hbm = pl.BlockSpec(memory_space=pl.ANY)
+    slots = jax.ShapeDtypeStruct((tables * bag, LANES), I32)
+    lists = jax.ShapeDtypeStruct((n, 2, LANES), I32)
+    count = len(plan(n, experts, features, tail_rows))
+    small = pltpu.VMEM((n, 8, LANES), F32)
+    numbers = pltpu.VMEM((n, 8, LANES), I32)
+    slot_scratch = pltpu.VMEM((tables * bag, LANES), I32)
+    dma = pltpu.SemaphoreType.DMA((n,))
+    hops = pltpu.SemaphoreType.DMA((count, n.bit_length()))
+    return pl.pallas_call(
+        functools.partial(forward_kernel, sizes),
+        out_shape=(
+            jax.ShapeDtypeStruct((8, LANES), F32), slots, lists, lists, lists,
+            jax.ShapeDtypeStruct((8, LANES), I32), jax.ShapeDtypeStruct((n + 1, cap, LANES), F32),
+            jax.ShapeDtypeStruct((count, 2, 8 * n >> levels, hidden), F32),
+        ),
+        in_specs=[vmem, vmem, smem, vmem, vmem, vmem, vmem, smem, hbm, hbm] + [vmem] * 6,
+        out_specs=(vmem,) * 8,
+        scratch_shapes=[
+            small, small, numbers, numbers,
+            pltpu.VMEM((2, 4 * n, LANES), F32), pltpu.VMEM((LANES, LANES), F32),
+            slot_scratch, slot_scratch, slot_scratch,
+            pltpu.SMEM((n, 2, LANES), I32), pltpu.VMEM((rows_dev + 8, LANES), F32), pltpu.VMEM((n, cap, LANES), F32),
+            pltpu.VMEM((2, tail_rows, hidden), F32), pltpu.VMEM((count, 2, 4 * n, hidden), F32),
+        ]
+        + [pltpu.VMEM((count, 2, 4 * n >> i, hidden), F32) for i in range(levels - 1)]
+        + [dma] * 6 + [hops] * 2 + [pltpu.SemaphoreType.DMA((count, 2)), pltpu.SemaphoreType.DMA((2,))],
+        compiler_params=pltpu.CompilerParams(collective_id=0, has_side_effects=True, vmem_limit_bytes=56 * 2**20),
+        name="forward",
+    )(
+        ids, lengths.T, counts, mask.reshape(1, samples), labels.T, row_home, table.T, mat_home, experts_m, experts_v,
+        towers_m.transpose(0, 2, 1), towers_v.transpose(0, 2, 1), gates_m.transpose(0, 2, 1), gates_v.transpose(0, 2, 1),
+        small_m, small_v,
+    )
+
+
+def backward_kernel(
+    sizes, lists_ref, stat_ref, items_ref, fields_ref, pooled_ref, moments_ref, experts_ref, gates_ref, towers_ref, small_ref,
+    lines_ref, experts_out, tail_out, *rest,
+):
+    n, cap, tail_rows = sizes
+    levels, early = n.bit_length() - 1, early_levels(n)
+    stages, rest = list(rest[:levels]), rest[levels:]
+    late_stages, rest = [moments_ref] + list(rest[: levels - early]), rest[levels - early :]
+    grads, tail, tail_w, news, rows_ref, side, rows_out = rest[:7]
+    send_c, recv_c, sends, receives, send_m, recv_m, send_w, recv_w, local = rest[7:]
+    experts, features, hidden = experts_ref.shape
+    tasks, tower, _ = towers_ref.shape
+    chains = plan(n, experts, features, tail_rows)
+    unit = 8 * n
+    me = lax.axis_index("dev")
+    greet_all(n, me)
+
+    def late_hop(c, i):
+        order = chains[c][2]
+        bit = order[early + i]
+        half = late_stages[i + 1].shape[2]
+        at = rows_at((1 - bit_of(me, bit)) * half, half)
+        return pltpu.make_async_remote_copy(
+            src_ref=late_stages[i].at[c, :, at],
+            dst_ref=late_stages[i + 1].at[c],
+            send_sem=send_m.at[c, i],
+            recv_sem=recv_m.at[c, i],
+            device_id=(me ^ bit,),
+            device_id_type=MESH,
+        )
+
+    chosen = owner_side(me, n, items_ref, experts, tasks, tower)
+
+    def late_settle(i):
+        for c, chain in enumerate(chains):
+            late_hop(c, i).wait()
+            half = late_stages[i + 1].shape[2]
+            mine = rows_at(bit_of(me, chain[2][early + i]) * half, half)
+            flag = chosen(chain, early + i, half)
+            for w in range(2):
+                late_stages[i + 1][c, w] = jnp.where(flag, late_stages[i][c, w, mine, :], late_stages[i + 1][c, w])
+            if i + 1 < levels - early:
+                late_hop(c, i + 1).start()
+
+    for c in range(len(chains)):
+        late_hop(c, 0).start()
+    lines_ref[n] = jnp.zeros((cap, LANES), F32)
+    fill_tail(tail_w, towers_ref, gates_ref, small_ref)
+
+    def hop(c, i):
+        array, first, order, _ = chains[c]
+        source = tail if array == experts else grads.at[array]
+        return halving(me, source.at[first : first + unit], stages, sends, receives, c, order, i)
+
+    def settle(c, i):
+        array, first, order, _ = chains[c]
+        hop(c, i).wait()
+        half = stages[i].shape[1]
+        at = bit_of(me, order[i]) * half
+        if i > 0:
+            kept = stages[i - 1][c, rows_at(at, half), :]
+        elif array == experts:
+            kept = tail[rows_at(first + at, half), :]
+        else:
+            kept = grads[array, rows_at(first + at, half), :]
+        stages[i][c] += kept
+        if i + 1 < levels:
+            hop(c, i + 1).start()
+
+    def region(c, i):
+        array, first, order, _ = chains[c]
+        at = rows_at(first + start_of(me, order[: i + 1], unit), unit >> (i + 1))
+        return tail_out.at[:, at] if array == experts else experts_out.at[array, :, at]
+
+    def doubling(c, i):
+        return pltpu.make_async_remote_copy(
+            src_ref=region(c, i),
+            dst_ref=region(c, i),
+            send_sem=send_w.at[c, i],
+            recv_sem=recv_w.at[c, i],
+            device_id=(me ^ chains[c][2][i],),
+            device_id_type=MESH,
+        )
+
+    def renew(c):
+        array, first, order, _ = chains[c]
+        at = rows_at(first + start_of(me, order, unit), 8)
+        weight = tail_w[at, :] if array == experts else experts_ref[array, at, :]
+        moment = late_stages[-1]
+        grad = stages[-1][c]
+        news[c, 0] = stepped(weight, *moments(moment[c, 0], moment[c, 1], grad))
+        news[c, 1] = grad
+        copy = pltpu.make_async_copy(news.at[c], region(c, levels - 1), local.at[c])
+        copy.start()
+        copy.wait()
+
+    steps = len(set(chain[3] for chain in chains)) + 2 * levels
+
+    def step(s):
+        for c, chain in enumerate(chains):
+            j = s - chain[3]
+            if 0 <= j < levels:
+                settle(c, j)
+            if j == levels - 1:
+                renew(c)
+                doubling(c, levels - 1).start()
+            i = 2 * levels - 2 - j
+            if 0 <= i < levels - 1:
+                doubling(c, i + 1).wait()
+                doubling(c, i).start()
+            if j == 2 * levels - 1:
+                doubling(c, 0).wait()
+
+    def ready(array):
+        for c, chain in enumerate(chains):
+            if chain[0] == array:
+                hop(c, 0).start()
+
+    dense_pass(
+        ready, stat_ref, fields_ref, pooled_ref, experts_ref, tail_w, towers_ref, small_ref, grads, tail, rows_ref, side
+    )
+    collect = collector(cap, lists_ref, rows_ref)
+
+    def collect_and_send(i):
+        k = n - i
+        collect(me ^ k, rows_out, me ^ k)
+        exchange(n, me, rows_out, lines_ref, send_c, recv_c, k).start()
+
+    group = n // 8
+    for s in range(1, 8):
+        for_range((s - 1) * group + 1, s * group + 1, collect_and_send)
+        if s <= levels - early:
+            late_settle(s - 1)
+        step(s - 1)
+    for_range(7 * group + 1, n, collect_and_send)
+    collect(me, lines_ref, me)
+    for s in range(7, steps):
+        step(s)
+    for_range(1, n, lambda k: exchange(n, me, rows_out, lines_ref, send_c, recv_c, k).wait())
+
+
+def backward(n, cap, tail_rows, lists, stat, items, fields, pooled, moment_slices, experts_w, gates_w, towers_w, small):
+    experts, features, hidden = experts_w.shape
+    samples = fields.shape[1]
+    levels, early = n.bit_length() - 1, early_levels(n)
+    count = len(plan(n, experts, features, tail_rows))
+    vmem = pl.BlockSpec(memory_space=pltpu.VMEM)
+    smem = pl.BlockSpec(memory_space=pltpu.SMEM)
+    dma = pltpu.SemaphoreType.DMA((n,))
+    hops = pltpu.SemaphoreType.DMA((count, levels))
+    return pl.pallas_call(
+        functools.partial(backward_kernel, (n, cap, tail_rows)),
+        out_shape=(
+            jax.ShapeDtypeStruct((n + 1, cap, LANES), F32),
+            jax.ShapeDtypeStruct((experts, 2, features, hidden), F32),
+            jax.ShapeDtypeStruct((2, tail_rows, hidden), F32),
+        ),
+        in_specs=[smem, smem, smem] + [vmem] * 7,
+        out_specs=(vmem, pl.BlockSpec(memory_space=pl.ANY), vmem),
+        scratch_shapes=[pltpu.VMEM((count, 4 * n >> i, hidden), F32) for i in range(levels)]
+        + [pltpu.VMEM((count, 2, 8 * n >> (early + i + 1), hidden), F32) for i in range(levels - early)]
+        + [
+            pltpu.VMEM((experts, features, hidden), F32), pltpu.VMEM((tail_rows, hidden), F32),
+            pltpu.VMEM((tail_rows, hidden), F32), pltpu.VMEM((count, 2, 8, hidden), F32),
+            pltpu.VMEM((features // LANES * samples + 8, LANES), F32), pltpu.VMEM((samples, samples), F32),
+            pltpu.VMEM((n, cap, LANES), F32),
+        ]
+        + [dma] * 2 + [hops] * 6 + [pltpu.SemaphoreType.DMA((count,))],
+        compiler_params=pltpu.CompilerParams(collective_id=1, has_side_effects=True, vmem_limit_bytes=56 * 2**20),
+        name="backward",
+    )(lists, stat, items, fields, pooled, moment_slices, experts_w, gates_w, towers_w, small)
+
+
+def finish_kernel(
+    owned_ref, whole_ref, first_ref, second_ref, tail_ref, towers_m_ref, towers_v_ref, gates_m_ref, gates_v_ref,
+    small_m_ref, small_v_ref,
+    new_ref, low_ref, first_new_ref, second_new_ref,
+    towers_ref, towers_low_ref, towers_m_new_ref, towers_v_new_ref, gates_ref, gates_m_new_ref, gates_v_new_ref,
+    small_ref, small_m_new_ref, small_v_new_ref, loss_ref,
+):
+    e, b = pl.program_id(0), pl.program_id(1)
+    new = whole_ref[0, 0]
+    new_ref[0] = new
+    low_ref[0] = new.astype(BF16)
+
+    @pl.when(owned_ref[e] == 1)
+    def _():
+        first_new_ref[0], second_new_ref[0] = moments(first_ref[0], second_ref[0], whole_ref[0, 1])
+
+    @pl.when(owned_ref[e] != 1)
+    def _():
+        first_new_ref[...] = jnp.zeros_like(first_new_ref)
+        second_new_ref[...] = jnp.zeros_like(second_new_ref)
+
+    @pl.when((e == 0) & (b == 0))
+    def _():
+        experts = pl.num_programs(0)
+        tasks, tower, hidden = towers_ref.shape
+        count = gates_ref.shape[1]
+
+        def mine(item, pair):
+            own = jnp.full((1, 1), owned_ref[item], I32) == 1
+            return [jnp.where(own, x, 0.0) for x in pair]
+
+        for k in range(tasks):
+            at = slice(k * tower, (k + 1) * tower)
+            towers_ref[k] = tail_ref[0, at]
+            towers_low_ref[k] = tail_ref[0, at].astype(BF16)
+            towers_m_new_ref[k], towers_v_new_ref[k] = mine(
+                experts + tasks + k, moments(towers_m_ref[k], towers_v_ref[k], tail_ref[1, at])
+            )
+            for part in range(2):
+                row = tasks * tower + part * GAP + k * count
+                at = slice(row, row + count)
+                to = slice(part * hidden, (part + 1) * hidden)
+                gates_ref[k, :, to] = tail_ref[0, at]
+                gates_m_new_ref[k, :, to], gates_v_new_ref[k, :, to] = mine(
+                    experts + k, moments(gates_m_ref[k, :, to], gates_v_ref[k, :, to], tail_ref[1, at])
+                )
+        base = tasks * tower + 2 * GAP
+        size = small_ref.shape[1]
+        for i in range(-(-size // hidden)):
+            last = min(size, (i + 1) * hidden)
+            to = slice(i * hidden, last)
+            line = slice(0, last - i * hidden)
+            small_ref[0:1, to] = tail_ref[0, base + i : base + i + 1, line]
+            small_m_new_ref[0:1, to], small_v_new_ref[0:1, to] = mine(
+                experts + 2 * tasks,
+                moments(small_m_ref[0:1, to], small_v_ref[0:1, to], tail_ref[1, base + i : base + i + 1, line]),
+            )
+        loss_ref[...] = tail_ref[1, base + 8 : base + 9, 0:LANES]
+
+
+def finish(owned, whole, tail, experts_m, experts_v, towers_m, towers_v, gates_m, gates_v, small_m, small_v):
+    experts, features, hidden = experts_m.shape
+    rows = min(features, 512)
+    here = lambda e, b, owned: (e, b, 0)
+    only_owner = lambda e, b, owned: (e, jnp.where(owned[e] == 1, b, 0), 0)
+    block = pl.BlockSpec((1, rows, hidden), here)
+    owners = pl.BlockSpec((1, rows, hidden), only_owner)
+
+    def full(x):
+        return pl.BlockSpec(x.shape, lambda e, b, owned: (0,) * len(x.shape))
+
+    small_size = small_m.shape[1]
+    towers = jax.ShapeDtypeStruct(towers_m.shape, F32)
+    gates = jax.ShapeDtypeStruct(gates_m.shape, F32)
+    small = jax.ShapeDtypeStruct((1, small_size), F32)
+    wide = jax.ShapeDtypeStruct(experts_m.shape, F32)
+    tail_shapes = (
+        towers, jax.ShapeDtypeStruct(towers_m.shape, BF16), towers, towers, gates, gates, gates, small, small, small,
+        jax.ShapeDtypeStruct((1, LANES), F32),
+    )
+    return pl.pallas_call(
+        finish_kernel,
+        grid_spec=pltpu.PrefetchScalarGridSpec(
+            num_scalar_prefetch=1,
+            grid=(experts, features // rows),
+            in_specs=[
+                pl.BlockSpec((1, 2, rows, hidden), lambda e, b, owned: (e, 0, b, 0)), owners, owners,
+                full(tail), full(towers_m), full(towers_v), full(gates_m), full(gates_v), full(small_m), full(small_v),
+            ],
+            out_specs=[block, block, block, block] + [full(x) for x in tail_shapes],
+        ),
+        out_shape=(wide, jax.ShapeDtypeStruct(experts_m.shape, BF16), wide, wide) + tail_shapes,
+        compiler_params=pltpu.CompilerParams(vmem_limit_bytes=40 * 2**20),
+        name="finish",
+    )(owned, whole, experts_m, experts_v, tail, towers_m, towers_v, gates_m, gates_v, small_m, small_v)
+
+def pool_kernel(nothing, tables, bag, pos_ref, lines_ref, pooled_ref):
+    samples = pos_ref.shape[1]
+    pooled_ref[...] = jnp.zeros_like(pooled_ref)
+    left = iota((1, LANES), 1) < LANES // 2
+
+    def sample(s):
+        @pl.when(pos_ref[0, s] != nothing)
+        def _():
+            for q in range(tables // 2):
+                sums = []
+                for parity in range(2):
+                    base = (2 * q + parity) * bag
+                    total = lines_ref[pl.ds(pos_ref[base, s], 1), :]
+                    for j in range(1, bag):
+                        total = total + lines_ref[pl.ds(pos_ref[base + j, s], 1), :]
+                    sums.append(total)
+                pooled_ref[pl.ds(q * samples + s, 1), :] = jnp.where(left, sums[0], sums[1])
+
+    for_range(0, samples, sample)
+
+
+def pool(n, cap, tables, bag, pos, lines):
+    samples = pos.shape[1]
+    return pl.pallas_call(
+        functools.partial(pool_kernel, n * cap, tables, bag),
+        out_shape=jax.ShapeDtypeStruct((tables // 2 * samples, LANES), F32),
+        in_specs=[pl.BlockSpec(memory_space=pltpu.SMEM), pl.BlockSpec(memory_space=pltpu.VMEM)],
+        out_specs=pl.BlockSpec(memory_space=pltpu.VMEM),
+        compiler_params=pltpu.CompilerParams(vmem_limit_bytes=24 * 2**20),
+        name="pool",
+    )(pos, lines.reshape((n + 1) * cap, LANES))
+
+
+def split2(x):
+    high = x.astype(BF16)
+    return high, (x - high.astype(F32)).astype(BF16)
+
+
+def dot3(a, b, dims=NN):
+    return dot(a[0], b[0], dims) + dot(a[0], b[1], dims) + dot(a[1], b[0], dims)
+
+
+def sigmoid(x):
+    return 1.0 / (1.0 + jnp.exp(-x))
+
+
+def dense_pass(
+    ready, stat_ref, fields_ref, pooled_ref, experts_ref, tail_w, towers_ref, small_ref, grads, tail, rows_ref, side
+):
+    samples = fields_ref.shape[1]
+    experts, features, hidden = experts_ref.shape
+    tasks, tower, _ = towers_ref.shape
+    tail[...] = jnp.zeros_like(tail)
+
+    def put_tail(row, value):
+        tail[row : row + value.shape[0], :] = value
+
+    start = experts * hidden
+    tower_at = start
+    weight_at = start + tasks * tower
+    bias_at = weight_at + tasks * tower
+    side[0:8, :] = fields_ref[...]
+    side[8:, :] = jnp.zeros((samples - 8, samples), F32)
+    by_sample = side[...].T
+    weight = by_sample[:, tasks : tasks + 1]
+    scale = weight / stat_ref[0].astype(F32)
+    x = jnp.concatenate([pooled_ref[q * samples : (q + 1) * samples] for q in range(features // LANES)], axis=1)
+    x2 = split2(x)
+    at = tasks * tower
+    gate_w = jnp.concatenate([tail_w[at + k * GAP : at + k * GAP + tasks * experts, :] for k in range(2)], axis=1)
+    gate_w2 = split2(gate_w)
+    gate_logits = dot3(x2, gate_w2, NT)
+    pres, sigs, hids = [], [], []
+    for e in range(experts):
+        pre = dot3(x2, split2(experts_ref[e])) + small_ref[0:1, e * hidden : (e + 1) * hidden]
+        sig = sigmoid(pre)
+        pres.append(pre)
+        sigs.append(sig)
+        hids.append(pre * sig)
+    dhids = [jnp.zeros((samples, hidden), F32) for _ in range(experts)]
+    dgate_logits = []
+    loss = jnp.zeros((samples, 1), F32)
+    tower_bias_grads, out_weight_grads, task_bias_grads = [], [], []
+    for k in range(tasks):
+        logits = [gate_logits[:, k * experts + e : k * experts + e + 1] for e in range(experts)]
+        top = functools.reduce(jnp.maximum, logits)
+        powers = [jnp.exp(v - top) for v in logits]
+        whole = functools.reduce(jnp.add, powers)
+        gates = [v / whole for v in powers]
+        mix = functools.reduce(jnp.add, [gates[e] * hids[e] for e in range(experts)])
+        mix2 = split2(mix)
+        tower2 = split2(towers_ref[k])
+        at = tower_at + k * tower
+        pre = dot3(mix2, tower2, NT) + small_ref[0:1, at : at + tower]
+        sig = sigmoid(pre)
+        zed = pre * sig
+        at = weight_at + k * tower
+        out_weight = small_ref[0:1, at : at + tower]
+        logit = jnp.sum(zed * out_weight, axis=1, keepdims=True) + small_ref[0:1, bias_at + k : bias_at + k + 1]
+        label = by_sample[:, k : k + 1]
+        softplus = jnp.maximum(logit, 0.0) + jnp.log1p(jnp.exp(-jnp.abs(logit)))
+        loss = loss + weight * (softplus - label * logit)
+        dlogit = scale * (sigmoid(logit) - label)
+        task_bias_grads.append(jnp.sum(dlogit, axis=0, keepdims=True))
+        out_weight_grads.append(jnp.sum(dlogit * zed, axis=0, keepdims=True))
+        dpre = dlogit * out_weight * (sig * (1.0 + pre * (1.0 - sig)))
+        tower_bias_grads.append(jnp.sum(dpre, axis=0, keepdims=True))
+        dpre2 = split2(dpre)
+        put_tail(k * tower, dot3(split2(dpre.T), mix2))
+        dmix = dot3(dpre2, tower2)
+        dgates = [jnp.sum(dmix * hids[e], axis=1, keepdims=True) for e in range(experts)]
+        mean = functools.reduce(jnp.add, [gates[e] * dgates[e] for e in range(experts)])
+        for e in range(experts):
+            dgate_logits.append(gates[e] * (dgates[e] - mean))
+            dhids[e] = dhids[e] + gates[e] * dmix
+    lane = iota((samples, LANES), 1)
+    dgl = jnp.zeros((samples, LANES), F32)
+    for i, v in enumerate(dgate_logits):
+        dgl = jnp.where(lane == i, v, dgl)
+    count = tasks * experts
+    dgl_t2 = split2(dgl.T[0:16])
+    dgates_w = dot3(dgl_t2, x2)
+    tail_at = tasks * tower
+    put_tail(tail_at, dgates_w[:, :hidden])
+    put_tail(tail_at + GAP, dgates_w[:, hidden:])
+    dx = dot3(split2(dgl[:, :count]), gate_w2)
+    expert_bias_grads, dpres = [], []
+    for e in range(experts):
+        dpre = dhids[e] * (sigs[e] * (1.0 + pres[e] * (1.0 - sigs[e])))
+        expert_bias_grads.append(jnp.sum(dpre, axis=0, keepdims=True))
+        dpres.append(split2(dpre))
+        dx = dx + dot3(dpres[e], split2(experts_ref[e]), NT)
+    for q in range(features // LANES):
+        rows_ref[q * samples : (q + 1) * samples, :] = dx[:, q * LANES : (q + 1) * LANES]
+    rows_ref[features // LANES * samples :, :] = jnp.zeros((8, LANES), F32)
+    small_at = tail_at + 2 * GAP
+    pad = jnp.zeros((1, 2 * hidden - 2 * tasks * tower - tasks), F32)
+    line = jnp.concatenate(tower_bias_grads + out_weight_grads + task_bias_grads + [pad], axis=1)
+    loss_row = jnp.where(iota((1, hidden), 1) == 0, jnp.sum(loss, axis=0, keepdims=True), 0.0)
+    for e in range(experts):
+        put_tail(small_at + e, expert_bias_grads[e])
+    for i in range(line.shape[1] // hidden):
+        put_tail(small_at + experts + i, line[:, i * hidden : (i + 1) * hidden])
+    put_tail(small_at + 8, loss_row)
+    ready(experts)
+    x_t2 = split2(x.T)
+    for e in range(experts):
+        grads[e] = dot3(x_t2, dpres[e])
+        ready(e)
+
+
+def update_kernel(
+    sizes, pairs_ref, lines_ref, table_ref, first_ref, second_ref,
+    table_new_ref, first_new_ref, second_new_ref, sums_even, sums_odd,
+):
+    n, cap = sizes
+    step = pl.program_id(0)
+    width, block = table_ref.shape
+    half = block // 2
+    rows = sums_even.shape[0] - 8
+
+    @pl.when(step == 0)
+    def _():
+        def clear(i):
+            at = pl.ds(pl.multiple_of(i * half, half), half)
+            sums_even[at, :] = jnp.zeros((half, LANES), F32)
+            sums_odd[at, :] = jnp.zeros((half, LANES), F32)
+
+        for_range(0, rows // half, clear)
+
+        def source(s):
+            count = jnp.minimum(jnp.maximum(pairs_ref[s, 0, LANES - 1], pairs_ref[s, 1, LANES - 1]), cap)
+
+            def add(g):
+                for i in range(4):
+                    r = g * 4 + i
+                    line = lines_ref[pl.ds(s * cap + r, 1), :]
+                    sums_even[pl.ds(pairs_ref[s, 0, r], 1), :] += line
+                    sums_odd[pl.ds(pairs_ref[s, 1, r], 1), :] += line
+
+            for_range(0, (count + 3) // 4, add)
+
+        for_range(0, n, source)
+
+    left = iota((LANES, LANES), 1) < width
+    for b in range(half // LANES):
+        at = pl.ds(pl.multiple_of(step * half + b * LANES, LANES), LANES)
+        both = jnp.where(left, sums_even[at, :], sums_odd[at, :]).T
+        for parity in range(2):
+            here = slice(parity * half + b * LANES, parity * half + (b + 1) * LANES)
+            grad = both[parity * width : (parity + 1) * width]
+            first = BETA_ONE * first_ref[:, here] + (1.0 - BETA_ONE) * grad
+            mean = jnp.sum(grad * grad, axis=0, keepdims=True) * (1.0 / width)
+            second = BETA_TWO * second_ref[:, here] + (1.0 - BETA_TWO) * mean
+            rate = (RATE_ROWS / (1.0 - BETA_ONE**STEP)) / (
+                jnp.sqrt(second * (1.0 / (1.0 - BETA_TWO**STEP))) + EPSILON
+            )
+            old = table_ref[:, here]
+            table_new_ref[:, here] = old - (first * rate + (RATE_ROWS * DECAY) * old)
+            first_new_ref[:, here] = first
+            second_new_ref[:, here] = second
+
+
+def update(n, cap, table_rows, pairs, lines, table, table_m, table_v):
+    rows_dev, width = table.shape
+    block = 2 * table_rows
+    wide = pl.BlockSpec((width, block), lambda i: (0, i))
+    thin = pl.BlockSpec((1, block), lambda i: (0, i))
+    sums = pltpu.VMEM((rows_dev // 2 + 8, LANES), F32)
+    table_new, first_new, second_new = pl.pallas_call(
+        functools.partial(update_kernel, (n, cap)),
+        grid=(rows_dev // block,),
+        out_shape=(
+            jax.ShapeDtypeStruct((width, rows_dev), F32), jax.ShapeDtypeStruct((width, rows_dev), F32),
+            jax.ShapeDtypeStruct((1, rows_dev), F32),
+        ),
+        in_specs=[
+            pl.BlockSpec(memory_space=pltpu.SMEM), pl.BlockSpec(((n + 1) * cap, LANES), lambda i: (0, 0)), wide, wide, thin,
+        ],
+        out_specs=(wide, wide, thin),
+        scratch_shapes=[sums, sums],
+        compiler_params=pltpu.CompilerParams(vmem_limit_bytes=48 * 2**20),
+        name="update_rows",
+    )(pairs, lines.reshape((n + 1) * cap, LANES), table.T, table_m.T, table_v.reshape(1, rows_dev))
+    return table_new.T, first_new.T, second_new.reshape(rows_dev)
+
+def moments(first, second, grad):
+    return (
+        BETA_ONE * first + (1.0 - BETA_ONE) * grad,
+        BETA_TWO * second + (1.0 - BETA_TWO) * grad * grad,
+    )
+
+
+def stepped(weight, first_new, second_new):
+    first_hat = first_new / (1.0 - BETA_ONE**STEP)
+    second_hat = second_new / (1.0 - BETA_TWO**STEP)
+    return weight - RATE_DENSE * (first_hat / (jnp.sqrt(second_hat) + EPSILON) + DECAY * weight)
+
+
+def all_sum(tree, axis):
+    n = lax.axis_size(axis)
+    bit = 1
+    while bit < n:
+        pairs = [(i, i ^ bit) for i in range(n)]
+        tree = jax.tree.map(lambda x: x + lax.ppermute(x, axis, pairs), tree)
+        bit *= 2
+    return tree
 
 
 def from_root(block, axis, source):
     block = jnp.where(lax.axis_index(axis) == source, block, jnp.zeros_like(block))
-    return lax.psum(block, axis)
+    return all_sum(block, axis)
 
 
 def dense_forward(params, pooled, labels, weights):
@@ -31,11 +1006,11 @@
     out_weight = small[start : start + tasks * tower].reshape(tasks, tower)
     task_bias = small[start + tasks * tower :]
     hidden_act = jax.nn.silu(
-        jnp.einsum("si,eih->seh", pooled, experts_w, precision=HIGHEST) + expert_bias
-    )
-    gate = jax.nn.softmax(jnp.einsum("si,kie->ske", pooled, gates_w, precision=HIGHEST), axis=-1)
-    mixed = jnp.einsum("ske,seh->skh", gate, hidden_act, precision=HIGHEST)
-    zed = jax.nn.silu(jnp.einsum("skh,khc->skc", mixed, towers_w, precision=HIGHEST) + tower_bias)
+        jnp.einsum("si,eih->seh", pooled, experts_w, precision=lax.Precision.HIGHEST) + expert_bias
+    )
+    gate = jax.nn.softmax(jnp.einsum("si,kie->ske", pooled, gates_w, precision=lax.Precision.HIGHEST), axis=-1)
+    mixed = jnp.einsum("ske,seh->skh", gate, hidden_act, precision=lax.Precision.HIGHEST)
+    zed = jax.nn.silu(jnp.einsum("skh,khc->skc", mixed, towers_w, precision=lax.Precision.HIGHEST) + tower_bias)
     logit = jnp.sum(zed * out_weight, axis=-1) + task_bias
     losses = jax.nn.softplus(logit) - labels * logit
     return jnp.sum(weights[:, None] * losses)
@@ -50,7 +1025,7 @@
     return (weight_new, first_new, second_new)
 
 
-def per_device(
+def plain_step(
     row_ids,
     lengths,
     counts,
@@ -118,7 +1093,7 @@
     local_loss, pull = jax.vjp(
         lambda dense, features: dense_forward(dense, features, labels, weights), params, pooled
     )
-    loss_sum, weight_sum = lax.psum((local_loss, jnp.sum(weights)), "dev")
+    loss_sum, weight_sum = all_sum((local_loss, jnp.sum(weights)), "dev")
     local_grads, pooled_grad = pull(1.0 / weight_sum)
     slot_grads = (
         jnp.broadcast_to(
@@ -145,7 +1120,7 @@
         first_hat / (jnp.sqrt(second_hat)[:, None] + EPSILON) + DECAY * table
     )
     grad_experts, grad_gates, grad_towers, grad_small = local_grads
-    grad_experts, grad_gates, grad_towers, grad_small = lax.psum(
+    grad_experts, grad_gates, grad_towers, grad_small = all_sum(
         (grad_experts, grad_gates, grad_towers, grad_small), "dev"
     )
     kinds = (
@@ -203,56 +1178,80 @@
     )
 
 
+def per_device(*args):
+    (
+        row_ids, lengths, counts, mask, labels, row_home, mat_home, table, table_m, table_v,
+        experts_w, gates_w, towers_w, small_params,
+        experts_m, experts_v, gates_m, gates_v, towers_m, towers_v, small_m, small_v,
+    ) = args
+    n = lax.axis_size("dev")
+    me = lax.axis_index("dev")
+    samples, tables, bag = row_ids.shape
+    rows_dev, width = table.shape
+    cap = max(8, (samples * tables * bag // n * 5 // 16 + 7) // 8 * 8)
+    experts, features, hidden = experts_w.shape
+    tasks, _, tower = towers_w.shape
+    tail_rows = -(-(tasks * tower + 2 * GAP + 16) // (8 * n)) * 8 * n
+    fields, pos, mine, theirs, pairs, stat, lines, moment_slices = forward(
+        n, cap, tail_rows, row_ids, lengths, counts, mask, labels, row_home, table, mat_home,
+        experts_m[0], experts_v[0], towers_m[0], towers_v[0], gates_m[0], gates_v[0], small_m, small_v,
+    )
+    most, weight_count = stat[4, 0], stat[5, 0]
+
+    def usual(fields, pos, mine, pairs, lines, moment_slices, weight_count, *args):
+        (
+            _, _, _, _, _, _, mat_home, table, table_m, table_v, experts_w, gates_w, towers_w, small_params,
+            experts_m, experts_v, gates_m, gates_v, towers_m, towers_v, small_m, small_v,
+        ) = args
+
+        def turned(x):
+            return x.transpose(0, 2, 1)
+
+        gates_t, towers_t, small = turned(gates_w), turned(towers_w), small_params.reshape(1, -1)
+        pooled = pool(n, cap, tables, bag, pos, lines)
+        back, whole, tail = backward(
+            n, cap, tail_rows, mine, weight_count[None], mat_home, fields, pooled, moment_slices,
+            experts_w, gates_t, towers_t, small,
+        )
+        rows_new = update(n, cap, rows_dev // tables, pairs, back, table, table_m, table_v)
+        (
+            experts_new, experts_low, experts_m_new, experts_v_new,
+            towers_new, towers_low, towers_m_new, towers_v_new, gates_new, gates_m_new, gates_v_new,
+            small_new, small_m_new, small_v_new, loss,
+        ) = finish(
+            (mat_home == me).astype(I32), whole, tail, experts_m[0], experts_v[0], turned(towers_m[0]), turned(towers_v[0]),
+            turned(gates_m[0]), turned(gates_v[0]), small_m, small_v,
+        )
+        gates_new = turned(gates_new)
+        small_new = small_new.reshape(-1)
+        return (
+            loss[0, 0], weight_count.astype(F32), *rows_new, experts_new, gates_new, turned(towers_new), small_new,
+            experts_m_new[None], experts_v_new[None], turned(gates_m_new)[None], turned(gates_v_new)[None],
+            turned(towers_m_new)[None], turned(towers_v_new)[None], small_m_new, small_v_new,
+            experts_low[None], gates_new.astype(BF16)[None], turned(towers_low)[None], small_new.astype(BF16)[None],
+        )
+
+    def crowded(fields, pos, mine, pairs, lines, moment_slices, weight_count, *args):
+        return plain_step(*args)
+
+    return lax.cond(
+        most <= cap, usual, crowded, fields, pos, mine, pairs, lines, moment_slices, weight_count, *args
+    )
+
+
 def solution(mesh):
+    def split(dims):
+        return P("dev", *(None,) * (dims - 1))
+
+    by_device = split(4)
     return jax.shard_map(
         per_device,
         mesh=mesh,
         in_specs=(
-            P("dev", None, None),
-            P("dev", None),
-            P("dev"),
-            P("dev"),
-            P("dev", None),
-            P(),
-            P(),
-            P("dev", None),
-            P("dev", None),
-            P("dev"),
-            P(),
-            P(),
-            P(),
-            P(),
-            P("dev", None, None, None),
-            P("dev", None, None, None),
-            P("dev", None, None, None),
-            P("dev", None, None, None),
-            P("dev", None, None, None),
-            P("dev", None, None, None),
-            P("dev", None),
-            P("dev", None),
-        ),
-        out_specs=(
-            P(),
-            P(),
-            P("dev", None),
-            P("dev", None),
-            P("dev"),
-            P(),
-            P(),
-            P(),
-            P(),
-            P("dev", None, None, None),
-            P("dev", None, None, None),
-            P("dev", None, None, None),
-            P("dev", None, None, None),
-            P("dev", None, None, None),
-            P("dev", None, None, None),
-            P("dev", None),
-            P("dev", None),
-            P("dev", None, None, None),
-            P("dev", None, None, None),
-            P("dev", None, None, None),
-            P("dev", None),
-        ),
+            split(3), split(2), split(1), split(1), split(2), P(), P(), split(2), split(2), split(1),
+            P(), P(), P(), P(),
+        ) + (by_device,) * 6 + (split(2),) * 2,
+        out_specs=(P(), P(), split(2), split(2), split(1), P(), P(), P(), P())
+        + (by_device,) * 6 + (split(2),) * 2 + (by_device,) * 3 + (split(2),),
         check_vma=False,
     )

time: 1280 us -> 280 us (0.22)
  local copies, waits for them, and re-layouts: 473 us -> 8.07 us
  waiting for transfers between devices: 272 us -> 0 us
  Pallas kernels: 0 us -> 265 us
  blocking collectives: 222 us -> 0 us
  other arithmetic: 216 us -> 0.83 us
  matrix products: 41.3 us -> 0 us
  between operations: 34 us -> 4.46 us
  starting transfers between devices: 16.6 us -> 0 us
    gather x22 -> x0, local copies, waits for them, and re-layouts: 296 us -> none  [the longest x1 121 us: per_device(): slot_rows = arrived[safe_owner, slot_rank] * live_float[:, None]]
    psum x2 -> x0, waiting for transfers between devices: 271 us -> none  [the longest x1 144 us: per_device(): lax.psum((grad_experts, grad_gates, grad_towers, grad_small), 'dev')]
    pallas_call x0 -> x5, Pallas kernels: none -> 265 us  [the longest x1 136 us: backward(): pl.pallas_call(functools.partial(backward_kernel, (n, cap, tail_rows)), o...]
    psum x3 -> x0, blocking collectives: 222 us -> none  [the longest x2 130 us: per_device(): loss_sum, weight_sum = lax.psum((local_loss, jnp.sum(weights)), 'dev')]
    unnamed x168 -> x32, local copies, waits for them, and re-layouts: 96.7 us -> 0.66 us
    scatter-add x1 -> x0, other arithmetic: 83.5 us -> none  [per_device(): grad_table = jnp.zeros((rows_dev, width), jnp.float32).at[asked_rows.resh...]
    dot_general x12 -> x0, matrix products: 41.3 us -> none  [the longest x3 19.3 us: dense_forward(): jnp.einsum('si,eih->seh', pooled, experts_w, precision=HIGHEST)]
    scatter x2 -> x0, local copies, waits for them, and re-layouts: 36.6 us -> none  [the longest x1 30.5 us: per_device(): slot_rank = jnp.zeros(slots, jnp.int32).at[order].set(sorted_rank)]
  transfers between devices with their start and end apart: 5 -> 0, of which waited for: 3 -> 0; matrix products, arithmetic and copies ran while one was open for 8% -> 0% of each run, Pallas kernels for 0% -> 0%
where the time goes in v3:
time: 280 us
  Pallas kernels  265 us (95%)
  local copies, waits for them, and re-layouts  8.07 us (3%)
  between operations  4.46 us (2%)
    pallas_call x1, Pallas kernels, backward(): pl.pallas_call(functools.partial(backward_kernel, (n, cap, tail_rows)), o...  136 us
    pallas_call x1, Pallas kernels, forward(): pl.pallas_call(functools.partial(forward_kernel, sizes), out_shape=(jax.S...  90.2 us
    pallas_call x1, Pallas kernels, update(): pl.pallas_call(functools.partial(update_kernel, (n, cap)), grid=(rows_dev...  20.8 us
    pallas_call x1, Pallas kernels, finish(): pl.pallas_call(finish_kernel, grid_spec=pltpu.PrefetchScalarGridSpec(num_...  9.88 us
    pallas_call x1, Pallas kernels, pool(): pl.pallas_call(functools.partial(pool_kernel, n * cap, tables, bag), out_...  8.46 us
    cond x20, local copies, waits for them, and re-layouts  5.78 us

profile of v3, /device:TPU:0, one launch (start us, length us, event | category | flops | bytes accessed | tf_op | source)
XLA Modules:
  0.0 280.2 jit_solution(14289160431873622969)
XLA Ops:
  1.3 0.0 copy-start.4
  1.3 0.0 copy-start.26
  1.3 0.0 copy-start.29
  1.3 0.0 copy-start.32
  1.4 0.0 copy-start.35
  1.4 0.0 copy-start.38
  1.4 90.2 %forward.1 = (f32[8,128]{1,0:T(8,128)}, s32[64,128]{1,0:T(8,128)}, s32[32,2,128]{2,1,0:T(2,128)}, s32[32,2,128]{2,1,0:T(2,128)}, s32[32,2,128]{2,1,0:T(2,128)}, ...) custom-call(s32[64,128]{1,0:T(8,128)} %bitcast.746, s32[16,128]{1,0:T(8,128)} %bitcast.755, ...), custom_call_target="tpu_custom_call" | custom-call | tf_op jit(solution)/shard_map/forward/pallas_call | solution.py:448
  91.6 0.5 slice.240
  92.9 184.4 %conditional.1 = (f32[]{:T(128)}, f32[]{:T(128)}, f32[16384]{0:T(1024)S(1)}, f32[5,1024,2]{1,2,0:T(2,128)}, f32[5,512,64]{1,2,0:T(8,128)}, /*index=5*/f32[1669]{...) conditional(s32[]{:T(128)} %bitcast.231, (s32[1]{0:T(128)}, ...), branch_computations={%region_0.20_spmd, %region_20.21_spmd} | conditional | flops 5726617600 | bytes 815011776 | solution.py:1237
  93.1 0.5 slice.280
  94.3 0.6 reshape.941.small_ref
  94.9 8.5 %pool.1.pooled_ref = f32[1024,128]{1,0:T(8,128)S(1)} custom-call(s32[64,128]{1,0:T(8,128)} %get-tuple-element.187.pos_ref, f32[2640,128]{1,0:T(8,128)} %bitcast.733), custom_call_target="tpu_custom_call" | custom-call | tf_op jit(solution)/shard_map/cond/branch_1_fun/pool/pallas_call | solution.py:767
  103.4 0.0 copy-start.1
  103.4 0.8 copy-done.1
  104.2 135.9 %backward.1 = (f32[33,80,128]{2,1,0:T(8,128)}, f32[2,2,1024,512]{3,2,1,0:T(8,128)}, f32[2,512,512]{2,1,0:T(8,128)}) custom-call(s32[32,2,128]{2,1,0:T(2,128)} %get-tuple-element.184.lists_ref, s32[1]{0:T(128)} %bitcast.176.stat_ref, s32[13]{0:T(128)S(1)} %get-tuple-element.182.items_ref, f32[8,128]{1,0:T(8,128)} %get-tuple-element.186.fields_ref, ...), custom_call_target="tpu_custom_call" | custom-call | tf_op jit(solution)/shard_map/cond/branch_1_fun/backward/pallas_call | solution.py:625
  240.0 0.0 copy-done.8
  240.1 0.0 copy-done.16
  240.1 0.0 copy-done.18
  240.1 0.0 copy-start
  240.1 3.4 %copy-done = f32[2,2,1024,512]{3,2,1,0:T(8,128)S(1)} copy-done((f32[2,2,1024,512]{3,2,1,0:T(8,128)S(1)}, f32[2,2,1024,512]{3,2,1,0:T(8,128)}, u32[]{:S(2)}) %copy-start) | copy-done | bytes 8388632 | tf_op jit(solution)/shard_map/cond
  243.5 1.6 copy-done.2
  245.1 9.9 %finish.1 = (f32[2,1024,512]{2,1,0:T(8,128)}, bf16[2,1024,512]{2,1,0:T(8,128)(2,1)}, f32[2,1024,512]{2,1,0:T(8,128)}, f32[2,1024,512]{2,1,0:T(8,128)}, f32[5,64,...) custom-call(s32[13]{0:T(128)S(1)} %compare_convert_fusion.owned_ref,, ...), custom_call_target="tpu_custom_call" | custom-call | tf_op jit(solution)/shard_map/cond/branch_1_fun/finish/pallas_call | solution.py:728
  255.0 0.8 convert_bitcast_fusion
  255.8 0.0 copy-start.64
  255.8 20.8 %update_rows.1 = (f32[64,16384]{1,0:T(8,128)}, f32[64,16384]{1,0:T(8,128)}, f32[1,16384]{1,0:T(1,128)S(1)}) custom-call(s32[32,2,128]{2,1,0:T(2,128)S(1)} %copy-done.56, f32[2640,128]{1,0:T(8,128)S(1)} %bitcast.700, f32[64,16384]{1,0:T(8,128)S(1)} %bitcast.707, f32[64,16384]{1,0:T(8,128)} %bitcast.714, f32[1,16384]{1,0:T(1,128)S(1)} %bitcast.743), custom_call_target="tpu_custom_call" | custom-call | tf_op jit(solution)/shard_map/cond/branch_1_fun/update_rows/pallas_call | solution.py:953
  277.3 0.0 copy-start.47
  277.3 0.0 copy-start.63
  277.3 0.0 copy-start.65
  277.3 0.0 copy-start.66
  277.4 0.0 copy-start.69
  277.4 0.6 copy-done.47
  277.9 0.0 copy-done.69
  (32 shorter events, 0.1 us)
Async XLA Ops:
  1.3 91.5 %copy-start.4 = (s32[16,256]{1,0:T(8,128)S(1)}, s32[16,256]{1,0:T(8,128)}, u32[]{:S(2)}) copy-start(s32[16,256]{1,0:T(8,128)} %homes_ref.1) | copy-start | bytes 49156
  1.3 91.5 %copy-start.26 = (f32[5,1024,2]{1,2,0:T(2,128)S(1)}, f32[5,1024,2]{1,2,0:T(2,128)}, u32[]{:S(2)}) copy-start(f32[5,1024,2]{1,2,0:T(2,128)} %param.37) | copy-start | bytes 122884
  1.3 91.5 %copy-start.29 = (f32[1,5,1024,2]{2,3,1,0:T(2,128)S(1)}, f32[1,5,1024,2]{2,3,1,0:T(2,128)}, u32[]{:S(2)}) copy-start(f32[1,5,1024,2]{2,3,1,0:T(2,128)} %param.43) | copy-start | bytes 122884
  1.3 91.5 %copy-start.32 = (f32[1,5,1024,2]{2,3,1,0:T(2,128)S(1)}, f32[1,5,1024,2]{2,3,1,0:T(2,128)}, u32[]{:S(2)}) copy-start(f32[1,5,1024,2]{2,3,1,0:T(2,128)} %param.42) | copy-start | bytes 122884
  1.4 91.5 %copy-start.35 = (f32[16384]{0:T(1024)S(1)}, f32[16384]{0:T(1024)}, u32[]{:S(2)}) copy-start(f32[16384]{0:T(1024)} %param.35) | copy-start | bytes 196612
  1.4 91.5 %copy-start.38 = (s32[128,16,4]{0,2,1:T(4,128)S(1)}, s32[128,16,4]{0,2,1:T(4,128)}, u32[]{:S(2)}) copy-start(s32[128,16,4]{0,2,1:T(4,128)} %param.26) | copy-start | bytes 98308
  1.4 91.5 %copy-start.41 = (s32[13]{0:T(128)S(1)}, s32[13]{0:T(128)}, u32[]{:S(2)}) copy-start(s32[13]{0:T(128)} %items_ref.1) | copy-start | bytes 160
  1.4 91.5 %copy-start.44 = (f32[1669]{0:T(1024)S(1)}, f32[1669]{0:T(1024)}, u32[]{:S(2)}) copy-start(f32[1669]{0:T(1024)} %param.39) | copy-start | bytes 20032
  1.4 91.5 %copy-start.48 = (f32[1,1669]{1,0:T(1,128)S(1)}, f32[1,1669]{1,0:T(1,128)}, u32[]{:S(2)}) copy-start(f32[1,1669]{1,0:T(1,128)} %small_m_ref.1) | copy-start | bytes 20032
  1.4 91.5 %copy-start.51 = (f32[1,1669]{1,0:T(1,128)S(1)}, f32[1,1669]{1,0:T(1,128)}, u32[]{:S(2)}) copy-start(f32[1,1669]{1,0:T(1,128)} %small_v_ref.1) | copy-start | bytes 20032
  1.4 91.5 %copy-start.59 = (s32[128,16]{0,1:T(8,128)S(1)}, s32[128,16]{0,1:T(8,128)}, u32[]{:S(2)}) copy-start(s32[128,16]{0,1:T(8,128)} %param.27) | copy-start | bytes 24580
  103.4 0.8 copy-start.1
  104.2 135.9 %copy-start.8 = (f32[1,2,1024,512]{3,2,1,0:T(8,128)S(1)}, f32[1,2,1024,512]{3,2,1,0:T(8,128)}, u32[]{:S(2)}) copy-start(f32[1,2,1024,512]{3,2,1,0:T(8,128)} %get-tuple-element.195) | copy-start | bytes 12582916 | tf_op jit(solution)/shard_map/cond
  104.2 135.9 %copy-start.16 = (f32[1,5,512,64]{2,3,1,0:T(8,128)S(1)}, f32[1,5,512,64]{2,3,1,0:T(8,128)}, u32[]{:S(2)}) copy-start(f32[1,5,512,64]{2,3,1,0:T(8,128)} %get-tuple-element.198) | copy-start | bytes 1966084 | tf_op jit(solution)/shard_map/cond
  104.2 135.9 %copy-start.18 = (f32[1,5,512,64]{2,3,1,0:T(8,128)S(1)}, f32[1,5,512,64]{2,3,1,0:T(8,128)}, u32[]{:S(2)}) copy-start(f32[1,5,512,64]{2,3,1,0:T(8,128)} %get-tuple-element.199) | copy-start | bytes 1966084 | tf_op jit(solution)/shard_map/cond
  240.1 3.4 %copy-start = (f32[2,2,1024,512]{3,2,1,0:T(8,128)S(1)}, f32[2,2,1024,512]{3,2,1,0:T(8,128)}, u32[]{:S(2)}) copy-start(f32[2,2,1024,512]{3,2,1,0:T(8,128)} %get-tuple-element.194.whole_ref) | copy-start | bytes 25165828 | tf_op jit(solution)/shard_map/cond
  243.5 1.6 copy-start.2
  245.1 10.7 %copy-start.3 = (f32[33,80,128]{2,1,0:T(8,128)S(1)}, f32[33,80,128]{2,1,0:T(8,128)}, u32[]{:S(2)}) copy-start(f32[33,80,128]{2,1,0:T(8,128)} %get-tuple-element.207) | copy-start | bytes 4055044 | tf_op jit(solution)/shard_map/cond
  245.1 10.7 %copy-start.7 = (f32[16384,64]{0,1:T(8,128)S(1)}, f32[16384,64]{0,1:T(8,128)}, u32[]{:S(2)}) copy-start(f32[16384,64]{0,1:T(8,128)} %get-tuple-element.208) | copy-start | bytes 12582916 | tf_op jit(solution)/shard_map/cond
  245.1 10.7 %copy-start.56 = (s32[32,2,128]{2,1,0:T(2,128)S(1)}, s32[32,2,128]{2,1,0:T(2,128)}, u32[]{:S(2)}) copy-start(s32[32,2,128]{2,1,0:T(2,128)} %get-tuple-element.206.pairs_ref) | copy-start | bytes 98308 | tf_op jit(solution)/shard_map/cond
  255.8 20.8 %copy-start.64 = (f32[1,1669]{1,0:T(1,128)S(1)}, f32[1,1669]{1,0:T(1,128)}, u32[]{:S(2)}) copy-start(f32[1,1669]{1,0:T(1,128)} %get-tuple-element.936) | copy-start | bytes 20032 | tf_op jit(solution)/shard_map/cond
  277.3 0.6 copy-start.47
  277.3 0.6 copy-start.63
  277.3 0.6 copy-start.65
  277.3 0.6 copy-start.66
  277.4 0.6 copy-start.69

commit v4 on v3

--- a/solution.py
+++ b/solution.py
@@ -36,7 +36,10 @@
         return carry
 
     lax.fori_loop(1, n, signal, 0)
-    pl.semaphore_wait(barrier, n - 1)
+
+
+def await_all(n):
+    pl.semaphore_wait(pltpu.get_barrier_semaphore(), n - 1)
 
 
 def exchange(n, me, source, target, sends, receives, k):
@@ -186,6 +189,7 @@
     me = lax.axis_index("dev")
     shift = lax.rem(me * 13, n)
     per_pair = LANES // n
+    greet_all(n, me)
     table_of = lax.div(iota((rows, LANES), 0), bag)
     slot_of = lax.rem(iota((rows, LANES), 0), bag)
     expand = jnp.where(lax.div(iota((rows, tables), 0), bag) == iota((rows, tables), 1), 1.0, 0.0).astype(BF16)
@@ -203,7 +207,7 @@
     high, middle, low = split3(field_scratch[...])
     spread = dot(pick, high, NT) + dot(pick, middle, NT) + dot(pick, low, NT)
     outbox[...] = spread.reshape(n, 8, LANES)
-    greet_all(n, me)
+    await_all(n)
     own_copy = pltpu.make_async_copy(outbox.at[me], inbox.at[me], sems.at[0])
     own_copy.start()
     for_range(1, n, lambda k: exchange(n, me, outbox, inbox, send_a, recv_a, k).start())
@@ -244,12 +248,13 @@
         if i + 1 < levels:
             hop(c, i + 1).start()
 
-    steps = len(set(chain[3] for chain in chains)) + levels - 1
-
-    def settle_step(s):
-        for c, chain in enumerate(chains):
-            if 0 <= s - chain[3] < levels:
-                settle(c, s - chain[3])
+    events = [(c, j) for t in range(16) for c, chain in enumerate(chains) for j in (t - chain[3],) if 0 <= j < levels]
+    done = [0]
+
+    def settle_some(count):
+        for c, j in events[done[0] : done[0] + count]:
+            settle(c, j)
+        done[0] += count
 
     homes = homes_ref[...]
     blocks = homes.shape[1]
@@ -266,7 +271,7 @@
     above = jnp.where(earlier | totals, 1.0, 0.0).astype(BF16)
     for_range(1, n, lambda k: exchange(n, me, outbox, inbox, send_a, recv_a, k).wait())
     own_copy.wait()
-    settle_step(0)
+    settle_some(4)
     arrived = inbox[...].reshape(n * 8, LANES).T
     high, middle, low = split3(arrived)
     fields = dot(high, gather_back) + dot(middle, gather_back) + dot(low, gather_back)
@@ -297,11 +302,11 @@
         rank = jnp.where(is_mine, (dot(flags, before) + bases[0:rows]).astype(I32), rank)
         return rank, jnp.maximum(most, count)
 
-    rank, most = lax.fori_loop(
-        0, n, rank_step, (jnp.zeros((rows, LANES), I32), jnp.zeros((8, LANES), I32)), unroll=4
-    )
+    rank, most = jnp.zeros((rows, LANES), I32), jnp.zeros((8, LANES), I32)
+    for part in range(4):
+        rank, most = lax.fori_loop(part * n // 4, (part + 1) * n // 4, rank_step, (rank, most), unroll=4)
+        settle_some(1)
     rank_ref[...] = rank
-    settle_step(1)
     most = jnp.max(most, axis=0, keepdims=True)
     pos_ref[...] = jnp.where(live, jnp.where(rank < cap, owner * cap + rank, n * cap + 1), n * cap)
     lists[...] = jnp.zeros_like(lists)
@@ -332,7 +337,9 @@
             lists[parity] += dot(jnp.concatenate(picks, axis=1), jnp.concatenate(places, axis=1), NT)
         return carry
 
-    lax.fori_loop(0, tables // 2, list_step, 0)
+    for part in range(2):
+        lax.fori_loop(part * tables // 4, (part + 1) * tables // 4, list_step, 0)
+        settle_some(1)
     sub = iota((8, LANES), 0)
     is_last = iota((1, LANES), 1) == LANES - 1
 
@@ -358,7 +365,7 @@
     post(0)
     own_copy = pltpu.make_async_copy(message.at[me], replies.at[me], sems.at[0])
     own_copy.start()
-    settle_step(2)
+    settle_some(2)
     width = table_ref.shape[0]
     rows_ref[rows_dev:, :] = jnp.zeros((rows_ref.shape[0] - rows_dev, LANES), F32)
 
@@ -366,8 +373,9 @@
         at = pl.ds(pl.multiple_of(b * LANES, LANES), LANES)
         rows_ref[at, :] = jnp.concatenate([table_ref[:, at]] * (LANES // width), axis=0).T
 
-    for_range(0, rows_dev // LANES, turn)
-    settle_step(3)
+    for part in range(4):
+        for_range(part * (rows_dev // LANES // 4), (part + 1) * (rows_dev // LANES // 4), turn)
+        settle_some(2)
     for_range(1, n, lambda k: exchange(n, me, message, replies, send_b, recv_b, k).wait())
     own_copy.wait()
 
@@ -394,14 +402,11 @@
         collect(me ^ k, rows_out, me ^ k)
         exchange(n, me, rows_out, lines_ref, send_c, recv_c, k).start()
 
-    group = n // 4
-    for s in range(1, 4):
-        for_range((s - 1) * group + 1, s * group + 1, collect_and_send)
-        settle_step(3 + s)
-    for_range(3 * group + 1, n, collect_and_send)
+    for part in range(8):
+        for_range(part * n // 8 + (part == 0), (part + 1) * n // 8, collect_and_send)
+        settle_some(3)
     collect(me, lines_ref, me)
-    for s in range(7, steps):
-        settle_step(s)
+    settle_some(len(events) - done[0])
     for_range(1, n, lambda k: exchange(n, me, rows_out, lines_ref, send_c, recv_c, k).wait())
 
 
@@ -488,6 +493,7 @@
     unit = 8 * n
     me = lax.axis_index("dev")
     greet_all(n, me)
+    await_all(n)
 
     def late_hop(c, i):
         order = chains[c][2]
@@ -548,13 +554,16 @@
 
     def doubling(c, i):
         return pltpu.make_async_remote_copy(
-            src_ref=region(c, i),
+            src_ref=news.at[c] if i == levels - 1 else region(c, i),
             dst_ref=region(c, i),
             send_sem=send_w.at[c, i],
             recv_sem=recv_w.at[c, i],
             device_id=(me ^ chains[c][2][i],),
             device_id_type=MESH,
         )
+
+    def place(c):
+        return pltpu.make_async_copy(news.at[c], region(c, levels - 1), local.at[c])
 
     def renew(c):
         array, first, order, _ = chains[c]
@@ -564,9 +573,7 @@
         grad = stages[-1][c]
         news[c, 0] = stepped(weight, *moments(moment[c, 0], moment[c, 1], grad))
         news[c, 1] = grad
-        copy = pltpu.make_async_copy(news.at[c], region(c, levels - 1), local.at[c])
-        copy.start()
-        copy.wait()
+        place(c).start()
 
     steps = len(set(chain[3] for chain in chains)) + 2 * levels
 
@@ -579,6 +586,8 @@
                 renew(c)
                 doubling(c, levels - 1).start()
             i = 2 * levels - 2 - j
+            if i == levels - 2:
+                place(c).wait()
             if 0 <= i < levels - 1:
                 doubling(c, i + 1).wait()
                 doubling(c, i).start()
@@ -589,6 +598,8 @@
         for c, chain in enumerate(chains):
             if chain[0] == array:
                 hop(c, 0).start()
+        if array == experts:
+            late_settle(0)
 
     dense_pass(
         ready, stat_ref, fields_ref, pooled_ref, experts_ref, tail_w, towers_ref, small_ref, grads, tail, rows_ref, side
@@ -603,8 +614,8 @@
     group = n // 8
     for s in range(1, 8):
         for_range((s - 1) * group + 1, s * group + 1, collect_and_send)
-        if s <= levels - early:
-            late_settle(s - 1)
+        if 3 <= s <= 1 + levels - early:
+            late_settle(s - 2)
         step(s - 1)
     for_range(7 * group + 1, n, collect_and_send)
     collect(me, lines_ref, me)
@@ -645,101 +656,201 @@
     )(lists, stat, items, fields, pooled, moment_slices, experts_w, gates_w, towers_w, small)
 
 
-def finish_kernel(
-    owned_ref, whole_ref, first_ref, second_ref, tail_ref, towers_m_ref, towers_v_ref, gates_m_ref, gates_v_ref,
-    small_m_ref, small_v_ref,
-    new_ref, low_ref, first_new_ref, second_new_ref,
+def close_kernel(
+    sizes,
+    owned_ref, pairs_ref, lines_ref, table_ref, row_first_ref, row_second_ref,
+    whole_ref, first_ref, second_ref, tail_ref, towers_m_ref, towers_v_ref, gates_m_ref, gates_v_ref, small_m_ref, small_v_ref,
+    table_new_ref, row_first_new_ref, row_second_new_ref, new_ref, low_ref, first_new_ref, second_new_ref,
+    towers_ref, towers_low_ref, towers_m_new_ref, towers_v_new_ref, gates_ref, gates_m_new_ref, gates_v_new_ref,
+    small_ref, small_m_new_ref, small_v_new_ref, loss_ref,
+    sums_even, sums_odd,
+):
+    n, cap, experts, first_steps, steps_each = sizes
+    step = pl.program_id(0)
+    width, block = table_ref.shape
+    half = block // 2
+    rows = sums_even.shape[0] - 8
+
+    @pl.when(step == 0)
+    def _():
+        def clear(i):
+            at = pl.ds(pl.multiple_of(i * half, half), half)
+            sums_even[at, :] = jnp.zeros((half, LANES), F32)
+            sums_odd[at, :] = jnp.zeros((half, LANES), F32)
+
+        for_range(0, rows // half, clear)
+        finish_tail(
+            owned_ref, experts, tail_ref, towers_m_ref, towers_v_ref, gates_m_ref, gates_v_ref, small_m_ref, small_v_ref,
+            towers_ref, towers_low_ref, towers_m_new_ref, towers_v_new_ref, gates_ref, gates_m_new_ref, gates_v_new_ref,
+            small_ref, small_m_new_ref, small_v_new_ref, loss_ref,
+        )
+
+    @pl.when(step < first_steps)
+    def _():
+        e = lax.div(step, steps_each)
+        new = whole_ref[0, 0]
+        new_ref[0] = new
+        low_ref[0] = new.astype(BF16)
+
+        @pl.when(owned_ref[e] == 1)
+        def _():
+            first_new_ref[0], second_new_ref[0] = moments(first_ref[0], second_ref[0], whole_ref[0, 1])
+
+        @pl.when(owned_ref[e] != 1)
+        def _():
+            first_new_ref[...] = jnp.zeros_like(first_new_ref)
+            second_new_ref[...] = jnp.zeros_like(second_new_ref)
+
+        def source(s):
+            count = jnp.minimum(jnp.maximum(pairs_ref[s, 0, LANES - 1], pairs_ref[s, 1, LANES - 1]), cap)
+
+            def add(g):
+                for i in range(8):
+                    r = g * 8 + i
+                    line = lines_ref[pl.ds(s * cap + r, 1), :]
+                    sums_even[pl.ds(pairs_ref[s, 0, r], 1), :] += line
+                    sums_odd[pl.ds(pairs_ref[s, 1, r], 1), :] += line
+
+            for_range(0, (count + 7) // 8, add)
+
+        for_range(step * n // first_steps, (step + 1) * n // first_steps, source)
+
+    @pl.when(step >= first_steps)
+    def _():
+        left = iota((LANES, LANES), 1) < width
+        for b in range(half // LANES):
+            at = pl.ds(pl.multiple_of((step - first_steps) * half + b * LANES, LANES), LANES)
+            both = jnp.where(left, sums_even[at, :], sums_odd[at, :]).T
+            for parity in range(2):
+                here = slice(parity * half + b * LANES, parity * half + (b + 1) * LANES)
+                grad = both[parity * width : (parity + 1) * width]
+                first = BETA_ONE * row_first_ref[:, here] + (1.0 - BETA_ONE) * grad
+                mean = jnp.sum(grad * grad, axis=0, keepdims=True) * (1.0 / width)
+                second = BETA_TWO * row_second_ref[:, here] + (1.0 - BETA_TWO) * mean
+                rate = (RATE_ROWS / (1.0 - BETA_ONE**STEP)) / (
+                    jnp.sqrt(second * (1.0 / (1.0 - BETA_TWO**STEP))) + EPSILON
+                )
+                old = table_ref[:, here]
+                table_new_ref[:, here] = old - (first * rate + (RATE_ROWS * DECAY) * old)
+                row_first_new_ref[:, here] = first
+                row_second_new_ref[:, here] = second
+
+
+def finish_tail(
+    owned_ref, experts, tail_ref, towers_m_ref, towers_v_ref, gates_m_ref, gates_v_ref, small_m_ref, small_v_ref,
     towers_ref, towers_low_ref, towers_m_new_ref, towers_v_new_ref, gates_ref, gates_m_new_ref, gates_v_new_ref,
     small_ref, small_m_new_ref, small_v_new_ref, loss_ref,
 ):
-    e, b = pl.program_id(0), pl.program_id(1)
-    new = whole_ref[0, 0]
-    new_ref[0] = new
-    low_ref[0] = new.astype(BF16)
-
-    @pl.when(owned_ref[e] == 1)
-    def _():
-        first_new_ref[0], second_new_ref[0] = moments(first_ref[0], second_ref[0], whole_ref[0, 1])
-
-    @pl.when(owned_ref[e] != 1)
-    def _():
-        first_new_ref[...] = jnp.zeros_like(first_new_ref)
-        second_new_ref[...] = jnp.zeros_like(second_new_ref)
-
-    @pl.when((e == 0) & (b == 0))
-    def _():
-        experts = pl.num_programs(0)
-        tasks, tower, hidden = towers_ref.shape
-        count = gates_ref.shape[1]
-
-        def mine(item, pair):
-            own = jnp.full((1, 1), owned_ref[item], I32) == 1
-            return [jnp.where(own, x, 0.0) for x in pair]
-
-        for k in range(tasks):
-            at = slice(k * tower, (k + 1) * tower)
-            towers_ref[k] = tail_ref[0, at]
-            towers_low_ref[k] = tail_ref[0, at].astype(BF16)
-            towers_m_new_ref[k], towers_v_new_ref[k] = mine(
-                experts + tasks + k, moments(towers_m_ref[k], towers_v_ref[k], tail_ref[1, at])
+    tasks, tower, hidden = towers_ref.shape
+    count = gates_ref.shape[1]
+
+    def mine(item, pair):
+        own = jnp.full((1, 1), owned_ref[item], I32) == 1
+        return [jnp.where(own, x, 0.0) for x in pair]
+
+    for k in range(tasks):
+        at = slice(k * tower, (k + 1) * tower)
+        towers_ref[k] = tail_ref[0, at]
+        towers_low_ref[k] = tail_ref[0, at].astype(BF16)
+        towers_m_new_ref[k], towers_v_new_ref[k] = mine(
+            experts + tasks + k, moments(towers_m_ref[k], towers_v_ref[k], tail_ref[1, at])
+        )
+        for part in range(2):
+            row = tasks * tower + part * GAP + k * count
+            at = slice(row, row + count)
+            to = slice(part * hidden, (part + 1) * hidden)
+            gates_ref[k, :, to] = tail_ref[0, at]
+            gates_m_new_ref[k, :, to], gates_v_new_ref[k, :, to] = mine(
+                experts + k, moments(gates_m_ref[k, :, to], gates_v_ref[k, :, to], tail_ref[1, at])
             )
-            for part in range(2):
-                row = tasks * tower + part * GAP + k * count
-                at = slice(row, row + count)
-                to = slice(part * hidden, (part + 1) * hidden)
-                gates_ref[k, :, to] = tail_ref[0, at]
-                gates_m_new_ref[k, :, to], gates_v_new_ref[k, :, to] = mine(
-                    experts + k, moments(gates_m_ref[k, :, to], gates_v_ref[k, :, to], tail_ref[1, at])
-                )
-        base = tasks * tower + 2 * GAP
-        size = small_ref.shape[1]
-        for i in range(-(-size // hidden)):
-            last = min(size, (i + 1) * hidden)
-            to = slice(i * hidden, last)
-            line = slice(0, last - i * hidden)
-            small_ref[0:1, to] = tail_ref[0, base + i : base + i + 1, line]
-            small_m_new_ref[0:1, to], small_v_new_ref[0:1, to] = mine(
-                experts + 2 * tasks,
-                moments(small_m_ref[0:1, to], small_v_ref[0:1, to], tail_ref[1, base + i : base + i + 1, line]),
-            )
-        loss_ref[...] = tail_ref[1, base + 8 : base + 9, 0:LANES]
-
-
-def finish(owned, whole, tail, experts_m, experts_v, towers_m, towers_v, gates_m, gates_v, small_m, small_v):
+    base = tasks * tower + 2 * GAP
+    size = small_ref.shape[1]
+    for i in range(-(-size // hidden)):
+        last = min(size, (i + 1) * hidden)
+        to = slice(i * hidden, last)
+        line = slice(0, last - i * hidden)
+        small_ref[0:1, to] = tail_ref[0, base + i : base + i + 1, line]
+        small_m_new_ref[0:1, to], small_v_new_ref[0:1, to] = mine(
+            experts + 2 * tasks,
+            moments(small_m_ref[0:1, to], small_v_ref[0:1, to], tail_ref[1, base + i : base + i + 1, line]),
+        )
+    loss_ref[...] = tail_ref[1, base + 8 : base + 9, 0:LANES]
+
+
+def close(
+    n, cap, table_rows, pairs, lines, table, table_m, table_v,
+    owned, whole, tail, experts_m, experts_v, towers_m, towers_v, gates_m, gates_v, small_m, small_v,
+):
+    rows_dev, width = table.shape
     experts, features, hidden = experts_m.shape
-    rows = min(features, 512)
-    here = lambda e, b, owned: (e, b, 0)
-    only_owner = lambda e, b, owned: (e, jnp.where(owned[e] == 1, b, 0), 0)
-    block = pl.BlockSpec((1, rows, hidden), here)
-    owners = pl.BlockSpec((1, rows, hidden), only_owner)
+    block = 2 * table_rows
+    rows = 256
+    steps_each = features // rows
+    first_steps = experts * steps_each
+    update_steps = rows_dev // block
+
+    def late(i, *_):
+        return (0, jnp.maximum(i - first_steps, 0))
+
+    def place(i):
+        i = jnp.minimum(i, first_steps - 1)
+        return lax.div(i, steps_each), lax.rem(i, steps_each)
+
+    def here(i, owned):
+        e, b = place(i)
+        return e, b, 0
+
+    def only_owner(i, owned):
+        e, b = place(i)
+        return e, jnp.where(owned[e] == 1, b, 0), 0
+
+    def both(i, owned):
+        e, b = place(i)
+        return e, 0, b, 0
+
+    wide, thin = pl.BlockSpec((width, block), late), pl.BlockSpec((1, block), late)
+    out_block, owners = pl.BlockSpec((1, rows, hidden), here), pl.BlockSpec((1, rows, hidden), only_owner)
 
     def full(x):
-        return pl.BlockSpec(x.shape, lambda e, b, owned: (0,) * len(x.shape))
-
-    small_size = small_m.shape[1]
+        return pl.BlockSpec(x.shape, lambda i, owned: (0,) * len(x.shape))
+
+    sums = pltpu.VMEM((rows_dev // 2 + 8, LANES), F32)
+    lines = lines.reshape((n + 1) * cap, LANES)
     towers = jax.ShapeDtypeStruct(towers_m.shape, F32)
     gates = jax.ShapeDtypeStruct(gates_m.shape, F32)
-    small = jax.ShapeDtypeStruct((1, small_size), F32)
-    wide = jax.ShapeDtypeStruct(experts_m.shape, F32)
+    small = jax.ShapeDtypeStruct(small_m.shape, F32)
     tail_shapes = (
         towers, jax.ShapeDtypeStruct(towers_m.shape, BF16), towers, towers, gates, gates, gates, small, small, small,
         jax.ShapeDtypeStruct((1, LANES), F32),
     )
-    return pl.pallas_call(
-        finish_kernel,
+    dense_shape = jax.ShapeDtypeStruct(experts_m.shape, F32)
+    rows_shape = jax.ShapeDtypeStruct((width, rows_dev), F32)
+    out_shape = (
+        rows_shape, rows_shape, jax.ShapeDtypeStruct((1, rows_dev), F32),
+        dense_shape, jax.ShapeDtypeStruct(experts_m.shape, BF16), dense_shape, dense_shape,
+    ) + tail_shapes
+    table_new, first_new, second_new, *others = pl.pallas_call(
+        functools.partial(close_kernel, (n, cap, experts, first_steps, steps_each)),
         grid_spec=pltpu.PrefetchScalarGridSpec(
             num_scalar_prefetch=1,
-            grid=(experts, features // rows),
+            grid=(first_steps + update_steps,),
             in_specs=[
-                pl.BlockSpec((1, 2, rows, hidden), lambda e, b, owned: (e, 0, b, 0)), owners, owners,
+                pl.BlockSpec(memory_space=pltpu.SMEM), full(lines), wide, wide, thin,
+                pl.BlockSpec((1, 2, rows, hidden), both), owners, owners,
                 full(tail), full(towers_m), full(towers_v), full(gates_m), full(gates_v), full(small_m), full(small_v),
             ],
-            out_specs=[block, block, block, block] + [full(x) for x in tail_shapes],
+            out_specs=[wide, wide, thin] + [out_block] * 4 + [full(x) for x in tail_shapes],
+            scratch_shapes=[sums, sums],
         ),
-        out_shape=(wide, jax.ShapeDtypeStruct(experts_m.shape, BF16), wide, wide) + tail_shapes,
-        compiler_params=pltpu.CompilerParams(vmem_limit_bytes=40 * 2**20),
-        name="finish",
-    )(owned, whole, experts_m, experts_v, tail, towers_m, towers_v, gates_m, gates_v, small_m, small_v)
+        out_shape=out_shape,
+        compiler_params=pltpu.CompilerParams(vmem_limit_bytes=58 * 2**20),
+        name="close",
+    )(
+        owned, pairs, lines, table.T, table_m.T, table_v.reshape(1, rows_dev),
+        whole, experts_m, experts_v, tail, towers_m, towers_v, gates_m, gates_v, small_m, small_v,
+    )
+    return (table_new.T, first_new.T, second_new.reshape(rows_dev)), others
+
 
 def pool_kernel(nothing, tables, bag, pos_ref, lines_ref, pooled_ref):
     samples = pos_ref.shape[1]
@@ -866,16 +977,11 @@
     tail_at = tasks * tower
     put_tail(tail_at, dgates_w[:, :hidden])
     put_tail(tail_at + GAP, dgates_w[:, hidden:])
-    dx = dot3(split2(dgl[:, :count]), gate_w2)
     expert_bias_grads, dpres = [], []
     for e in range(experts):
         dpre = dhids[e] * (sigs[e] * (1.0 + pres[e] * (1.0 - sigs[e])))
         expert_bias_grads.append(jnp.sum(dpre, axis=0, keepdims=True))
         dpres.append(split2(dpre))
-        dx = dx + dot3(dpres[e], split2(experts_ref[e]), NT)
-    for q in range(features // LANES):
-        rows_ref[q * samples : (q + 1) * samples, :] = dx[:, q * LANES : (q + 1) * LANES]
-    rows_ref[features // LANES * samples :, :] = jnp.zeros((8, LANES), F32)
     small_at = tail_at + 2 * GAP
     pad = jnp.zeros((1, 2 * hidden - 2 * tasks * tower - tasks), F32)
     line = jnp.concatenate(tower_bias_grads + out_weight_grads + task_bias_grads + [pad], axis=1)
@@ -890,82 +996,13 @@
     for e in range(experts):
         grads[e] = dot3(x_t2, dpres[e])
         ready(e)
-
-
-def update_kernel(
-    sizes, pairs_ref, lines_ref, table_ref, first_ref, second_ref,
-    table_new_ref, first_new_ref, second_new_ref, sums_even, sums_odd,
-):
-    n, cap = sizes
-    step = pl.program_id(0)
-    width, block = table_ref.shape
-    half = block // 2
-    rows = sums_even.shape[0] - 8
-
-    @pl.when(step == 0)
-    def _():
-        def clear(i):
-            at = pl.ds(pl.multiple_of(i * half, half), half)
-            sums_even[at, :] = jnp.zeros((half, LANES), F32)
-            sums_odd[at, :] = jnp.zeros((half, LANES), F32)
-
-        for_range(0, rows // half, clear)
-
-        def source(s):
-            count = jnp.minimum(jnp.maximum(pairs_ref[s, 0, LANES - 1], pairs_ref[s, 1, LANES - 1]), cap)
-
-            def add(g):
-                for i in range(4):
-                    r = g * 4 + i
-                    line = lines_ref[pl.ds(s * cap + r, 1), :]
-                    sums_even[pl.ds(pairs_ref[s, 0, r], 1), :] += line
-                    sums_odd[pl.ds(pairs_ref[s, 1, r], 1), :] += line
-
-            for_range(0, (count + 3) // 4, add)
-
-        for_range(0, n, source)
-
-    left = iota((LANES, LANES), 1) < width
-    for b in range(half // LANES):
-        at = pl.ds(pl.multiple_of(step * half + b * LANES, LANES), LANES)
-        both = jnp.where(left, sums_even[at, :], sums_odd[at, :]).T
-        for parity in range(2):
-            here = slice(parity * half + b * LANES, parity * half + (b + 1) * LANES)
-            grad = both[parity * width : (parity + 1) * width]
-            first = BETA_ONE * first_ref[:, here] + (1.0 - BETA_ONE) * grad
-            mean = jnp.sum(grad * grad, axis=0, keepdims=True) * (1.0 / width)
-            second = BETA_TWO * second_ref[:, here] + (1.0 - BETA_TWO) * mean
-            rate = (RATE_ROWS / (1.0 - BETA_ONE**STEP)) / (
-                jnp.sqrt(second * (1.0 / (1.0 - BETA_TWO**STEP))) + EPSILON
-            )
-            old = table_ref[:, here]
-            table_new_ref[:, here] = old - (first * rate + (RATE_ROWS * DECAY) * old)
-            first_new_ref[:, here] = first
-            second_new_ref[:, here] = second
-
-
-def update(n, cap, table_rows, pairs, lines, table, table_m, table_v):
-    rows_dev, width = table.shape
-    block = 2 * table_rows
-    wide = pl.BlockSpec((width, block), lambda i: (0, i))
-    thin = pl.BlockSpec((1, block), lambda i: (0, i))
-    sums = pltpu.VMEM((rows_dev // 2 + 8, LANES), F32)
-    table_new, first_new, second_new = pl.pallas_call(
-        functools.partial(update_kernel, (n, cap)),
-        grid=(rows_dev // block,),
-        out_shape=(
-            jax.ShapeDtypeStruct((width, rows_dev), F32), jax.ShapeDtypeStruct((width, rows_dev), F32),
-            jax.ShapeDtypeStruct((1, rows_dev), F32),
-        ),
-        in_specs=[
-            pl.BlockSpec(memory_space=pltpu.SMEM), pl.BlockSpec(((n + 1) * cap, LANES), lambda i: (0, 0)), wide, wide, thin,
-        ],
-        out_specs=(wide, wide, thin),
-        scratch_shapes=[sums, sums],
-        compiler_params=pltpu.CompilerParams(vmem_limit_bytes=48 * 2**20),
-        name="update_rows",
-    )(pairs, lines.reshape((n + 1) * cap, LANES), table.T, table_m.T, table_v.reshape(1, rows_dev))
-    return table_new.T, first_new.T, second_new.reshape(rows_dev)
+    dx = dot3(split2(dgl[:, :count]), gate_w2)
+    for e in range(experts):
+        dx = dx + dot3(dpres[e], split2(experts_ref[e]), NT)
+    for q in range(features // LANES):
+        rows_ref[q * samples : (q + 1) * samples, :] = dx[:, q * LANES : (q + 1) * LANES]
+    rows_ref[features // LANES * samples :, :] = jnp.zeros((8, LANES), F32)
+
 
 def moments(first, second, grad):
     return (
@@ -1213,12 +1250,12 @@
             n, cap, tail_rows, mine, weight_count[None], mat_home, fields, pooled, moment_slices,
             experts_w, gates_t, towers_t, small,
         )
-        rows_new = update(n, cap, rows_dev // tables, pairs, back, table, table_m, table_v)
-        (
+        rows_new, (
             experts_new, experts_low, experts_m_new, experts_v_new,
             towers_new, towers_low, towers_m_new, towers_v_new, gates_new, gates_m_new, gates_v_new,
             small_new, small_m_new, small_v_new, loss,
-        ) = finish(
+        ) = close(
+            n, cap, rows_dev // tables, pairs, back, table, table_m, table_v,
             (mat_home == me).astype(I32), whole, tail, experts_m[0], experts_v[0], turned(towers_m[0]), turned(towers_v[0]),
             turned(gates_m[0]), turned(gates_v[0]), small_m, small_v,
         )

time: 280 us -> 262 us (0.936)
  Pallas kernels: 265 us -> 251 us
  local copies, waits for them, and re-layouts: 8.07 us -> 3.09 us
    pallas_call x1, Pallas kernels: 90.2 us -> 84.6 us  [forward(): pl.pallas_call(functools.partial(forward_kernel, sizes), out_shape=(jax.S...]
    cond x20 -> x10, local copies, waits for them, and re-layouts: 5.78 us -> 0.8 us
    pallas_call x1, Pallas kernels: 136 us -> 131 us  [backward(): pl.pallas_call(functools.partial(backward_kernel, (n, cap, tail_rows)), o...]
    pallas_call x2 -> x1, Pallas kernels: 30.7 us -> 27.4 us  [close(): pl.pallas_call(functools.partial(close_kernel, (n, cap, experts, first_st...]
where the time goes in v4:
time: 262 us
  Pallas kernels  251 us (96%)
  between operations  4.45 us (2%)
  local copies, waits for them, and re-layouts  3.09 us (1%)
    pallas_call x1, Pallas kernels, backward(): pl.pallas_call(functools.partial(backward_kernel, (n, cap, tail_rows)), o...  131 us
    pallas_call x1, Pallas kernels, forward(): pl.pallas_call(functools.partial(forward_kernel, sizes), out_shape=(jax.S...  84.6 us
    pallas_call x1, Pallas kernels, close(): pl.pallas_call(functools.partial(close_kernel, (n, cap, experts, first_st...  27.4 us
    pallas_call x1, Pallas kernels, pool(): pl.pallas_call(functools.partial(pool_kernel, n * cap, tables, bag), out_...  8.19 us

profile of v4, /device:TPU:0, one launch (start us, length us, event | category | flops | bytes accessed | tf_op | source)
XLA Modules:
  0.0 262.4 jit_solution(9063538127644596832)
XLA Ops:
  1.3 0.0 copy-start.1
  1.3 0.0 copy-start.22
  1.3 0.0 copy-start.25
  1.3 0.0 copy-start.28
  1.4 0.0 copy-start.31
  1.4 0.0 copy-start.34
  1.4 0.0 copy-start.37
  1.4 0.0 copy-start.40
  1.4 0.0 copy-start.44
  1.4 0.0 copy-start.47
  1.4 0.0 copy-start.54
  1.4 84.6 %forward.1 = (f32[8,128]{1,0:T(8,128)}, s32[64,128]{1,0:T(8,128)}, s32[32,2,128]{2,1,0:T(2,128)}, s32[32,2,128]{2,1,0:T(2,128)}, s32[32,2,128]{2,1,0:T(2,128)}, ...) custom-call(s32[64,128]{1,0:T(8,128)} %bitcast.745, s32[16,128]{1,0:T(8,128)} %bitcast.754, ...), custom_call_target="tpu_custom_call" | custom-call | tf_op jit(solution)/shard_map/forward/pallas_call | solution.py:453
  86.1 0.5 slice.240
  87.2 0.0 copy-done.1
  87.4 172.1 %conditional.1 = (f32[]{:T(128)}, f32[]{:T(128)}, f32[16384]{0:T(1024)S(1)}, f32[5,1024,2]{1,2,0:T(2,128)}, f32[5,512,64]{1,2,0:T(8,128)}, /*index=5*/f32[1669]{...) conditional(s32[]{:T(128)} %bitcast.231, (s32[1]{0:T(128)}, ...), branch_computations={%region_0.20_spmd, %region_20.21_spmd} | conditional | flops 5726617600 | bytes 809605056 | solution.py:1274
  87.6 0.5 slice.280
  88.8 0.5 compare_convert_fusion.owned_ref
  89.3 0.6 reshape.941.small_ref
  89.9 8.2 %pool.1.pooled_ref = f32[1024,128]{1,0:T(8,128)S(1)} custom-call(s32[64,128]{1,0:T(8,128)} %get-tuple-element.188.pos_ref, f32[2640,128]{1,0:T(8,128)} %bitcast.732), custom_call_target="tpu_custom_call" | custom-call | tf_op jit(solution)/shard_map/cond/branch_1_fun/pool/pallas_call | solution.py:878
  98.1 0.0 copy-start
  98.1 0.8 copy-done
  98.9 130.9 %backward.1 = (f32[33,80,128]{2,1,0:T(8,128)}, f32[2,2,1024,512]{3,2,1,0:T(8,128)}, f32[2,512,512]{2,1,0:T(8,128)}) custom-call(s32[32,2,128]{2,1,0:T(2,128)} %get-tuple-element.185.lists_ref, s32[1]{0:T(128)} %bitcast.176.stat_ref, s32[13]{0:T(128)S(1)} %get-tuple-element.182.items_ref, f32[8,128]{1,0:T(8,128)} %get-tuple-element.187.fields_ref, ...), custom_call_target="tpu_custom_call" | custom-call | tf_op jit(solution)/shard_map/cond/branch_1_fun/backward/pallas_call | solution.py:636
  229.9 27.4 %close.1 = (f32[64,16384]{1,0:T(8,128)}, f32[64,16384]{1,0:T(8,128)}, f32[1,16384]{1,0:T(1,128)S(1)}, f32[2,1024,512]{2,1,0:T(8,128)}, bf16[2,1024,512]{2,1,0:T(...) custom-call(s32[13]{0:T(128)} %compare_convert_fusion.owned_ref, ...), custom_call_target="tpu_custom_call" | custom-call | tf_op jit(solution)/shard_map/cond/branch_1_fun/close/pallas_call | solution.py:832
  257.2 0.8 fusion.230
  258.0 0.8 convert_bitcast_fusion
  259.5 0.0 copy-start.43
  259.5 0.0 copy-start.57
  259.5 0.0 copy-start.58
  259.5 0.0 copy-start.60
  259.5 0.6 copy-done.43
  260.1 0.0 copy-done.58
  260.1 0.0 copy-done.60
  (19 shorter events, 0.0 us)
Async XLA Ops:
  1.3 85.9 %copy-start.1 = (s32[16,256]{1,0:T(8,128)S(1)}, s32[16,256]{1,0:T(8,128)}, u32[]{:S(2)}) copy-start(s32[16,256]{1,0:T(8,128)} %homes_ref.1) | copy-start | bytes 49156
  1.3 85.9 %copy-start.22 = (f32[5,1024,2]{1,2,0:T(2,128)S(1)}, f32[5,1024,2]{1,2,0:T(2,128)}, u32[]{:S(2)}) copy-start(f32[5,1024,2]{1,2,0:T(2,128)} %param.37) | copy-start | bytes 122884
  1.3 85.9 %copy-start.25 = (f32[1,5,1024,2]{2,3,1,0:T(2,128)S(1)}, f32[1,5,1024,2]{2,3,1,0:T(2,128)}, u32[]{:S(2)}) copy-start(f32[1,5,1024,2]{2,3,1,0:T(2,128)} %param.43) | copy-start | bytes 122884
  1.3 85.9 %copy-start.28 = (f32[1,5,1024,2]{2,3,1,0:T(2,128)S(1)}, f32[1,5,1024,2]{2,3,1,0:T(2,128)}, u32[]{:S(2)}) copy-start(f32[1,5,1024,2]{2,3,1,0:T(2,128)} %param.42) | copy-start | bytes 122884
  1.4 85.9 %copy-start.31 = (f32[16384]{0:T(1024)S(1)}, f32[16384]{0:T(1024)}, u32[]{:S(2)}) copy-start(f32[16384]{0:T(1024)} %param.35) | copy-start | bytes 196612
  1.4 85.9 %copy-start.34 = (s32[128,16,4]{0,2,1:T(4,128)S(1)}, s32[128,16,4]{0,2,1:T(4,128)}, u32[]{:S(2)}) copy-start(s32[128,16,4]{0,2,1:T(4,128)} %param.26) | copy-start | bytes 98308
  1.4 85.9 %copy-start.37 = (s32[13]{0:T(128)S(1)}, s32[13]{0:T(128)}, u32[]{:S(2)}) copy-start(s32[13]{0:T(128)} %items_ref.1) | copy-start | bytes 160
  1.4 85.9 %copy-start.40 = (f32[1669]{0:T(1024)S(1)}, f32[1669]{0:T(1024)}, u32[]{:S(2)}) copy-start(f32[1669]{0:T(1024)} %param.39) | copy-start | bytes 20032
  1.4 85.9 %copy-start.44 = (f32[1,1669]{1,0:T(1,128)S(1)}, f32[1,1669]{1,0:T(1,128)}, u32[]{:S(2)}) copy-start(f32[1,1669]{1,0:T(1,128)} %small_m_ref.1) | copy-start | bytes 20032
  1.4 85.9 %copy-start.47 = (f32[1,1669]{1,0:T(1,128)S(1)}, f32[1,1669]{1,0:T(1,128)}, u32[]{:S(2)}) copy-start(f32[1,1669]{1,0:T(1,128)} %small_v_ref.1) | copy-start | bytes 20032
  1.4 85.9 %copy-start.54 = (s32[128,16]{0,1:T(8,128)S(1)}, s32[128,16]{0,1:T(8,128)}, u32[]{:S(2)}) copy-start(s32[128,16]{0,1:T(8,128)} %param.27) | copy-start | bytes 24580
  98.1 0.8 copy-start
  98.9 131.0 %copy-start.5 = (f32[16384,64]{0,1:T(8,128)S(1)}, f32[16384,64]{0,1:T(8,128)}, u32[]{:S(2)}) copy-start(f32[16384,64]{0,1:T(8,128)} %get-tuple-element.196) | copy-start | bytes 12582916 | tf_op jit(solution)/shard_map/cond
  98.9 131.0 %copy-start.14 = (f32[1,5,512,64]{2,3,1,0:T(8,128)S(1)}, f32[1,5,512,64]{2,3,1,0:T(8,128)}, u32[]{:S(2)}) copy-start(f32[1,5,512,64]{2,3,1,0:T(8,128)} %get-tuple-element.203) | copy-start | bytes 1966084 | tf_op jit(solution)/shard_map/cond
  98.9 131.0 %copy-start.16 = (f32[1,5,512,64]{2,3,1,0:T(8,128)S(1)}, f32[1,5,512,64]{2,3,1,0:T(8,128)}, u32[]{:S(2)}) copy-start(f32[1,5,512,64]{2,3,1,0:T(8,128)} %get-tuple-element.204) | copy-start | bytes 1966084 | tf_op jit(solution)/shard_map/cond
  98.9 131.0 %copy-start.55 = (s32[32,2,128]{2,1,0:T(2,128)S(1)}, s32[32,2,128]{2,1,0:T(2,128)}, u32[]{:S(2)}) copy-start(s32[32,2,128]{2,1,0:T(2,128)} %get-tuple-element.184.pairs_ref) | copy-start | bytes 98308 | tf_op jit(solution)/shard_map/cond
  259.5 0.6 copy-start.43
  259.5 0.6 copy-start.57
  259.5 0.6 copy-start.58
  259.5 0.6 copy-start.60

commit v5 on v4

--- a/solution.py
+++ b/solution.py
@@ -173,11 +173,11 @@
 
 def forward_kernel(
     sizes,
-    ids_ref, lengths_ref, counts_ref, mask_ref, labels_ref, homes_ref, table_ref, items_ref,
+    ids_ref, lengths_ref, counts_ref, mask_ref, labels_ref, homes_ref, table_hbm, items_ref,
     experts_m_ref, experts_v_ref, towers_m_ref, towers_v_ref, gates_m_ref, gates_v_ref, small_m_ref, small_v_ref,
     fields_ref, pos_ref, mine_ref, theirs_ref, pairs_ref, stat_ref, lines_ref, moments_ref,
     outbox, inbox, message, replies, lists, field_scratch, owner_ref, rank_ref, local_ref, asked_smem, rows_ref, rows_out,
-    tails, kept_ref, *rest,
+    tails, kept_ref, table_ref, *rest,
 ):
     n, cap, tables, bag, tasks, experts, per_table, block_rows, rows_dev = sizes
     levels = early_levels(n)
@@ -190,6 +190,8 @@
     shift = lax.rem(me * 13, n)
     per_pair = LANES // n
     greet_all(n, me)
+    table_copy = pltpu.make_async_copy(table_hbm, table_ref, sems.at[1])
+    table_copy.start()
     table_of = lax.div(iota((rows, LANES), 0), bag)
     slot_of = lax.rem(iota((rows, LANES), 0), bag)
     expand = jnp.where(lax.div(iota((rows, tables), 0), bag) == iota((rows, tables), 1), 1.0, 0.0).astype(BF16)
@@ -305,7 +307,7 @@
     rank, most = jnp.zeros((rows, LANES), I32), jnp.zeros((8, LANES), I32)
     for part in range(4):
         rank, most = lax.fori_loop(part * n // 4, (part + 1) * n // 4, rank_step, (rank, most), unroll=4)
-        settle_some(1)
+        settle_some(2)
     rank_ref[...] = rank
     most = jnp.max(most, axis=0, keepdims=True)
     pos_ref[...] = jnp.where(live, jnp.where(rank < cap, owner * cap + rank, n * cap + 1), n * cap)
@@ -367,6 +369,7 @@
     own_copy.start()
     settle_some(2)
     width = table_ref.shape[0]
+    table_copy.wait()
     rows_ref[rows_dev:, :] = jnp.zeros((rows_ref.shape[0] - rows_dev, LANES), F32)
 
     def turn(b):
@@ -404,7 +407,7 @@
 
     for part in range(8):
         for_range(part * n // 8 + (part == 0), (part + 1) * n // 8, collect_and_send)
-        settle_some(3)
+        settle_some(3 * (part >= 4))
     collect(me, lines_ref, me)
     settle_some(len(events) - done[0])
     for_range(1, n, lambda k: exchange(n, me, rows_out, lines_ref, send_c, recv_c, k).wait())
@@ -457,7 +460,7 @@
             jax.ShapeDtypeStruct((8, LANES), I32), jax.ShapeDtypeStruct((n + 1, cap, LANES), F32),
             jax.ShapeDtypeStruct((count, 2, 8 * n >> levels, hidden), F32),
         ),
-        in_specs=[vmem, vmem, smem, vmem, vmem, vmem, vmem, smem, hbm, hbm] + [vmem] * 6,
+        in_specs=[vmem, vmem, smem, vmem, vmem, vmem, hbm, smem, hbm, hbm] + [vmem] * 6,
         out_specs=(vmem,) * 8,
         scratch_shapes=[
             small, small, numbers, numbers,
@@ -465,6 +468,7 @@
             slot_scratch, slot_scratch, slot_scratch,
             pltpu.SMEM((n, 2, LANES), I32), pltpu.VMEM((rows_dev + 8, LANES), F32), pltpu.VMEM((n, cap, LANES), F32),
             pltpu.VMEM((2, tail_rows, hidden), F32), pltpu.VMEM((count, 2, 4 * n, hidden), F32),
+            pltpu.VMEM((width, rows_dev), F32),
         ]
         + [pltpu.VMEM((count, 2, 4 * n >> i, hidden), F32) for i in range(levels - 1)]
         + [dma] * 6 + [hops] * 2 + [pltpu.SemaphoreType.DMA((count, 2)), pltpu.SemaphoreType.DMA((2,))],
@@ -478,21 +482,23 @@
 
 
 def backward_kernel(
-    sizes, lists_ref, stat_ref, items_ref, fields_ref, pooled_ref, moments_ref, experts_ref, gates_ref, towers_ref, small_ref,
+    sizes, lists_ref, stat_ref, items_ref, fields_ref, pooled_ref, moments_ref, experts_hbm, gates_ref, towers_ref, small_ref,
     lines_ref, experts_out, tail_out, *rest,
 ):
     n, cap, tail_rows = sizes
     levels, early = n.bit_length() - 1, early_levels(n)
     stages, rest = list(rest[:levels]), rest[levels:]
     late_stages, rest = [moments_ref] + list(rest[: levels - early]), rest[levels - early :]
-    grads, tail, tail_w, news, rows_ref, side, rows_out = rest[:7]
-    send_c, recv_c, sends, receives, send_m, recv_m, send_w, recv_w, local = rest[7:]
+    grads, tail, tail_w, news, rows_ref, side, rows_out, experts_ref = rest[:8]
+    send_c, recv_c, sends, receives, send_m, recv_m, send_w, recv_w, local = rest[8:]
     experts, features, hidden = experts_ref.shape
     tasks, tower, _ = towers_ref.shape
     chains = plan(n, experts, features, tail_rows)
     unit = 8 * n
     me = lax.axis_index("dev")
     greet_all(n, me)
+    weights_copy = pltpu.make_async_copy(experts_hbm, experts_ref, local.at[0])
+    weights_copy.start()
     await_all(n)
 
     def late_hop(c, i):
@@ -579,7 +585,7 @@
 
     def step(s):
         for c, chain in enumerate(chains):
-            j = s - chain[3]
+            j = s - chain[3] // 2
             if 0 <= j < levels:
                 settle(c, j)
             if j == levels - 1:
@@ -601,6 +607,7 @@
         if array == experts:
             late_settle(0)
 
+    weights_copy.wait()
     dense_pass(
         ready, stat_ref, fields_ref, pooled_ref, experts_ref, tail_w, towers_ref, small_ref, grads, tail, rows_ref, side
     )
@@ -611,16 +618,16 @@
         collect(me ^ k, rows_out, me ^ k)
         exchange(n, me, rows_out, lines_ref, send_c, recv_c, k).start()
 
-    group = n // 8
-    for s in range(1, 8):
-        for_range((s - 1) * group + 1, s * group + 1, collect_and_send)
-        if 3 <= s <= 1 + levels - early:
-            late_settle(s - 2)
-        step(s - 1)
-    for_range(7 * group + 1, n, collect_and_send)
+    sent = 0
+    for s in range(steps):
+        goal = min(n - 1, sent + (16 if s == 0 else 4))
+        if goal > sent:
+            for_range(sent + 1, goal + 1, collect_and_send)
+            sent = goal
+        if 2 <= s < 2 + levels - early - 1:
+            late_settle(s - 2 + 1)
+        step(s)
     collect(me, lines_ref, me)
-    for s in range(7, steps):
-        step(s)
     for_range(1, n, lambda k: exchange(n, me, rows_out, lines_ref, send_c, recv_c, k).wait())
 
 
@@ -640,7 +647,7 @@
             jax.ShapeDtypeStruct((experts, 2, features, hidden), F32),
             jax.ShapeDtypeStruct((2, tail_rows, hidden), F32),
         ),
-        in_specs=[smem, smem, smem] + [vmem] * 7,
+        in_specs=[smem, smem, smem] + [vmem] * 3 + [pl.BlockSpec(memory_space=pl.ANY)] + [vmem] * 3,
         out_specs=(vmem, pl.BlockSpec(memory_space=pl.ANY), vmem),
         scratch_shapes=[pltpu.VMEM((count, 4 * n >> i, hidden), F32) for i in range(levels)]
         + [pltpu.VMEM((count, 2, 8 * n >> (early + i + 1), hidden), F32) for i in range(levels - early)]
@@ -648,7 +655,7 @@
             pltpu.VMEM((experts, features, hidden), F32), pltpu.VMEM((tail_rows, hidden), F32),
             pltpu.VMEM((tail_rows, hidden), F32), pltpu.VMEM((count, 2, 8, hidden), F32),
             pltpu.VMEM((features // LANES * samples + 8, LANES), F32), pltpu.VMEM((samples, samples), F32),
-            pltpu.VMEM((n, cap, LANES), F32),
+            pltpu.VMEM((n, cap, LANES), F32), pltpu.VMEM((experts, features, hidden), F32),
         ]
         + [dma] * 2 + [hops] * 6 + [pltpu.SemaphoreType.DMA((count,))],
         compiler_params=pltpu.CompilerParams(collective_id=1, has_side_effects=True, vmem_limit_bytes=56 * 2**20),
@@ -891,7 +898,11 @@
 
 
 def dot3(a, b, dims=NN):
-    return dot(a[0], b[0], dims) + dot(a[0], b[1], dims) + dot(a[1], b[0], dims)
+    count = a[0].shape[0]
+    if count > LANES:
+        return dot(a[0], b[0], dims) + dot(a[0], b[1], dims) + dot(a[1], b[0], dims)
+    both = dot(jnp.concatenate(a, axis=0), b[0], dims)
+    return both[:count] + both[count:] + dot(a[0], b[1], dims)
 
 
 def sigmoid(x):

time: 262 us -> 253 us (0.966)
  Pallas kernels: 251 us -> 240 us
    pallas_call x1, Pallas kernels: 131 us -> 121 us  [backward(): pl.pallas_call(functools.partial(backward_kernel, (n, cap, tail_rows)), o...]
where the time goes in v5:
time: 253 us; the launch traced here: 251 us
  Pallas kernels  240 us (95%)
  between operations  4.45 us (2%)
  local copies, waits for them, and re-layouts  3.09 us (1%)
    pallas_call x1, Pallas kernels, backward(): pl.pallas_call(functools.partial(backward_kernel, (n, cap, tail_rows)), o...  121 us
    pallas_call x1, Pallas kernels, forward(): pl.pallas_call(functools.partial(forward_kernel, sizes), out_shape=(jax.S...  83.3 us
    pallas_call x1, Pallas kernels, close(): pl.pallas_call(functools.partial(close_kernel, (n, cap, experts, first_st...  27.1 us
    pallas_call x1, Pallas kernels, pool(): pl.pallas_call(functools.partial(pool_kernel, n * cap, tables, bag), out_...  8.39 us

profile of v5, /device:TPU:0, one launch (start us, length us, event | category | flops | bytes accessed | tf_op | source)
XLA Modules:
  0.0 251.1 jit_solution(11911917213212381926)
XLA Ops:
  1.3 0.0 copy-start.1
  1.3 0.0 copy-start.22
  1.3 0.0 copy-start.25
  1.3 0.0 copy-start.28
  1.4 0.0 copy-start.31
  1.4 0.0 copy-start.34
  1.4 0.0 copy-start.37
  1.4 0.0 copy-start.40
  1.4 0.0 copy-start.44
  1.4 0.0 copy-start.47
  1.4 0.0 copy-start.54
  1.4 83.3 %forward.1 = (f32[8,128]{1,0:T(8,128)}, s32[64,128]{1,0:T(8,128)}, s32[32,2,128]{2,1,0:T(2,128)}, s32[32,2,128]{2,1,0:T(2,128)}, s32[32,2,128]{2,1,0:T(2,128)}, ...) custom-call(s32[64,128]{1,0:T(8,128)} %bitcast.745, s32[16,128]{1,0:T(8,128)} %bitcast.754, ...), custom_call_target="tpu_custom_call" | custom-call | tf_op jit(solution)/shard_map/forward/pallas_call | solution.py:456
  84.7 0.5 slice.240
  85.9 0.0 copy-done.1
  86.0 162.2 %conditional.1 = (f32[]{:T(128)}, f32[]{:T(128)}, f32[16384]{0:T(1024)S(1)}, f32[5,1024,2]{1,2,0:T(2,128)}, f32[5,512,64]{1,2,0:T(8,128)}, /*index=5*/f32[1669]{...) conditional(s32[]{:T(128)} %bitcast.231, (s32[1]{0:T(128)}, ...), branch_computations={%region_0.20_spmd, %region_20.21_spmd} | conditional | flops 5726617600 | bytes 809605056 | solution.py:1285
  86.2 0.5 slice.280
  87.4 0.5 compare_convert_fusion.owned_ref
  87.9 0.6 reshape.941.small_ref
  88.5 8.4 %pool.1.pooled_ref = f32[1024,128]{1,0:T(8,128)S(1)} custom-call(s32[64,128]{1,0:T(8,128)} %get-tuple-element.188.pos_ref, f32[2640,128]{1,0:T(8,128)} %bitcast.732), custom_call_target="tpu_custom_call" | custom-call | tf_op jit(solution)/shard_map/cond/branch_1_fun/pool/pallas_call | solution.py:885
  96.9 0.0 copy-start
  96.9 0.8 copy-done
  97.7 121.1 %backward.1 = (f32[33,80,128]{2,1,0:T(8,128)}, f32[2,2,1024,512]{3,2,1,0:T(8,128)}, f32[2,512,512]{2,1,0:T(8,128)}) custom-call(s32[32,2,128]{2,1,0:T(2,128)} %get-tuple-element.185.lists_ref, s32[1]{0:T(128)} %bitcast.176.stat_ref, s32[13]{0:T(128)S(1)} %get-tuple-element.182.items_ref, f32[8,128]{1,0:T(8,128)} %get-tuple-element.187.fields_ref, ...), custom_call_target="tpu_custom_call" | custom-call | tf_op jit(solution)/shard_map/cond/branch_1_fun/backward/pallas_call | solution.py:643
  218.8 27.1 %close.1 = (f32[64,16384]{1,0:T(8,128)}, f32[64,16384]{1,0:T(8,128)}, f32[1,16384]{1,0:T(1,128)S(1)}, f32[2,1024,512]{2,1,0:T(8,128)}, bf16[2,1024,512]{2,1,0:T(...) custom-call(s32[13]{0:T(128)} %compare_convert_fusion.owned_ref, ...), custom_call_target="tpu_custom_call" | custom-call | tf_op jit(solution)/shard_map/cond/branch_1_fun/close/pallas_call | solution.py:839
  245.9 0.8 fusion.230
  246.7 0.8 convert_bitcast_fusion
  248.1 0.0 copy-start.43
  248.2 0.0 copy-start.57
  248.2 0.0 copy-start.58
  248.2 0.0 copy-start.60
  248.2 0.6 copy-done.43
  248.8 0.0 copy-done.57
  248.8 0.0 copy-done.60
  (19 shorter events, 0.0 us)
Async XLA Ops:
  1.3 84.5 %copy-start.1 = (s32[16,256]{1,0:T(8,128)S(1)}, s32[16,256]{1,0:T(8,128)}, u32[]{:S(2)}) copy-start(s32[16,256]{1,0:T(8,128)} %homes_ref.1) | copy-start | bytes 49156
  1.3 84.5 %copy-start.22 = (f32[5,1024,2]{1,2,0:T(2,128)S(1)}, f32[5,1024,2]{1,2,0:T(2,128)}, u32[]{:S(2)}) copy-start(f32[5,1024,2]{1,2,0:T(2,128)} %param.37) | copy-start | bytes 122884
  1.3 84.5 %copy-start.25 = (f32[1,5,1024,2]{2,3,1,0:T(2,128)S(1)}, f32[1,5,1024,2]{2,3,1,0:T(2,128)}, u32[]{:S(2)}) copy-start(f32[1,5,1024,2]{2,3,1,0:T(2,128)} %param.43) | copy-start | bytes 122884
  1.3 84.5 %copy-start.28 = (f32[1,5,1024,2]{2,3,1,0:T(2,128)S(1)}, f32[1,5,1024,2]{2,3,1,0:T(2,128)}, u32[]{:S(2)}) copy-start(f32[1,5,1024,2]{2,3,1,0:T(2,128)} %param.42) | copy-start | bytes 122884
  1.4 84.5 %copy-start.31 = (f32[16384]{0:T(1024)S(1)}, f32[16384]{0:T(1024)}, u32[]{:S(2)}) copy-start(f32[16384]{0:T(1024)} %param.35) | copy-start | bytes 196612
  1.4 84.5 %copy-start.34 = (s32[128,16,4]{0,2,1:T(4,128)S(1)}, s32[128,16,4]{0,2,1:T(4,128)}, u32[]{:S(2)}) copy-start(s32[128,16,4]{0,2,1:T(4,128)} %param.26) | copy-start | bytes 98308
  1.4 84.5 %copy-start.37 = (s32[13]{0:T(128)S(1)}, s32[13]{0:T(128)}, u32[]{:S(2)}) copy-start(s32[13]{0:T(128)} %items_ref.1) | copy-start | bytes 160
  1.4 84.5 %copy-start.40 = (f32[1669]{0:T(1024)S(1)}, f32[1669]{0:T(1024)}, u32[]{:S(2)}) copy-start(f32[1669]{0:T(1024)} %param.39) | copy-start | bytes 20032
  1.4 84.5 %copy-start.44 = (f32[1,1669]{1,0:T(1,128)S(1)}, f32[1,1669]{1,0:T(1,128)}, u32[]{:S(2)}) copy-start(f32[1,1669]{1,0:T(1,128)} %small_m_ref.1) | copy-start | bytes 20032
  1.4 84.5 %copy-start.47 = (f32[1,1669]{1,0:T(1,128)S(1)}, f32[1,1669]{1,0:T(1,128)}, u32[]{:S(2)}) copy-start(f32[1,1669]{1,0:T(1,128)} %small_v_ref.1) | copy-start | bytes 20032
  1.4 84.5 %copy-start.54 = (s32[128,16]{0,1:T(8,128)S(1)}, s32[128,16]{0,1:T(8,128)}, u32[]{:S(2)}) copy-start(s32[128,16]{0,1:T(8,128)} %param.27) | copy-start | bytes 24580
  96.9 0.8 copy-start
  97.7 121.1 %copy-start.5 = (f32[16384,64]{0,1:T(8,128)S(1)}, f32[16384,64]{0,1:T(8,128)}, u32[]{:S(2)}) copy-start(f32[16384,64]{0,1:T(8,128)} %get-tuple-element.196) | copy-start | bytes 12582916 | tf_op jit(solution)/shard_map/cond
  97.7 121.1 %copy-start.14 = (f32[1,5,512,64]{2,3,1,0:T(8,128)S(1)}, f32[1,5,512,64]{2,3,1,0:T(8,128)}, u32[]{:S(2)}) copy-start(f32[1,5,512,64]{2,3,1,0:T(8,128)} %get-tuple-element.203) | copy-start | bytes 1966084 | tf_op jit(solution)/shard_map/cond
  97.7 121.1 %copy-start.16 = (f32[1,5,512,64]{2,3,1,0:T(8,128)S(1)}, f32[1,5,512,64]{2,3,1,0:T(8,128)}, u32[]{:S(2)}) copy-start(f32[1,5,512,64]{2,3,1,0:T(8,128)} %get-tuple-element.204) | copy-start | bytes 1966084 | tf_op jit(solution)/shard_map/cond
  97.7 121.1 %copy-start.55 = (s32[32,2,128]{2,1,0:T(2,128)S(1)}, s32[32,2,128]{2,1,0:T(2,128)}, u32[]{:S(2)}) copy-start(s32[32,2,128]{2,1,0:T(2,128)} %get-tuple-element.184.pairs_ref) | copy-start | bytes 98308 | tf_op jit(solution)/shard_map/cond
  248.1 0.6 copy-start.43
  248.2 0.6 copy-start.57
  248.2 0.6 copy-start.58
  248.2 0.6 copy-start.60

commit v6 on v5

--- a/solution.py
+++ b/solution.py
@@ -1236,7 +1236,7 @@
     me = lax.axis_index("dev")
     samples, tables, bag = row_ids.shape
     rows_dev, width = table.shape
-    cap = max(8, (samples * tables * bag // n * 5 // 16 + 7) // 8 * 8)
+    cap = max(8, (samples * tables * bag // n * 11 // 32 + 7) // 8 * 8)
     experts, features, hidden = experts_w.shape
     tasks, _, tower = towers_w.shape
     tail_rows = -(-(tasks * tower + 2 * GAP + 16) // (8 * n)) * 8 * n

time: 253 us -> 260 us (1.028)
  Pallas kernels: 240 us -> 248 us
    pallas_call x1, Pallas kernels: 121 us -> 125 us  [backward(): pl.pallas_call(functools.partial(backward_kernel, (n, cap, tail_rows)), o...]
    pallas_call x1, Pallas kernels: 83.3 us -> 86 us  [forward(): pl.pallas_call(functools.partial(forward_kernel, sizes), out_shape=(jax.S...]
where the time goes in v6:
time: 260 us; the launch traced here: 259 us
  Pallas kernels  248 us (95%)
  between operations  4.45 us (2%)
  local copies, waits for them, and re-layouts  3.09 us (1%)
    pallas_call x1, Pallas kernels, backward(): pl.pallas_call(functools.partial(backward_kernel, (n, cap, tail_rows)), o...  125 us
    pallas_call x1, Pallas kernels, forward(): pl.pallas_call(functools.partial(forward_kernel, sizes), out_shape=(jax.S...  86 us
    pallas_call x1, Pallas kernels, close(): pl.pallas_call(functools.partial(close_kernel, (n, cap, experts, first_st...  27.6 us
    pallas_call x1, Pallas kernels, pool(): pl.pallas_call(functools.partial(pool_kernel, n * cap, tables, bag), out_...  8.51 us

profile of v6, /device:TPU:0, one launch (start us, length us, event | category | flops | bytes accessed | tf_op | source)
XLA Modules:
  0.0 258.8 jit_solution(9364846452091886153)
XLA Ops:
  1.3 0.0 copy-start.1
  1.3 0.0 copy-start.22
  1.3 0.0 copy-start.25
  1.3 0.0 copy-start.28
  1.4 0.0 copy-start.31
  1.4 0.0 copy-start.34
  1.4 0.0 copy-start.37
  1.4 0.0 copy-start.40
  1.4 86.0 %forward.1 = (f32[8,128]{1,0:T(8,128)}, s32[64,128]{1,0:T(8,128)}, s32[32,2,128]{2,1,0:T(2,128)}, s32[32,2,128]{2,1,0:T(2,128)}, s32[32,2,128]{2,1,0:T(2,128)}, ...) custom-call(s32[64,128]{1,0:T(8,128)} %bitcast.745, s32[16,128]{1,0:T(8,128)} %bitcast.754, ...), custom_call_target="tpu_custom_call" | custom-call | tf_op jit(solution)/shard_map/forward/pallas_call | solution.py:456
  87.5 0.5 slice.240
  88.7 167.2 %conditional.1 = (f32[]{:T(128)}, f32[]{:T(128)}, f32[16384]{0:T(1024)S(1)}, f32[5,1024,2]{1,2,0:T(2,128)}, f32[5,512,64]{1,2,0:T(8,128)}, /*index=5*/f32[1669]{...) conditional(s32[]{:T(128)} %bitcast.231, (s32[1]{0:T(128)}, ...), branch_computations={%region_0.20_spmd, %region_20.21_spmd} | conditional | flops 5726617600 | bytes 809605056 | solution.py:1285
  89.0 0.5 slice.280
  90.1 0.5 compare_convert_fusion.owned_ref
  90.7 0.6 reshape.941.small_ref
  91.3 8.5 %pool.1.pooled_ref = f32[1024,128]{1,0:T(8,128)S(1)} custom-call(s32[64,128]{1,0:T(8,128)} %get-tuple-element.188.pos_ref, f32[2904,128]{1,0:T(8,128)} %bitcast.732), custom_call_target="tpu_custom_call" | custom-call | tf_op jit(solution)/shard_map/cond/branch_1_fun/pool/pallas_call | solution.py:885
  99.8 0.0 copy-start
  99.8 0.8 copy-done
  100.6 125.4 %backward.1 = (f32[33,88,128]{2,1,0:T(8,128)}, f32[2,2,1024,512]{3,2,1,0:T(8,128)}, f32[2,512,512]{2,1,0:T(8,128)}) custom-call(s32[32,2,128]{2,1,0:T(2,128)} %get-tuple-element.185.lists_ref, s32[1]{0:T(128)} %bitcast.176.stat_ref, s32[13]{0:T(128)S(1)} %get-tuple-element.182.items_ref, f32[8,128]{1,0:T(8,128)} %get-tuple-element.187.fields_ref, ...), custom_call_target="tpu_custom_call" | custom-call | tf_op jit(solution)/shard_map/cond/branch_1_fun/backward/pallas_call | solution.py:643
  226.0 0.0 copy-done.4
  226.0 0.0 copy-done.14
  226.0 0.0 copy-done.16
  226.0 0.0 copy-done.55
  226.0 27.6 %close.1 = (f32[64,16384]{1,0:T(8,128)}, f32[64,16384]{1,0:T(8,128)}, f32[1,16384]{1,0:T(1,128)S(1)}, f32[2,1024,512]{2,1,0:T(8,128)}, bf16[2,1024,512]{2,1,0:T(...) custom-call(s32[13]{0:T(128)} %compare_convert_fusion.owned_ref, ...), custom_call_target="tpu_custom_call" | custom-call | tf_op jit(solution)/shard_map/cond/branch_1_fun/close/pallas_call | solution.py:839
  253.7 0.8 fusion.230
  254.5 0.8 convert_bitcast_fusion
  255.9 0.0 copy-start.43
  255.9 0.0 copy-start.57
  255.9 0.0 copy-start.58
  255.9 0.0 copy-start.60
  255.9 0.6 copy-done.43
  256.5 0.0 copy-done.57
  256.5 0.0 copy-done.60
  (19 shorter events, 0.0 us)
Async XLA Ops:
  1.3 87.3 %copy-start.1 = (s32[16,256]{1,0:T(8,128)S(1)}, s32[16,256]{1,0:T(8,128)}, u32[]{:S(2)}) copy-start(s32[16,256]{1,0:T(8,128)} %homes_ref.1) | copy-start | bytes 49156
  1.3 87.3 %copy-start.22 = (f32[5,1024,2]{1,2,0:T(2,128)S(1)}, f32[5,1024,2]{1,2,0:T(2,128)}, u32[]{:S(2)}) copy-start(f32[5,1024,2]{1,2,0:T(2,128)} %param.37) | copy-start | bytes 122884
  1.3 87.3 %copy-start.25 = (f32[1,5,1024,2]{2,3,1,0:T(2,128)S(1)}, f32[1,5,1024,2]{2,3,1,0:T(2,128)}, u32[]{:S(2)}) copy-start(f32[1,5,1024,2]{2,3,1,0:T(2,128)} %param.43) | copy-start | bytes 122884
  1.3 87.3 %copy-start.28 = (f32[1,5,1024,2]{2,3,1,0:T(2,128)S(1)}, f32[1,5,1024,2]{2,3,1,0:T(2,128)}, u32[]{:S(2)}) copy-start(f32[1,5,1024,2]{2,3,1,0:T(2,128)} %param.42) | copy-start | bytes 122884
  1.4 87.3 %copy-start.31 = (f32[16384]{0:T(1024)S(1)}, f32[16384]{0:T(1024)}, u32[]{:S(2)}) copy-start(f32[16384]{0:T(1024)} %param.35) | copy-start | bytes 196612
  1.4 87.3 %copy-start.34 = (s32[128,16,4]{0,2,1:T(4,128)S(1)}, s32[128,16,4]{0,2,1:T(4,128)}, u32[]{:S(2)}) copy-start(s32[128,16,4]{0,2,1:T(4,128)} %param.26) | copy-start | bytes 98308
  1.4 87.3 %copy-start.37 = (s32[13]{0:T(128)S(1)}, s32[13]{0:T(128)}, u32[]{:S(2)}) copy-start(s32[13]{0:T(128)} %items_ref.1) | copy-start | bytes 160
  1.4 87.3 %copy-start.40 = (f32[1669]{0:T(1024)S(1)}, f32[1669]{0:T(1024)}, u32[]{:S(2)}) copy-start(f32[1669]{0:T(1024)} %param.39) | copy-start | bytes 20032
  1.4 87.3 %copy-start.44 = (f32[1,1669]{1,0:T(1,128)S(1)}, f32[1,1669]{1,0:T(1,128)}, u32[]{:S(2)}) copy-start(f32[1,1669]{1,0:T(1,128)} %small_m_ref.1) | copy-start | bytes 20032
  1.4 87.3 %copy-start.47 = (f32[1,1669]{1,0:T(1,128)S(1)}, f32[1,1669]{1,0:T(1,128)}, u32[]{:S(2)}) copy-start(f32[1,1669]{1,0:T(1,128)} %small_v_ref.1) | copy-start | bytes 20032
  1.4 87.3 %copy-start.54 = (s32[128,16]{0,1:T(8,128)S(1)}, s32[128,16]{0,1:T(8,128)}, u32[]{:S(2)}) copy-start(s32[128,16]{0,1:T(8,128)} %param.27) | copy-start | bytes 24580
  99.8 0.8 copy-start
  100.6 125.4 %copy-start.4 = (f32[16384,64]{0,1:T(8,128)S(1)}, f32[16384,64]{0,1:T(8,128)}, u32[]{:S(2)}) copy-start(f32[16384,64]{0,1:T(8,128)} %get-tuple-element.196) | copy-start | bytes 12582916 | tf_op jit(solution)/shard_map/cond
  100.6 125.4 %copy-start.14 = (f32[1,5,512,64]{2,3,1,0:T(8,128)S(1)}, f32[1,5,512,64]{2,3,1,0:T(8,128)}, u32[]{:S(2)}) copy-start(f32[1,5,512,64]{2,3,1,0:T(8,128)} %get-tuple-element.203) | copy-start | bytes 1966084 | tf_op jit(solution)/shard_map/cond
  100.6 125.4 %copy-start.16 = (f32[1,5,512,64]{2,3,1,0:T(8,128)S(1)}, f32[1,5,512,64]{2,3,1,0:T(8,128)}, u32[]{:S(2)}) copy-start(f32[1,5,512,64]{2,3,1,0:T(8,128)} %get-tuple-element.204) | copy-start | bytes 1966084 | tf_op jit(solution)/shard_map/cond
  100.6 125.5 %copy-start.55 = (s32[32,2,128]{2,1,0:T(2,128)S(1)}, s32[32,2,128]{2,1,0:T(2,128)}, u32[]{:S(2)}) copy-start(s32[32,2,128]{2,1,0:T(2,128)} %get-tuple-element.184.pairs_ref) | copy-start | bytes 98308 | tf_op jit(solution)/shard_map/cond
  255.9 0.6 copy-start.43
  255.9 0.6 copy-start.57
  255.9 0.6 copy-start.58
  255.9 0.6 copy-start.60

commit v7 on v6

--- a/solution.py
+++ b/solution.py
@@ -791,7 +791,7 @@
     rows_dev, width = table.shape
     experts, features, hidden = experts_m.shape
     block = 2 * table_rows
-    rows = 256
+    rows = min(512, features)
     steps_each = features // rows
     first_steps = experts * steps_each
     update_steps = rows_dev // block

time: 260 us -> 259 us (level)
  no operation moved by 1% of the time
where the time goes in v7:
time: 259 us; the launch traced here: 258 us
  Pallas kernels  247 us (95%)
  between operations  4.45 us (2%)
  local copies, waits for them, and re-layouts  3.09 us (1%)
    pallas_call x1, Pallas kernels, backward(): pl.pallas_call(functools.partial(backward_kernel, (n, cap, tail_rows)), o...  125 us
    pallas_call x1, Pallas kernels, forward(): pl.pallas_call(functools.partial(forward_kernel, sizes), out_shape=(jax.S...  86 us
    pallas_call x1, Pallas kernels, close(): pl.pallas_call(functools.partial(close_kernel, (n, cap, experts, first_st...  27.4 us
    pallas_call x1, Pallas kernels, pool(): pl.pallas_call(functools.partial(pool_kernel, n * cap, tables, bag), out_...  8.58 us

profile of v7, /device:TPU:0, one launch (start us, length us, event | category | flops | bytes accessed | tf_op | source)
XLA Modules:
  0.0 258.3 jit_solution(4044391752181224723)
XLA Ops:
  1.3 0.0 copy-start.1
  1.3 0.0 copy-start.22
  1.3 0.0 copy-start.25
  1.3 0.0 copy-start.28
  1.4 0.0 copy-start.31
  1.4 0.0 copy-start.34
  1.4 0.0 copy-start.37
  1.4 0.0 copy-start.40
  1.4 0.0 copy-start.44
  1.4 0.0 copy-start.47
  1.4 0.0 copy-start.54
  1.4 86.0 %forward.1 = (f32[8,128]{1,0:T(8,128)}, s32[64,128]{1,0:T(8,128)}, s32[32,2,128]{2,1,0:T(2,128)}, s32[32,2,128]{2,1,0:T(2,128)}, s32[32,2,128]{2,1,0:T(2,128)}, ...) custom-call(s32[64,128]{1,0:T(8,128)} %bitcast.745, s32[16,128]{1,0:T(8,128)} %bitcast.754, ...), custom_call_target="tpu_custom_call" | custom-call | tf_op jit(solution)/shard_map/forward/pallas_call | solution.py:456
  87.5 0.5 slice.240
  88.6 0.0 copy-done.1
  88.6 0.0 copy-done.22
  88.7 166.7 %conditional.1 = (f32[]{:T(128)}, f32[]{:T(128)}, f32[16384]{0:T(1024)S(1)}, f32[5,1024,2]{1,2,0:T(2,128)}, f32[5,512,64]{1,2,0:T(8,128)}, /*index=5*/f32[1669]{...) conditional(s32[]{:T(128)} %bitcast.231, (s32[1]{0:T(128)}, ...), branch_computations={%region_0.20_spmd, %region_20.21_spmd} | conditional | flops 5726617600 | bytes 809605056 | solution.py:1285
  89.0 0.5 slice.280
  90.1 0.5 compare_convert_fusion.owned_ref
  90.7 0.6 reshape.941.small_ref
  91.3 8.6 %pool.1.pooled_ref = f32[1024,128]{1,0:T(8,128)S(1)} custom-call(s32[64,128]{1,0:T(8,128)} %get-tuple-element.188.pos_ref, f32[2904,128]{1,0:T(8,128)} %bitcast.732), custom_call_target="tpu_custom_call" | custom-call | tf_op jit(solution)/shard_map/cond/branch_1_fun/pool/pallas_call | solution.py:885
  99.8 0.0 copy-start
  99.9 0.8 copy-done
  100.7 125.1 %backward.1 = (f32[33,88,128]{2,1,0:T(8,128)}, f32[2,2,1024,512]{3,2,1,0:T(8,128)}, f32[2,512,512]{2,1,0:T(8,128)}) custom-call(s32[32,2,128]{2,1,0:T(2,128)} %get-tuple-element.185.lists_ref, s32[1]{0:T(128)} %bitcast.176.stat_ref, s32[13]{0:T(128)S(1)} %get-tuple-element.182.items_ref, f32[8,128]{1,0:T(8,128)} %get-tuple-element.187.fields_ref, ...), custom_call_target="tpu_custom_call" | custom-call | tf_op jit(solution)/shard_map/cond/branch_1_fun/backward/pallas_call | solution.py:643
  225.8 27.4 %close.1 = (f32[64,16384]{1,0:T(8,128)}, f32[64,16384]{1,0:T(8,128)}, f32[1,16384]{1,0:T(1,128)S(1)}, f32[2,1024,512]{2,1,0:T(8,128)}, bf16[2,1024,512]{2,1,0:T(...) custom-call(s32[13]{0:T(128)} %compare_convert_fusion.owned_ref, ...), custom_call_target="tpu_custom_call" | custom-call | tf_op jit(solution)/shard_map/cond/branch_1_fun/close/pallas_call | solution.py:839
  253.2 0.8 fusion.230
  254.0 0.8 convert_bitcast_fusion
  255.4 0.0 copy-start.43
  255.4 0.0 copy-start.57
  255.4 0.0 copy-start.58
  255.5 0.0 copy-start.60
  255.5 0.6 copy-done.43
  256.1 0.0 copy-done.60
  (19 shorter events, 0.0 us)
Async XLA Ops:
  1.3 87.3 %copy-start.1 = (s32[16,256]{1,0:T(8,128)S(1)}, s32[16,256]{1,0:T(8,128)}, u32[]{:S(2)}) copy-start(s32[16,256]{1,0:T(8,128)} %homes_ref.1) | copy-start | bytes 49156
  1.3 87.3 %copy-start.22 = (f32[5,1024,2]{1,2,0:T(2,128)S(1)}, f32[5,1024,2]{1,2,0:T(2,128)}, u32[]{:S(2)}) copy-start(f32[5,1024,2]{1,2,0:T(2,128)} %param.37) | copy-start | bytes 122884
  1.3 87.3 %copy-start.25 = (f32[1,5,1024,2]{2,3,1,0:T(2,128)S(1)}, f32[1,5,1024,2]{2,3,1,0:T(2,128)}, u32[]{:S(2)}) copy-start(f32[1,5,1024,2]{2,3,1,0:T(2,128)} %param.43) | copy-start | bytes 122884
  1.3 87.3 %copy-start.28 = (f32[1,5,1024,2]{2,3,1,0:T(2,128)S(1)}, f32[1,5,1024,2]{2,3,1,0:T(2,128)}, u32[]{:S(2)}) copy-start(f32[1,5,1024,2]{2,3,1,0:T(2,128)} %param.42) | copy-start | bytes 122884
  1.4 87.3 %copy-start.31 = (f32[16384]{0:T(1024)S(1)}, f32[16384]{0:T(1024)}, u32[]{:S(2)}) copy-start(f32[16384]{0:T(1024)} %param.35) | copy-start | bytes 196612
  1.4 87.3 %copy-start.34 = (s32[128,16,4]{0,2,1:T(4,128)S(1)}, s32[128,16,4]{0,2,1:T(4,128)}, u32[]{:S(2)}) copy-start(s32[128,16,4]{0,2,1:T(4,128)} %param.26) | copy-start | bytes 98308
  1.4 87.3 %copy-start.37 = (s32[13]{0:T(128)S(1)}, s32[13]{0:T(128)}, u32[]{:S(2)}) copy-start(s32[13]{0:T(128)} %items_ref.1) | copy-start | bytes 160
  1.4 87.3 %copy-start.40 = (f32[1669]{0:T(1024)S(1)}, f32[1669]{0:T(1024)}, u32[]{:S(2)}) copy-start(f32[1669]{0:T(1024)} %param.39) | copy-start | bytes 20032
  1.4 87.3 %copy-start.44 = (f32[1,1669]{1,0:T(1,128)S(1)}, f32[1,1669]{1,0:T(1,128)}, u32[]{:S(2)}) copy-start(f32[1,1669]{1,0:T(1,128)} %small_m_ref.1) | copy-start | bytes 20032
  1.4 87.3 %copy-start.47 = (f32[1,1669]{1,0:T(1,128)S(1)}, f32[1,1669]{1,0:T(1,128)}, u32[]{:S(2)}) copy-start(f32[1,1669]{1,0:T(1,128)} %small_v_ref.1) | copy-start | bytes 20032
  1.4 87.3 %copy-start.54 = (s32[128,16]{0,1:T(8,128)S(1)}, s32[128,16]{0,1:T(8,128)}, u32[]{:S(2)}) copy-start(s32[128,16]{0,1:T(8,128)} %param.27) | copy-start | bytes 24580
  99.8 0.8 copy-start
  100.6 125.1 %copy-start.4 = (f32[16384,64]{0,1:T(8,128)S(1)}, f32[16384,64]{0,1:T(8,128)}, u32[]{:S(2)}) copy-start(f32[16384,64]{0,1:T(8,128)} %get-tuple-element.196) | copy-start | bytes 12582916 | tf_op jit(solution)/shard_map/cond
  100.6 125.1 %copy-start.14 = (f32[1,5,512,64]{2,3,1,0:T(8,128)S(1)}, f32[1,5,512,64]{2,3,1,0:T(8,128)}, u32[]{:S(2)}) copy-start(f32[1,5,512,64]{2,3,1,0:T(8,128)} %get-tuple-element.203) | copy-start | bytes 1966084 | tf_op jit(solution)/shard_map/cond
  100.6 125.1 %copy-start.16 = (f32[1,5,512,64]{2,3,1,0:T(8,128)S(1)}, f32[1,5,512,64]{2,3,1,0:T(8,128)}, u32[]{:S(2)}) copy-start(f32[1,5,512,64]{2,3,1,0:T(8,128)} %get-tuple-element.204) | copy-start | bytes 1966084 | tf_op jit(solution)/shard_map/cond
  100.6 125.1 %copy-start.55 = (s32[32,2,128]{2,1,0:T(2,128)S(1)}, s32[32,2,128]{2,1,0:T(2,128)}, u32[]{:S(2)}) copy-start(s32[32,2,128]{2,1,0:T(2,128)} %get-tuple-element.184.pairs_ref) | copy-start | bytes 98308 | tf_op jit(solution)/shard_map/cond
  255.4 0.6 copy-start.43
  255.4 0.6 copy-start.57
  255.4 0.6 copy-start.58
  255.5 0.6 copy-start.60
